TPU v7x, 32 devices: a whole 2x2x4 slice. The times are simulated.
32 devices in a mesh: fsdp: 32 (over z, y, x, core).
Axes of the slice: x: 2, y: 2, z: 4, core: 2. Of those that a mesh axis runs over, the one named last changes fastest.
Arguments:
- inputs: bfloat16 [2, 32, 512, 1024], P(None, 'fsdp'), may hold values from -6 to 6
- timesteps: int32 [2, 32], P(None, 'fsdp'), may hold values from 0 to 4999
- segments: int32 [2, 32, 512], P(None, 'fsdp'), may hold values from 0 to 31, never falling along the last dimension, each value on 1 to 256 neighbouring positions
- cotangent: bfloat16 [2, 32, 512, 1024], P(None, 'fsdp'), may hold values from -6 to 6
- query_weight: bfloat16 [1024, 1024], P('fsdp'), may hold values from -0.1875 to 0.1875
- key_weight: bfloat16 [1024, 1024], P('fsdp'), may hold values from -0.1875 to 0.1875
- value_weight: bfloat16 [1024, 1024], P('fsdp'), may hold values from -0.1875 to 0.1875
- output_weight: bfloat16 [1024, 1024], P('fsdp'), may hold values from -0.75 to 0.75
- inner_weight: bfloat16 [1024, 4096], P('fsdp'), may hold values from -0.1875 to 0.1875
- outer_weight: bfloat16 [4096, 1024], P('fsdp'), may hold values from -0.09375 to 0.09375
- time_weight: bfloat16 [1024, 1024], P('fsdp'), may hold values from -0.1875 to 0.1875
- query_bias: bfloat16 [1024], P('fsdp'), may hold values from -3 to 3
- value_bias: bfloat16 [1024], P('fsdp'), may hold values from -3 to 3
- output_bias: bfloat16 [1024], P('fsdp'), may hold values from -3 to 3
- inner_bias: bfloat16 [4096], P('fsdp'), may hold values from -3 to 3
- outer_bias: bfloat16 [1024], P('fsdp'), may hold values from -3 to 3
- first_gain: bfloat16 [1024], P('fsdp'), may hold values from 0.5 to 1.5
- first_shift: bfloat16 [1024], P('fsdp'), may hold values from -2 to 2
- second_gain: bfloat16 [1024], P('fsdp'), may hold values from 0.5 to 1.5
- second_shift: bfloat16 [1024], P('fsdp'), may hold values from -2 to 2
Outputs:
- layer_output: bfloat16 [2, 32, 512, 1024], P(None, 'fsdp')
- input_grad: float32 [2, 32, 512, 1024], P(None, 'fsdp')
- query_weight_grad: float32 [1024, 1024], P('fsdp')
- key_weight_grad: float32 [1024, 1024], P('fsdp')
- value_weight_grad: float32 [1024, 1024], P('fsdp')
- output_weight_grad: float32 [1024, 1024], P('fsdp')
- inner_weight_grad: float32 [1024, 4096], P('fsdp')
- outer_weight_grad: float32 [4096, 1024], P('fsdp')
- time_weight_grad: float32 [1024, 1024], P('fsdp')
- query_bias_grad: float32 [1024], P('fsdp')
- value_bias_grad: float32 [1024], P('fsdp')
- output_bias_grad: float32 [1024], P('fsdp')
- inner_bias_grad: float32 [4096], P('fsdp')
- outer_bias_grad: float32 [1024], P('fsdp')
- first_gain_grad: float32 [1024], P('fsdp')
- first_shift_grad: float32 [1024], P('fsdp')
- second_gain_grad: float32 [1024], P('fsdp')
- second_shift_grad: float32 [1024], P('fsdp')
Inputs may be any that keep to these rules, and one draw needn't show every extreme that they name: `segments`: within a row the segment numbers never fall; each document holds 1 to 256 positions, and in every row one document holds exactly 256.
All inputs are finite; a program needn't handle non-finite values.
Results may differ from a plain program's by a relative error of at most 0.022.
Values may be sent and summed in bfloat16 or wider, within the bound.
No kernel may reach another device: no remote copies, remote signals or barrier semaphores. Data moves between devices by JAX's collectives and lax.ppermute only.
A program may use at most 256 MiB of HBM per device.

v0:
```python
import math

import jax
import jax.numpy as jnp
from jax import lax
from jax.sharding import PartitionSpec as P

D = 1024
H = 16


INV_ROOT_TWO = 0.7071067811865476
INV_ROOT_TAU = 0.3989422804014327


def matmul(operand, factor):
    return jnp.dot(operand, factor, preferred_element_type=jnp.float32)


def matmul_left(operand, factor):
    return lax.dot_general(
        operand, factor, (((0,), (0,)), ((), ())), preferred_element_type=jnp.float32
    )


def matmul_right(operand, factor):
    return lax.dot_general(
        operand, factor, (((1,), (1,)), ((), ())), preferred_element_type=jnp.float32
    )


def features(step_ids):
    half_width = D // 2
    freqs = jnp.exp(-math.log(10000.0) * jnp.arange(half_width, dtype=jnp.float32) / half_width)
    angles = step_ids.astype(jnp.float32)[..., None] * freqs
    return jnp.concatenate([jnp.sin(angles), jnp.cos(angles)], axis=-1)


def normalize(values_in):
    center = values_in - jnp.mean(values_in, axis=-1, keepdims=True)
    spread = lax.rsqrt(jnp.mean(center * center, axis=-1, keepdims=True) + 1e-05)
    return (center * spread, spread)


def norm_back(grad_normed, normed, spread):
    mean_grad = jnp.mean(grad_normed, axis=-1, keepdims=True)
    mean_cross = jnp.mean(grad_normed * normed, axis=-1, keepdims=True)
    return spread * (grad_normed - mean_grad - normed * mean_cross)


def split_heads(rows_in):
    row_length = rows_in.shape[0]
    return rows_in.reshape(row_length, H, rows_in.shape[1] // H)


def row_scores(queries, key_rows, segment_ids):
    head_dim = queries.shape[1] // H
    scores = jnp.einsum(
        "qhd,khd->hqk",
        split_heads(queries),
        split_heads(key_rows),
        preferred_element_type=jnp.float32,
    ) * (1.0 / math.sqrt(head_dim))
    same_doc = (segment_ids[:, None] == segment_ids[None, :])[None]
    return jnp.where(same_doc, scores, -1e30)


def attend_row(queries, key_rows, values, segment_ids):
    scores = row_scores(queries, key_rows, segment_ids)
    top_score = jnp.max(scores, axis=-1, keepdims=True)
    log_total = top_score + jnp.log(jnp.sum(jnp.exp(scores - top_score), axis=-1, keepdims=True))
    soft_low = jnp.exp(scores - log_total).astype(jnp.bfloat16)
    context = jnp.einsum(
        "hqk,khd->qhd", soft_low, split_heads(values), preferred_element_type=jnp.float32
    )
    return (context.reshape(queries.shape).astype(jnp.bfloat16), log_total)


def attend_back(queries, key_rows, values, segment_ids, log_total, grad_context):
    head_dim = queries.shape[1] // H
    score_scale = 1.0 / math.sqrt(head_dim)
    soft = jnp.exp(row_scores(queries, key_rows, segment_ids) - log_total)
    context_heads = split_heads(grad_context)
    grad_values = jnp.einsum(
        "hqk,qhd->khd", soft.astype(jnp.bfloat16), context_heads, preferred_element_type=jnp.float32
    )
    grad_soft = jnp.einsum(
        "qhd,khd->hqk", context_heads, split_heads(values), preferred_element_type=jnp.float32
    )
    inner_sum = jnp.sum(soft * grad_soft, axis=-1, keepdims=True)
    grad_scores = (soft * (grad_soft - inner_sum)).astype(jnp.bfloat16)
    grad_queries = (
        jnp.einsum(
            "hqk,khd->qhd", grad_scores, split_heads(key_rows), preferred_element_type=jnp.float32
        )
        * score_scale
    )
    grad_keys = (
        jnp.einsum(
            "hqk,qhd->khd", grad_scores, split_heads(queries), preferred_element_type=jnp.float32
        )
        * score_scale
    )
    flat_shape = queries.shape
    return (
        grad_queries.reshape(flat_shape).astype(jnp.bfloat16),
        grad_keys.reshape(flat_shape).astype(jnp.bfloat16),
        grad_values.reshape(flat_shape).astype(jnp.bfloat16),
    )


def collect(params):
    return (
        lax.all_gather(params[0], "fsdp", axis=0, tiled=True),
        lax.all_gather(params[1], "fsdp", axis=0, tiled=True),
        lax.all_gather(params[2], "fsdp", axis=0, tiled=True),
        lax.all_gather(params[3], "fsdp", axis=0, tiled=True),
        lax.all_gather(params[4], "fsdp", axis=0, tiled=True),
        lax.all_gather(params[5], "fsdp", axis=0, tiled=True),
        lax.all_gather(params[6], "fsdp", axis=0, tiled=True),
        lax.all_gather(params[7], "fsdp", axis=0, tiled=True),
        lax.all_gather(params[8], "fsdp", axis=0, tiled=True),
        lax.all_gather(params[9], "fsdp", axis=0, tiled=True),
        lax.all_gather(params[10], "fsdp", axis=0, tiled=True),
        lax.all_gather(params[11], "fsdp", axis=0, tiled=True),
        lax.all_gather(params[12], "fsdp", axis=0, tiled=True),
        lax.all_gather(params[13], "fsdp", axis=0, tiled=True),
        lax.all_gather(params[14], "fsdp", axis=0, tiled=True),
        lax.all_gather(params[15], "fsdp", axis=0, tiled=True),
    )


def collect_again(params):
    return (
        lax.all_gather(params[0], "fsdp", axis=0, tiled=True),
        lax.all_gather(params[1], "fsdp", axis=0, tiled=True),
        lax.all_gather(params[2], "fsdp", axis=0, tiled=True),
        lax.all_gather(params[3], "fsdp", axis=0, tiled=True),
        lax.all_gather(params[4], "fsdp", axis=0, tiled=True),
        lax.all_gather(params[5], "fsdp", axis=0, tiled=True),
        lax.all_gather(params[6], "fsdp", axis=0, tiled=True),
        lax.all_gather(params[7], "fsdp", axis=0, tiled=True),
        lax.all_gather(params[8], "fsdp", axis=0, tiled=True),
        lax.all_gather(params[9], "fsdp", axis=0, tiled=True),
        lax.all_gather(params[10], "fsdp", axis=0, tiled=True),
        lax.all_gather(params[11], "fsdp", axis=0, tiled=True),
        lax.all_gather(params[12], "fsdp", axis=0, tiled=True),
        lax.all_gather(params[13], "fsdp", axis=0, tiled=True),
        lax.all_gather(params[14], "fsdp", axis=0, tiled=True),
        lax.all_gather(params[15], "fsdp", axis=0, tiled=True),
    )


def forward(gathered, inputs, step_ids, segment_ids):
    (
        query_weight,
        key_weight,
        value_weight,
        output_weight,
        inner_weight,
        outer_weight,
        time_weight,
        query_bias,
        value_bias,
        output_bias,
        inner_bias,
        outer_bias,
        first_gain,
        first_shift,
        second_gain,
        second_shift,
    ) = gathered
    row_count, row_length, model_width = inputs.shape
    token_count = row_count * row_length
    feats = features(step_ids).astype(jnp.bfloat16)
    temb = matmul(feats, time_weight)
    stream = (inputs.astype(jnp.float32) + temb[:, None, :]).reshape(token_count, model_width)
    stream_low = stream.astype(jnp.bfloat16)
    queries = (matmul(stream_low, query_weight) + query_bias.astype(jnp.float32)).astype(
        jnp.bfloat16
    )
    key_rows = matmul(stream_low, key_weight).astype(jnp.bfloat16)
    values = (matmul(stream_low, value_weight) + value_bias.astype(jnp.float32)).astype(
        jnp.bfloat16
    )
    row_shape = (row_count, row_length, model_width)
    context, log_total = lax.map(
        lambda member: attend_row(*member),
        (
            queries.reshape(row_shape),
            key_rows.reshape(row_shape),
            values.reshape(row_shape),
            segment_ids,
        ),
    )
    context = context.reshape(token_count, model_width)
    mixed = stream + (matmul(context, output_weight) + output_bias.astype(jnp.float32))
    normed_first, spread_first = normalize(mixed)
    first = normed_first * first_gain.astype(jnp.float32) + first_shift.astype(jnp.float32)
    first_low = first.astype(jnp.bfloat16)
    inner_pre = matmul(first_low, inner_weight) + inner_bias.astype(jnp.float32)
    active_low = jax.nn.gelu(inner_pre, approximate=False).astype(jnp.bfloat16)
    second = first + (matmul(active_low, outer_weight) + outer_bias.astype(jnp.float32))
    normed_second, spread_second = normalize(second)
    result_rows = normed_second * second_gain.astype(jnp.float32) + second_shift.astype(jnp.float32)
    saved = (
        feats,
        stream_low,
        queries,
        key_rows,
        values,
        log_total,
        context,
        normed_first,
        spread_first,
        first_low,
        inner_pre,
        active_low,
        normed_second,
        spread_second,
    )
    return (result_rows.astype(jnp.bfloat16).reshape(row_shape), saved)


def backward(gathered, saved, segment_ids, grad_rows):
    (
        query_weight,
        key_weight,
        value_weight,
        output_weight,
        inner_weight,
        outer_weight,
        time_weight,
        query_bias,
        value_bias,
        output_bias,
        inner_bias,
        outer_bias,
        first_gain,
        first_shift,
        second_gain,
        second_shift,
    ) = gathered
    (
        feats,
        stream_low,
        queries,
        key_rows,
        values,
        log_total,
        context,
        normed_first,
        spread_first,
        first_low,
        inner_pre,
        active_low,
        normed_second,
        spread_second,
    ) = saved
    row_count, row_length, model_width = grad_rows.shape
    token_count = row_count * row_length
    row_shape = (row_count, row_length, model_width)
    grad_out = grad_rows.astype(jnp.float32).reshape(token_count, model_width)
    second_gain_grad = jnp.sum(grad_out * normed_second, axis=0)
    second_shift_grad = jnp.sum(grad_out, axis=0)
    grad_second = norm_back(
        grad_out * second_gain.astype(jnp.float32), normed_second, spread_second
    )
    grad_second_low = grad_second.astype(jnp.bfloat16)
    outer_weight_grad = matmul_left(active_low, grad_second_low)
    outer_bias_grad = jnp.sum(grad_second_low.astype(jnp.float32), axis=0)
    grad_active = matmul_right(grad_second_low, outer_weight)
    normal_cdf = 0.5 * (1.0 + lax.erf(inner_pre * INV_ROOT_TWO))
    normal_pdf = jnp.exp(-0.5 * inner_pre * inner_pre) * INV_ROOT_TAU
    grad_inner_low = (grad_active * (normal_cdf + inner_pre * normal_pdf)).astype(jnp.bfloat16)
    inner_weight_grad = matmul_left(first_low, grad_inner_low)
    inner_bias_grad = jnp.sum(grad_inner_low.astype(jnp.float32), axis=0)
    grad_first = grad_second + matmul_right(grad_inner_low, inner_weight)
    first_gain_grad = jnp.sum(grad_first * normed_first, axis=0)
    first_shift_grad = jnp.sum(grad_first, axis=0)
    grad_mixed = norm_back(grad_first * first_gain.astype(jnp.float32), normed_first, spread_first)
    grad_mixed_low = grad_mixed.astype(jnp.bfloat16)
    output_weight_grad = matmul_left(context, grad_mixed_low)
    output_bias_grad = jnp.sum(grad_mixed_low.astype(jnp.float32), axis=0)
    grad_context = matmul_right(grad_mixed_low, output_weight).astype(jnp.bfloat16)
    grad_queries, grad_keys, grad_values = lax.map(
        lambda member: attend_back(*member),
        (
            queries.reshape(row_shape),
            key_rows.reshape(row_shape),
            values.reshape(row_shape),
            segment_ids,
            log_total,
            grad_context.reshape(row_shape),
        ),
    )
    grad_queries = grad_queries.reshape(token_count, model_width)
    grad_keys = grad_keys.reshape(token_count, model_width)
    grad_values = grad_values.reshape(token_count, model_width)
    query_weight_grad = matmul_left(stream_low, grad_queries)
    key_weight_grad = matmul_left(stream_low, grad_keys)
    value_weight_grad = matmul_left(stream_low, grad_values)
    query_bias_grad = jnp.sum(grad_queries.astype(jnp.float32), axis=0)
    value_bias_grad = jnp.sum(grad_values.astype(jnp.float32), axis=0)
    grad_stream = (
        grad_mixed
        + matmul_right(grad_queries, query_weight)
        + matmul_right(grad_keys, key_weight)
        + matmul_right(grad_values, value_weight)
    )
    grad_stream = grad_stream.reshape(row_shape)
    grad_temb = jnp.sum(grad_stream, axis=1)
    time_weight_grad = jnp.dot(
        feats.astype(jnp.float32).T, grad_temb, precision=lax.Precision.HIGHEST
    )
    grads = (
        query_weight_grad,
        key_weight_grad,
        value_weight_grad,
        output_weight_grad,
        inner_weight_grad,
        outer_weight_grad,
        time_weight_grad,
        query_bias_grad,
        value_bias_grad,
        output_bias_grad,
        inner_bias_grad,
        outer_bias_grad,
        first_gain_grad,
        first_shift_grad,
        second_gain_grad,
        second_shift_grad,
    )
    return (grad_stream, grads)


def on_device(
    inputs,
    timesteps,
    segments,
    cotangent,
    query_weight,
    key_weight,
    value_weight,
    output_weight,
    inner_weight,
    outer_weight,
    time_weight,
    query_bias,
    value_bias,
    output_bias,
    inner_bias,
    outer_bias,
    first_gain,
    first_shift,
    second_gain,
    second_shift,
):
    params = (
        query_weight,
        key_weight,
        value_weight,
        output_weight,
        inner_weight,
        outer_weight,
        time_weight,
        query_bias,
        value_bias,
        output_bias,
        inner_bias,
        outer_bias,
        first_gain,
        first_shift,
        second_gain,
        second_shift,
    )
    batch_count = inputs.shape[0]
    totals = None
    output_list = []
    grad_list = []
    for batch_index in range(batch_count):
        gathered = collect(params)
        result_rows, saved = forward(
            gathered, inputs[batch_index], timesteps[batch_index], segments[batch_index]
        )
        gathered_back = collect_again(params)
        grad_stream, grads = backward(
            gathered_back, saved, segments[batch_index], cotangent[batch_index]
        )
        output_list.append(result_rows)
        grad_list.append(grad_stream)
        totals = grads if totals is None else jax.tree.map(jnp.add, totals, grads)
    totals = lax.psum_scatter(totals, "fsdp", scatter_dimension=0, tiled=True)
    return (jnp.stack(output_list), jnp.stack(grad_list)) + tuple(totals)


def solution(mesh):
    return jax.shard_map(
        on_device,
        mesh=mesh,
        in_specs=(
            P(None, "fsdp", None, None),
            P(None, "fsdp"),
            P(None, "fsdp", None),
            P(None, "fsdp", None, None),
            P("fsdp", None),
            P("fsdp", None),
            P("fsdp", None),
            P("fsdp", None),
            P("fsdp", None),
            P("fsdp", None),
            P("fsdp", None),
            P("fsdp"),
            P("fsdp"),
            P("fsdp"),
            P("fsdp"),
            P("fsdp"),
            P("fsdp"),
            P("fsdp"),
            P("fsdp"),
            P("fsdp"),
        ),
        out_specs=(
            P(None, "fsdp", None, None),
            P(None, "fsdp", None, None),
            P("fsdp", None),
            P("fsdp", None),
            P("fsdp", None),
            P("fsdp", None),
            P("fsdp", None),
            P("fsdp", None),
            P("fsdp", None),
            P("fsdp"),
            P("fsdp"),
            P("fsdp"),
            P("fsdp"),
            P("fsdp"),
            P("fsdp"),
            P("fsdp"),
            P("fsdp"),
            P("fsdp"),
        ),
        check_vma=False,
    )
```

profile of v0, /device:TPU:0, one launch (start us, length us, event | category | flops | bytes accessed | tf_op | source)
XLA Modules:
  0.0 1616.3 jit_solution(18199363383497973175)
XLA Ops:
  21.4 42.3 %all-reduce.18 = (bf16[1024]{0:T(1024)(128)(2,1)S(1)}, bf16[1024]{0:T(1024)(128)(2,1)S(1)}, bf16[1024]{0:T(1024)(128)(2,1)S(1)}, bf16[1024]{0:T(1024)(128)(2,1)S...) all-reduce(bf16[1024]{0:T(1024)(128)(2,1)S(1)} %dynamic-update-slic, ...), channel_id=1, replica_groups=mesh['fsdp'=32] {'fsdp'}, use_global_device_ids=true, to_apply=%add | all-reduce | flops 8192 | bytes 32768
  67.4 40.2 %all-gather = bf16[32,1,128]{2,1,0:T(2,128)(2,1)S(1)} all-gather(bf16[1,1,128]{2,1,0:T(2,128)(2,1)} %bitcast.249), channel_id=1, replica_groups=mesh['fsdp'=32] {'fsdp'}, dimensions={0}, use_global_device_ids=true | all-gather | bytes 8448 | tf_op jit(solution)/shard_map/all_gather | solution.py:124
  110.8 17.7 %all-gather.13.cloned.1.call-done = bf16[1024,1024]{1,0:T(8,128)(2,1)} async-done(((bf16[32,1024]{1,0:T(8,128)(2,1)}), bf16[1024,1024]{1,0:T(8,128)(2,1)}) %all-gather.13.cloned.1.call-update) | async-done | bytes 2097168 | tf_op jit(solution)/shard_map/all_gather | solution.py:114
  139.4 47.2 %all-gather.15.cloned.1.call-done = bf16[1024,1024]{1,0:T(8,128)(2,1)} async-done(((bf16[32,1024]{1,0:T(8,128)(2,1)}), bf16[1024,1024]{1,0:T(8,128)(2,1)}) %all-gather.15.cloned.1.call-update) | async-done | bytes 2097168 | tf_op jit(solution)/shard_map/all_gather | solution.py:115
  191.9 52.6 %all-gather.11.cloned.1.call-done = bf16[1024,1024]{1,0:T(8,128)(2,1)} async-done(((bf16[32,1024]{1,0:T(8,128)(2,1)}), bf16[1024,1024]{1,0:T(8,128)(2,1)}) %all-gather.11.cloned.1.call-update) | async-done | bytes 2097168 | tf_op jit(solution)/shard_map/all_gather | solution.py:116
  289.9 12.7 all-gather.17.cloned.1.call-done
  337.1 44.5 %all-gather.19.cloned.1.call-done = bf16[1024,4096]{1,0:T(8,128)(2,1)} async-done(((bf16[32,4096]{1,0:T(8,128)(2,1)}), bf16[1024,4096]{1,0:T(8,128)(2,1)}) %all-gather.19.cloned.1.call-update) | async-done | bytes 8388624 | tf_op jit(solution)/shard_map/all_gather | solution.py:118
  392.1 43.4 %fusion.6 = (bf16[512,4096]{1,0:T(8,128)(2,1)}, bf16[512,4096]{1,0:T(8,128)(2,1)}, f32[512,4096]{1,0:T(8,128)}) fusion(f32[4096]{0:T(1024)S(1)} %bitcast.246, f32[512,4096]{1,0:T(8,128)S(1)} %fusion.110, bf16[1024,4096]{1,0:T(8,128)(2,1)S(1)} %copy-done.90, f32[512,1024]{1,0:T(8,128)S(1)} %copy-done.24, f32[1024]{0:T(1024)S(1)} %convert_element_type.365, ...), kind=kOutput, calls=%fused_computation.20 | convolution fusion | flops 4574412800 | bytes 35680256 | tf_op jit(solution)/shard_map/dot_general | solution.py:17
  435.6 25.0 %all-gather.21.cloned.1.call-done = bf16[4096,1024]{1,0:T(8,128)(2,1)} async-done(((bf16[128,1024]{1,0:T(8,128)(2,1)}), bf16[4096,1024]{1,0:T(8,128)(2,1)}) %all-gather.21.cloned.1.call-update) | async-done | bytes 8388624 | tf_op jit(solution)/shard_map/all_gather | solution.py:119
  482.3 13.5 convert_reduce_fusion.1
  507.7 13.0 convert_reduce_fusion
  520.7 12.7 convert_reduce_fusion.7
  579.7 12.6 multiply_reduce_fusion.1
  592.4 12.4 multiply_convert_fusion.1
  622.1 12.6 multiply_convert_fusion
  678.3 13.5 fusion.112
  704.1 13.4 fusion.96
  731.4 40.7 %all-reduce.17 = (f32[1024]{0:T(1024)S(1)}, f32[1024]{0:T(1024)S(1)}, f32[1024]{0:T(1024)S(1)}, f32[4096]{0:T(1024)S(1)}, f32[1024]{0:T(1024)S(1)}, /*index=5*/f...) all-reduce(f32[1024]{0:T(1024)S(1)} %add.391, ...), channel_id=9, replica_groups=mesh['fsdp'=32] {'fsdp'}, use_global_device_ids=true, to_apply=%region_33.34.clone | all-reduce | flops 12288 | bytes 98304
  782.5 38.9 %reduce-scatter.12.cloned.1.call-done = f32[32,1024]{1,0:T(8,128)} async-done(((f32[1024,1024]{1,0:T(8,128)}), f32[32,1024]{1,0:T(8,128)}) %reduce-scatter.12.cloned.1.call-update) | async-done | bytes 131088 | tf_op jit(solution)/shard_map/reduce_scatter | solution.py:393
  821.4 139.6 %reduce-scatter.8.cloned.1.call-done = f32[32,1024]{1,0:T(8,128)} async-done(((f32[1024,1024]{1,0:T(8,128)}), f32[32,1024]{1,0:T(8,128)}) %reduce-scatter.8.cloned.1.call-update) | async-done | bytes 131088 | tf_op jit(solution)/shard_map/reduce_scatter | solution.py:393
  961.0 139.9 %reduce-scatter.10.cloned.1.call-done = f32[32,1024]{1,0:T(8,128)} async-done(((f32[1024,1024]{1,0:T(8,128)}), f32[32,1024]{1,0:T(8,128)}) %reduce-scatter.10.cloned.1.call-update) | async-done | bytes 131088 | tf_op jit(solution)/shard_map/reduce_scatter | solution.py:393
  1100.9 139.5 %reduce-scatter.20.cloned.1.call-done = f32[32,1024]{1,0:T(8,128)} async-done(((f32[1024,1024]{1,0:T(8,128)}), f32[32,1024]{1,0:T(8,128)}) %reduce-scatter.20.cloned.1.call-update) | async-done | bytes 131088 | tf_op jit(solution)/shard_map/reduce_scatter | solution.py:393
  1240.4 181.5 %reduce-scatter.16.cloned.1.call-done = f32[32,4096]{1,0:T(8,128)} async-done(((f32[1024,4096]{1,0:T(8,128)}), f32[32,4096]{1,0:T(8,128)}) %reduce-scatter.16.cloned.1.call-update) | async-done | bytes 524304 | tf_op jit(solution)/shard_map/reduce_scatter | solution.py:393
  1421.9 187.4 %reduce-scatter.18.cloned.1.call-done = f32[128,1024]{1,0:T(8,128)} async-done(((f32[4096,1024]{1,0:T(8,128)}), f32[128,1024]{1,0:T(8,128)}) %reduce-scatter.18.cloned.1.call-update) | async-done | bytes 524304 | tf_op jit(solution)/shard_map/reduce_scatter | solution.py:393
  (359 shorter events, 302.8 us)
Async XLA Ops:
  7.2 101.7 %all-gather.9.cloned.1.call-start = ((), (), s32[]{:S(2)}) async-start(), calls=%async_computation.7 | async-start | bytes 2162688 | tf_op jit(solution)/shard_map/all_gather | solution.py:120
  7.9 120.5 %all-gather.13.cloned.1.call-start = ((), (), s32[]{:S(2)}) async-start(), calls=%async_computation.9 | async-start | bytes 2162688 | tf_op jit(solution)/shard_map/all_gather | solution.py:114
  8.7 177.9 %all-gather.15.cloned.1.call-start = ((), (), s32[]{:S(2)}) async-start(), calls=%async_computation.10 | async-start | bytes 2162688 | tf_op jit(solution)/shard_map/all_gather | solution.py:115
  9.4 235.2 %all-gather.11.cloned.1.call-start = ((), (), s32[]{:S(2)}) async-start(), calls=%async_computation.8 | async-start | bytes 2162688 | tf_op jit(solution)/shard_map/all_gather | solution.py:116
  10.0 292.6 %all-gather.17.cloned.1.call-start = ((), (), s32[]{:S(2)}) async-start(), calls=%async_computation.11 | async-start | bytes 2162688 | tf_op jit(solution)/shard_map/all_gather | solution.py:117
  10.6 371.0 %all-gather.19.cloned.1.call-start = ((), (), s32[]{:S(2)}) async-start(), calls=%async_computation.12 | async-start | bytes 8650752 | tf_op jit(solution)/shard_map/all_gather | solution.py:118
  11.1 449.4 %all-gather.21.cloned.1.call-start = ((), (), s32[]{:S(2)}) async-start(), calls=%async_computation.13 | async-start | bytes 8650752 | tf_op jit(solution)/shard_map/all_gather | solution.py:119
  11.9 770.6 %reduce-scatter.14.cloned.1.call-start = ((), (), s32[]{:S(2)}) async-start(), calls=%async_computation.17 | async-start | bytes 4325376 | tf_op jit(solution)/shard_map/reduce_scatter | solution.py:393
  63.7 407.2 %copy-start.65 = (f32[1024]{0:T(1024)}, f32[1024]{0:T(1024)S(1)}, u32[]{:S(2)}) copy-start(f32[1024]{0:T(1024)S(1)} %convert_element_type.365) | copy-start | bytes 12292
  107.9 172.3 %copy-start.35 = (pred[512,512]{0,1:T(8,128)(4,1)}, pred[512,512]{0,1:T(8,128)(4,1)S(1)}, u32[]{:S(2)}) copy-start(pred[512,512]{0,1:T(8,128)(4,1)S(1)} %broadcast_compare_fusion) | copy-start | bytes 786436
  110.8 223.2 %copy-start.63 = (f32[1,1024]{1,0:T(1,128)}, f32[1,1024]{1,0:T(1,128)S(1)}, u32[]{:S(2)}) copy-start(f32[1,1024]{1,0:T(1,128)S(1)} %fusion.126) | copy-start | bytes 12292
  135.2 167.3 %copy-start.61 = (f32[1,1024]{1,0:T(1,128)}, f32[1,1024]{1,0:T(1,128)S(1)}, u32[]{:S(2)}) copy-start(f32[1,1024]{1,0:T(1,128)S(1)} %fusion.127) | copy-start | bytes 12292
  191.9 114.7 %copy-start.10 = (bf16[512,1024]{0,1:T(8,128)(2,1)}, bf16[512,1024]{0,1:T(8,128)(2,1)S(1)}, u32[]{:S(2)}) copy-start(bf16[512,1024]{0,1:T(8,128)(2,1)S(1)} %copy.80) | copy-start | bytes 3145732
  306.2 75.4 %copy-start.2 = (f32[512,1024]{1,0:T(8,128)}, f32[512,1024]{1,0:T(8,128)S(1)}, u32[]{:S(2)}) copy-start(f32[512,1024]{1,0:T(8,128)S(1)} %get-tuple-element.189) | copy-start | bytes 6291460
  306.2 75.4 %copy-start.67 = (f32[512]{0:T(512)}, f32[512]{0:T(512)S(1)}, u32[]{:S(2)}) copy-start(f32[512]{0:T(512)S(1)} %broadcast_multiply_fusion.9) | copy-start | bytes 6148
  306.6 75.0 %copy-start.70 = (f32[512]{0:T(512)}, f32[512]{0:T(512)S(1)}, u32[]{:S(2)}) copy-start(f32[512]{0:T(512)S(1)} %add_rsqrt_fusion.1) | copy-start | bytes 6148
  392.1 68.4 %copy-start.89 = (f32[1024]{0:T(1024)S(1)}, f32[1024]{0:T(1024)}, u32[]{:S(2)}) copy-start(f32[1024]{0:T(1024)} %convert_element_type.369) | copy-start | bytes 12292
  541.7 279.7 %reduce-scatter.12.cloned.1.call-start = ((), (), s32[]{:S(2)}) async-start(), calls=%async_computation.16 | async-start | bytes 4325376 | tf_op jit(solution)/shard_map/reduce_scatter | solution.py:393
  579.7 381.3 %reduce-scatter.8.cloned.1.call-start = ((), (), s32[]{:S(2)}) async-start(), calls=%async_computation.14 | async-start | bytes 4325376 | tf_op jit(solution)/shard_map/reduce_scatter | solution.py:393
  642.3 458.6 %reduce-scatter.10.cloned.1.call-start = ((), (), s32[]{:S(2)}) async-start(), calls=%async_computation.15 | async-start | bytes 4325376 | tf_op jit(solution)/shard_map/reduce_scatter | solution.py:393
  660.6 579.8 %reduce-scatter.20.cloned.1.call-start = ((), (), s32[]{:S(2)}) async-start(), calls=%async_computation.20 | async-start | bytes 4325376 | tf_op jit(solution)/shard_map/reduce_scatter | solution.py:393
  678.0 743.9 %reduce-scatter.16.cloned.1.call-start = ((), (), s32[]{:S(2)}) async-start(), calls=%async_computation.18 | async-start | bytes 17301504 | tf_op jit(solution)/shard_map/reduce_scatter | solution.py:393
  703.7 905.6 %reduce-scatter.18.cloned.1.call-start = ((), (), s32[]{:S(2)}) async-start(), calls=%async_computation.19 | async-start | bytes 17301504 | tf_op jit(solution)/shard_map/reduce_scatter | solution.py:393
  731.1 49.1 %copy-start.31 = (f32[512,1024]{1,0:T(8,128)S(1)}, f32[512,1024]{1,0:T(8,128)}, u32[]{:S(2)}) copy-start(f32[512,1024]{1,0:T(8,128)} %get-tuple-element.204) | copy-start | bytes 6291460
  (86 other events, 526.4 us)
Sparse Core Ops, SparseCore 0:
  10.9 59.3 all-gather.8
  73.1 55.2 all-gather.12
  131.3 55.2 all-gather.14
  189.3 55.2 all-gather.10
  247.3 55.2 all-gather.16
  305.3 76.2 all-gather.18
  384.5 76.0 all-gather.20
  541.8 139.4 reduce-scatter.13
  684.1 137.2 reduce-scatter.11
  824.1 136.8 reduce-scatter.7
  963.8 137.0 reduce-scatter.9
  1103.6 136.7 reduce-scatter.19
  1243.3 178.5 reduce-scatter.15
  1424.6 184.6 reduce-scatter.17
where the time goes:
time: 1620 us
  waiting for transfers between devices  1030 us (64%)
  matrix products  332 us (20%)
  blocking collectives  123 us (8%)
  other arithmetic  64.5 us (4%)
  local copies, waits for them, and re-layouts  47.2 us (3%)
  between operations  16.9 us (1%)
    reduce_scatter x7, waiting for transfers between devices, on_device(): totals = lax.psum_scatter(totals, 'fsdp', scatter_dimension=0, tiled=True)  827 us
    dot_general x14, matrix products, matmul(): return jnp.dot(operand, factor, preferred_element_type=jnp.float32)  95.8 us
    unnamed x2, blocking collectives  83.1 us
    dot_general x12, matrix products, matmul_right(): lax.dot_general(operand, factor, (((1,), (1,)), ((), ())), preferred_elem...  71.8 us
    dot_general x12, matrix products, matmul_left(): lax.dot_general(operand, factor, (((0,), (0,)), ((), ())), preferred_elem...  68.8 us
    all_gather x1, waiting for transfers between devices, collect(): lax.all_gather(params[2], 'fsdp', axis=0, tiled=True)  52.6 us
    all_gather x1, waiting for transfers between devices, collect(): lax.all_gather(params[1], 'fsdp', axis=0, tiled=True)  47.2 us
    all_gather x1, waiting for transfers between devices, collect(): lax.all_gather(params[4], 'fsdp', axis=0, tiled=True)  44.5 us
  transfers between devices with their start and end apart: 14, of which 12 were waited for; matrix products, arithmetic and copies ran while one was open for 21% of the time, Pallas kernels for 0%

commit v1 on v0

v1 whole, which is shorter than its diff:
```python
import functools
import math

import jax
import jax.numpy as jnp
from jax import lax
from jax.experimental import pallas as pl
from jax.experimental.pallas import tpu as pltpu
from jax.sharding import PartitionSpec as P

D = 1024
H = 16


INV_ROOT_TWO = 0.7071067811865476
INV_ROOT_TAU = 0.3989422804014327
F32 = jnp.float32
BF16 = jnp.bfloat16


def matmul(operand, factor):
    return jnp.dot(operand, factor, preferred_element_type=F32)


def matmul_left(operand, factor):
    return lax.dot_general(
        operand, factor, (((0,), (0,)), ((), ())), preferred_element_type=F32
    )


def matmul_right(operand, factor):
    return lax.dot_general(
        operand, factor, (((1,), (1,)), ((), ())), preferred_element_type=F32
    )


def features(step_ids):
    half_width = D // 2
    freqs = jnp.exp(-math.log(10000.0) * jnp.arange(half_width, dtype=F32) / half_width)
    angles = step_ids.astype(F32)[..., None] * freqs
    return jnp.concatenate([jnp.sin(angles), jnp.cos(angles)], axis=-1)


def normalize(values_in):
    center = values_in - jnp.mean(values_in, axis=-1, keepdims=True)
    spread = lax.rsqrt(jnp.mean(center * center, axis=-1, keepdims=True) + 1e-05)
    return (center * spread, spread)


def norm_back(grad_normed, normed, spread):
    mean_grad = jnp.mean(grad_normed, axis=-1, keepdims=True)
    mean_cross = jnp.mean(grad_normed * normed, axis=-1, keepdims=True)
    return spread * (grad_normed - mean_grad - normed * mean_cross)


class Net:
    def __init__(self, n):
        self.n = n
        self.bits = n.bit_length() - 1
        chip = self.bits - 1
        sizes = [(chip + 2 - i) // 3 for i in range(3)]
        groups, top = [], self.bits - 1
        for size in sizes:
            groups.append(tuple(range(top, top - size, -1)))
            top -= size
        self.outer, self.middle, self.near = groups
        self.core = (0,)

    def masks(self, group):
        found = []
        for pick in range(1, 1 << len(group)):
            mask = 0
            for place, bit in enumerate(group):
                if pick >> place & 1:
                    mask |= 1 << bit
            found.append(mask)
        return found

    def swap(self, array, mask):
        return lax.ppermute(array, "fsdp", [(i, i ^ mask) for i in range(self.n)])

    def gather(self, shard, order):
        masks = self.masks(order[0])
        first = jnp.stack([shard] + [self.swap(shard, mask) for mask in masks])
        pieces = [([0] + masks, first)]
        for group in order[1:]:
            fresh = []
            for mask in self.masks(group):
                for sources, array in pieces:
                    fresh.append(([source ^ mask for source in sources], self.swap(array, mask)))
            pieces += fresh
        return pieces

    def take(self, term, bits, mask, present, me):
        present = list(present)
        for bit in bits:
            place = present.index(bit)
            low = 1 << (len(present) - 1 - place)
            value = (me >> bit & 1) ^ (mask >> bit & 1)
            rest = term.shape[1:]
            term = term.reshape((1 << place, 2, low) + rest)
            term = lax.dynamic_index_in_dim(term, value, 1, keepdims=False)
            term = term.reshape((low << place,) + rest)
            present.remove(bit)
        return term

    def scatter(self, halves, order, me):
        keep, send = halves
        terms, present = [keep, self.swap(send, 1)], list(range(self.bits - 1, 0, -1))
        for group in order:
            received = []
            for mask in self.masks(group):
                parts = [self.take(term, group, mask, present, me).astype(F32) for term in terms]
                received.append(self.swap(sum(parts[1:], parts[0]).astype(keep.dtype), mask))
            terms = [self.take(term, group, 0, present, me) for term in terms] + received
            present = [bit for bit in present if bit not in group]
        parts = [term.astype(F32)[0] for term in terms]
        return sum(parts[1:], parts[0])

    def scatter_whole(self, whole, order, me):
        present = list(range(self.bits - 1, -1, -1))
        halves = [self.take(whole, self.core, mask, present, me) for mask in (0, 1)]
        return self.scatter(halves, order, me)


class Weights:
    def __init__(self, net, me, wanted):
        self.arrays, self.plans, self.shapes = [], [], []
        seen = {}
        for pieces, which in wanted:
            rows, columns = pieces[0][1].shape[-2:]
            plan = []
            if rows % 16:
                blocks = jnp.concatenate([array[:, which] for _, array in pieces])
                order = jnp.asarray([s for own, _ in pieces for s in own], jnp.int32)
                place = jnp.zeros((net.n,), jnp.int32).at[order ^ me].set(jnp.arange(net.n))
                whole = blocks[place].reshape(net.n * rows // 16, 16, columns)
                plan.append((len(self.arrays), None, None))
                self.arrays.append(whole)
                self.shapes.append(whole.shape)
            else:
                for own, array in pieces:
                    if id(array) not in seen:
                        seen[id(array)] = len(self.arrays)
                        self.arrays.append(array)
                    for j, source in enumerate(own):
                        plan.append((seen[id(array)], (j, which), source))
                self.shapes.append((net.n, rows, columns))
            self.plans.append(plan)
        self.slots = max(len(plan) for plan in self.plans)

    def scratch(self):
        return [pltpu.VMEM(shape, BF16) for shape in self.shapes] + [
            pltpu.SemaphoreType.DMA((len(self.plans), self.slots))
        ]

    def copies(self, w, me, array_refs, held_ref, sems):
        found = []
        for slot, (array, index, source) in enumerate(self.plans[w]):
            if index is None:
                pair = (array_refs[array], held_ref)
            else:
                pair = (array_refs[array].at[index], held_ref.at[me ^ source])
            found.append(pltpu.make_async_copy(*pair, sems.at[w, slot]))
        return found

    def start(self, w, *refs):
        for copy in self.copies(w, *refs):
            copy.start()

    def wait(self, w, *refs):
        for copy in self.copies(w, *refs):
            copy.wait()


def flat(held):
    return held.reshape(-1, held.shape[-1])


SMEM_SPEC = pl.BlockSpec(memory_space=pltpu.SMEM)
ANY_SPEC = pl.BlockSpec(memory_space=pl.ANY)


def full_spec(shape):
    return pl.BlockSpec(shape, lambda *_: (0,) * len(shape))


def tile_spec(tile, columns):
    return pl.BlockSpec((tile, columns), lambda i: (i, 0))


def call(body, name, grid, ins, outs, scratch, flops, vmem, read, exps=0):
    return pl.pallas_call(
        body,
        grid=grid,
        in_specs=[spec for _, spec in ins],
        out_specs=[spec for _, _, spec in outs],
        out_shape=[jax.ShapeDtypeStruct(shape, dtype) for shape, dtype, _ in outs],
        scratch_shapes=scratch,
        compiler_params=pltpu.CompilerParams(
            vmem_limit_bytes=vmem << 20,
            dimension_semantics=("arbitrary",) * len(grid),
        ),
        cost_estimate=pl.CostEstimate(flops=flops, bytes_accessed=read, transcendentals=exps),
        name=name,
    )(*[array for array, _ in ins])


def project_body(weights, tile, row_length, me_ref, *refs):
    count = len(weights.arrays)
    arrays, refs = refs[:count], refs[count:]
    feats_ref, x_ref, qb_ref, vb_ref = refs[:4]
    temb_ref, low_ref, q_ref, k_ref, v_ref = refs[4:9]
    tw, qw, kw, vw, sems = refs[9:14]
    me, step = me_ref[0], pl.program_id(0)

    @pl.when(step == 0)
    def _():
        for w, held in enumerate((tw, qw, kw, vw)):
            weights.start(w, me, arrays, held, sems)
        weights.wait(0, me, arrays, tw, sems)
        temb_ref[...] = matmul(feats_ref[...], flat(tw[...]))
        for w, held in ((1, qw), (2, kw), (3, vw)):
            weights.wait(w, me, arrays, held, sems)

    row = step * tile // row_length
    low = (x_ref[...].astype(F32) + temb_ref[pl.ds(row, 1), :]).astype(BF16)
    low_ref[...] = low
    q_ref[...] = (matmul(low, flat(qw[...])) + qb_ref[...]).astype(BF16)
    k_ref[...] = matmul(low, flat(kw[...])).astype(BF16)
    v_ref[...] = (matmul(low, flat(vw[...])) + vb_ref[...]).astype(BF16)


def project(net, me, flow_tq, flow_kv, feats, x, query_bias, value_bias, row_length):
    tokens, width = x.shape
    tile = min(256, row_length)
    weights = Weights(net, me, [(flow_tq, 0), (flow_tq, 1), (flow_kv, 0), (flow_kv, 1)])
    ins = (
        [(me.reshape(1), SMEM_SPEC)]
        + [(array, ANY_SPEC) for array in weights.arrays]
        + [(feats, full_spec(feats.shape)), (x, tile_spec(tile, width))]
        + [(bias, full_spec((1, width))) for bias in (query_bias, value_bias)]
    )
    outs = [(feats.shape, F32, full_spec(feats.shape))]
    outs += [((tokens, width), BF16, tile_spec(tile, width))] * 4
    return call(
        functools.partial(project_body, weights, tile, row_length),
        "project",
        (tokens // tile,),
        ins,
        outs,
        weights.scratch(),
        6 * tokens * width * width,
        40,
        8 * width * width + 10 * tokens * width,
    )


def same_document(segc_ref, segr_ref, bias_ref):
    @pl.when(pl.program_id(1) == 0)
    def _():
        bias_ref[...] = jnp.where(segc_ref[0] == segr_ref[0], 0.0, -1e30)


def own_lanes(shape, head, head_dim):
    lanes = lax.broadcasted_iota(jnp.int32, shape, len(shape) - 1)
    return (lanes // head_dim) == head


def attend_body(head_dim, segc_ref, segr_ref, q_ref, k_ref, v_ref, out_ref, log_ref, bias_ref):
    same_document(segc_ref, segr_ref, bias_ref)
    queries, key_rows, values = q_ref[...], k_ref[...], v_ref[...]
    scale = 1.0 / math.sqrt(head_dim)
    per = queries.shape[1] // head_dim
    total = None
    for head in range(per):
        mine = own_lanes(queries.shape, head, head_dim)
        keys_own = jnp.where(mine, key_rows * BF16(scale), BF16(0))
        scores = matmul_right(keys_own, queries) + bias_ref[...]
        top = jnp.max(scores, axis=0, keepdims=True)
        raised = jnp.exp(scores - top)
        amount = jnp.sum(raised, axis=0, keepdims=True)
        log_ref[0, 0, pl.ds(head, 1), :] = top + jnp.log(amount)
        soft_low = (raised * (1.0 / amount)).astype(BF16)
        context = matmul_left(soft_low, values)
        total = context if total is None else jnp.where(mine, context, total)
    out_ref[...] = total.astype(BF16)


def attend_back_body(
    head_dim, segc_ref, segr_ref, q_ref, k_ref, v_ref, log_ref, g_ref, gq_ref, gk_ref, gv_ref, bias_ref
):
    same_document(segc_ref, segr_ref, bias_ref)
    queries, key_rows, values, grads = q_ref[...], k_ref[...], v_ref[...], g_ref[...]
    scale = 1.0 / math.sqrt(head_dim)
    per = queries.shape[1] // head_dim
    totals = None
    for head in range(per):
        mine = own_lanes(queries.shape, head, head_dim)
        keys_own = jnp.where(mine, key_rows * BF16(scale), BF16(0))
        scores = matmul_right(keys_own, queries) + bias_ref[...]
        soft = jnp.exp(scores - log_ref[0, 0, pl.ds(head, 1), :])
        grad_soft = matmul_right(jnp.where(mine, values, BF16(0)), grads)
        inner_sum = jnp.sum(soft * grad_soft, axis=0, keepdims=True)
        grad_scores = (soft * (grad_soft - inner_sum)).astype(BF16)
        parts = (
            matmul_left(grad_scores, key_rows),
            matmul(grad_scores, queries),
            matmul(soft.astype(BF16), grads),
        )
        if totals is None:
            totals = parts
        else:
            totals = tuple(jnp.where(mine, part, total) for part, total in zip(parts, totals))
    gq_ref[...] = (totals[0] * scale).astype(BF16)
    gk_ref[...] = (totals[1] * scale).astype(BF16)
    gv_ref[...] = totals[2].astype(BF16)


def attention_specs(rows, row_length, lanes):
    segc = pl.BlockSpec((1, row_length, 1), lambda i, j: (i, 0, 0))
    segr = pl.BlockSpec((1, 1, row_length), lambda i, j: (i, 0, 0))
    block = pl.BlockSpec((row_length, lanes), lambda i, j: (i, j))
    return segc, segr, block


def attend(queries, key_rows, values, segments):
    rows, row_length = segments.shape
    tokens, width = queries.shape
    head_dim = width // H
    lanes = 128
    blocks, per = width // lanes, lanes // head_dim
    segc, segr, block = attention_specs(rows, row_length, lanes)
    log_spec = pl.BlockSpec((1, 1, per, row_length), lambda i, j: (i, j, 0, 0))
    return call(
        functools.partial(attend_body, head_dim),
        "attend",
        (rows, blocks),
        [(segments[:, :, None], segc), (segments[:, None, :], segr)]
        + [(array, block) for array in (queries, key_rows, values)],
        [
            ((tokens, width), BF16, block),
            ((rows, blocks, per, row_length), F32, log_spec),
        ],
        [pltpu.VMEM((row_length, row_length), F32)],
        4 * tokens * row_length * width * 4,
        32,
        8 * tokens * width,
        tokens * row_length * H,
    )


def attend_back(queries, key_rows, values, segments, log_total, grad_context):
    rows, row_length = segments.shape
    tokens, width = queries.shape
    head_dim = width // H
    lanes = 128
    blocks, per = width // lanes, lanes // head_dim
    segc, segr, block = attention_specs(rows, row_length, lanes)
    log_spec = pl.BlockSpec((1, 1, per, row_length), lambda i, j: (i, j, 0, 0))
    return call(
        functools.partial(attend_back_body, head_dim),
        "attend_back",
        (rows, blocks),
        [(segments[:, :, None], segc), (segments[:, None, :], segr)]
        + [(array, block) for array in (queries, key_rows, values)]
        + [(log_total, log_spec), (grad_context, block)],
        [((tokens, width), BF16, block)] * 3,
        [pltpu.VMEM((row_length, row_length), F32)],
        10 * tokens * row_length * width * 4,
        32,
        14 * tokens * width,
        tokens * row_length * H,
    )


def add_to(ref, value, step):
    part = jnp.sum(value, axis=0, keepdims=True)

    @pl.when(step == 0)
    def _():
        ref[...] = part

    @pl.when(step != 0)
    def _():
        ref[...] += part


def ffn_body(weights, tile, row_length, chunk, me_ref, *refs):
    count = len(weights.arrays)
    arrays, refs = refs[:count], refs[count:]
    (context_ref, x_ref, temb_ref, cot_ref, ob_ref, ib_ref, ub_ref) = refs[:7]
    (fg_ref, fs_ref, sg_ref, ss_ref) = refs[7:11]
    (out_ref, first_low_ref, normed_ref, spread_ref, active_ref, slope_ref) = refs[11:17]
    (gs_ref, gs_low_ref, sgg_ref, ssg_ref, obg_ref) = refs[17:22]
    ow, iw, uw, sems = refs[22:26]
    acc_ref = refs[26]
    me, step = me_ref[0], pl.program_id(0)

    @pl.when(step == 0)
    def _():
        for w, held in enumerate((ow, iw, uw)):
            weights.start(w, me, arrays, held, sems)
        weights.wait(0, me, arrays, ow, sems)

    row = step * tile // row_length
    stream = x_ref[...].astype(F32) + temb_ref[pl.ds(row, 1), :]
    mixed = stream + (matmul(context_ref[...], flat(ow[...])) + ob_ref[...])
    normed, spread = normalize(mixed)
    normed_ref[...] = normed
    spread_ref[...] = spread
    first = normed * fg_ref[...] + fs_ref[...]
    first_low_ref[...] = first.astype(BF16)
    acc_ref[...] = first + ub_ref[...]

    @pl.when(step == 0)
    def _():
        for w, held in ((1, iw), (2, uw)):
            weights.wait(w, me, arrays, held, sems)

    unit = uw.shape[1]
    hidden = iw.shape[2]

    @pl.loop(0, hidden // chunk)
    def _(j):
        columns = pl.ds(pl.multiple_of(j * chunk, chunk), chunk)
        pre = matmul(first_low_ref[...], flat(iw[:, :, columns])) + ib_ref[:, columns]
        normal_cdf = 0.5 * (1.0 + lax.erf(pre * INV_ROOT_TWO))
        normal_pdf = jnp.exp(-0.5 * pre * pre) * INV_ROOT_TAU
        active = (pre * normal_cdf).astype(BF16)
        active_ref[:, columns] = active
        slope_ref[:, columns] = (normal_cdf + pre * normal_pdf).astype(BF16)
        acc_ref[...] += matmul(active, flat(uw[pl.ds(j * (chunk // unit), chunk // unit)]))

    normed_second, spread_second = normalize(acc_ref[...])
    out_ref[...] = (normed_second * sg_ref[...] + ss_ref[...]).astype(BF16)
    grad_out = cot_ref[...].astype(F32)
    add_to(sgg_ref, grad_out * normed_second, step)
    add_to(ssg_ref, grad_out, step)
    grad_second = norm_back(grad_out * sg_ref[...], normed_second, spread_second)
    gs_ref[...] = grad_second
    low = grad_second.astype(BF16)
    gs_low_ref[...] = low
    add_to(obg_ref, low.astype(F32), step)


def ffn(net, me, flows, context, x, temb, cotangent, vectors, row_length):
    tokens, width = x.shape
    hidden = vectors[1].shape[1]
    tile = min(256, row_length)
    weights = Weights(net, me, [(flow, 0) for flow in flows])
    tiled, wide = tile_spec(tile, width), tile_spec(tile, hidden)
    ins = (
        [(me.reshape(1), SMEM_SPEC)]
        + [(array, ANY_SPEC) for array in weights.arrays]
        + [(context, tiled), (x, tiled), (temb, full_spec(temb.shape)), (cotangent, tiled)]
        + [(vector, full_spec(vector.shape)) for vector in vectors]
    )
    row = ((1, width), F32, full_spec((1, width)))
    outs = [
        ((tokens, width), BF16, tiled),
        ((tokens, width), BF16, tiled),
        ((tokens, width), F32, tiled),
        ((tokens, 1), F32, tile_spec(tile, 1)),
        ((tokens, hidden), BF16, wide),
        ((tokens, hidden), BF16, wide),
        ((tokens, width), F32, tiled),
        ((tokens, width), BF16, tiled),
        row,
        row,
        row,
    ]
    return call(
        functools.partial(ffn_body, weights, tile, row_length, 512),
        "ffn",
        (tokens // tile,),
        ins,
        outs,
        weights.scratch() + [pltpu.VMEM((tile, width), F32)],
        2 * tokens * width * (2 * hidden + width),
        60,
        4 * width * hidden + 4 * tokens * hidden + 20 * tokens * width,
        2 * tokens * hidden,
    )


def ffn_back_body(weights, chunk, me_ref, *refs):
    count = len(weights.arrays)
    arrays, refs = refs[:count], refs[count:]
    (gs_ref, gs_low_ref, slope_ref, normed_ref, spread_ref, fg_ref) = refs[:6]
    (gi_ref, gm_ref, gm_low_ref, gc_ref) = refs[6:10]
    (ibg_ref, fgg_ref, fsg_ref, obg_ref) = refs[10:14]
    ow, iw, uw, sems = refs[14:18]
    acc_ref = refs[18]
    me, step = me_ref[0], pl.program_id(0)

    @pl.when(step == 0)
    def _():
        for w, held in ((2, uw), (1, iw), (0, ow)):
            weights.start(w, me, arrays, held, sems)
        for w, held in ((2, uw), (1, iw)):
            weights.wait(w, me, arrays, held, sems)

    acc_ref[...] = gs_ref[...]
    unit = uw.shape[1]
    hidden = iw.shape[2]

    @pl.loop(0, hidden // chunk)
    def _(j):
        columns = pl.ds(pl.multiple_of(j * chunk, chunk), chunk)
        held = flat(uw[pl.ds(j * (chunk // unit), chunk // unit)])
        grad_active = matmul_right(gs_low_ref[...], held)
        low = (grad_active * slope_ref[:, columns].astype(F32)).astype(BF16)
        gi_ref[:, columns] = low
        acc_ref[...] += matmul_right(low, flat(iw[:, :, columns]))

    add_to(ibg_ref, gi_ref[...].astype(F32), step)
    grad_first, normed = acc_ref[...], normed_ref[...]
    add_to(fgg_ref, grad_first * normed, step)
    add_to(fsg_ref, grad_first, step)
    grad_mixed = norm_back(grad_first * fg_ref[...], normed, spread_ref[...])
    gm_ref[...] = grad_mixed
    low = grad_mixed.astype(BF16)
    gm_low_ref[...] = low
    add_to(obg_ref, low.astype(F32), step)

    @pl.when(step == 0)
    def _():
        weights.wait(0, me, arrays, ow, sems)

    gc_ref[...] = matmul_right(low, flat(ow[...])).astype(BF16)


def ffn_back(net, me, flows, gs, gs_low, slope, normed, spread, first_gain):
    tokens, width = gs.shape
    hidden = slope.shape[1]
    tile = min(256, tokens)
    weights = Weights(net, me, [(flow, 0) for flow in flows])
    tiled, wide = tile_spec(tile, width), tile_spec(tile, hidden)
    ins = (
        [(me.reshape(1), SMEM_SPEC)]
        + [(array, ANY_SPEC) for array in weights.arrays]
        + [(gs, tiled), (gs_low, tiled), (slope, wide), (normed, tiled)]
        + [(spread, tile_spec(tile, 1)), (first_gain, full_spec(first_gain.shape))]
    )
    row = ((1, width), F32, full_spec((1, width)))
    outs = [
        ((tokens, hidden), BF16, wide),
        ((tokens, width), F32, tiled),
        ((tokens, width), BF16, tiled),
        ((tokens, width), BF16, tiled),
        ((1, hidden), F32, full_spec((1, hidden))),
        row,
        row,
        row,
    ]
    return call(
        functools.partial(ffn_back_body, weights, 512),
        "ffn_back",
        (tokens // tile,),
        ins,
        outs,
        weights.scratch() + [pltpu.VMEM((tile, width), F32)],
        2 * tokens * width * (2 * hidden + width),
        60,
        4 * width * hidden + 4 * tokens * hidden + 20 * tokens * width,
    )


def product_body(rows, me_ref, a_ref, b_ref, keep_ref, send_ref):
    core = me_ref[0] & 1
    total = matmul_left(a_ref[...], b_ref[...])
    total = total.reshape(-1, 2, rows, total.shape[-1])
    low, high = total[:, 0], total[:, 1]
    keep_ref[...] = jnp.where(core == 0, low, high).astype(BF16)
    send_ref[...] = jnp.where(core == 0, high, low).astype(BF16)


def product(net, me, left, right, tile=512, lanes=512):
    tokens, width = left.shape
    columns = right.shape[1]
    rows = width // net.n
    lanes = min(lanes, columns)
    shape = (net.n // 2, rows, columns)
    block = pl.BlockSpec((tile // (2 * rows), rows, lanes), lambda i, j: (i, 0, j))
    return call(
        functools.partial(product_body, rows),
        "product",
        (width // tile, columns // lanes),
        [
            (me.reshape(1), SMEM_SPEC),
            (left, pl.BlockSpec((tokens, tile), lambda i, j: (0, i))),
            (right, pl.BlockSpec((tokens, lanes), lambda i, j: (0, j))),
        ],
        [(shape, BF16, block), (shape, BF16, block)],
        [],
        2 * tokens * width * columns,
        48,
        2 * (tokens * width + tokens * columns + width * columns),
    )


def stream_back_body(weights, tile, row_length, me_ref, *refs):
    count = len(weights.arrays)
    arrays, refs = refs[:count], refs[count:]
    gm_ref, gq_ref, gk_ref, gv_ref, out_ref, gt_ref, qbg_ref, vbg_ref = refs[:8]
    qw, kw, vw, sems = refs[8:12]
    me, step = me_ref[0], pl.program_id(0)

    @pl.when(step == 0)
    def _():
        for w, held in enumerate((qw, kw, vw)):
            weights.start(w, me, arrays, held, sems)
        for w, held in enumerate((qw, kw, vw)):
            weights.wait(w, me, arrays, held, sems)

    add_to(qbg_ref, gq_ref[...].astype(F32), step)
    add_to(vbg_ref, gv_ref[...].astype(F32), step)
    total = (
        gm_ref[...]
        + matmul_right(gq_ref[...], flat(qw[...]))
        + matmul_right(gk_ref[...], flat(kw[...]))
        + matmul_right(gv_ref[...], flat(vw[...]))
    )
    out_ref[...] = total
    row = pl.ds(step * tile // row_length, 1)
    part = jnp.sum(total, axis=0, keepdims=True)
    opens = lax.rem(step * tile, row_length) == 0
    gt_ref[row, :] = part + jnp.where(opens, 0.0, gt_ref[row, :])


def stream_back(net, me, flow_tq, flow_kv, gm, gq, gk, gv, rows):
    tokens, width = gm.shape
    row_length = tokens // rows
    tile = min(256, row_length)
    weights = Weights(net, me, [(flow_tq, 1), (flow_kv, 0), (flow_kv, 1)])
    tiled = tile_spec(tile, width)
    row = ((1, width), F32, full_spec((1, width)))
    return call(
        functools.partial(stream_back_body, weights, tile, row_length),
        "stream_back",
        (tokens // tile,),
        [(me.reshape(1), SMEM_SPEC)]
        + [(array, ANY_SPEC) for array in weights.arrays]
        + [(array, tiled) for array in (gm, gq, gk, gv)],
        [((tokens, width), F32, tiled), ((rows, width), F32, full_spec((rows, width))), row, row],
        weights.scratch(),
        6 * tokens * width * width,
        40,
        6 * width * width + 14 * tokens * width,
    )


def in_order(net, me, pieces):
    blocks = jnp.concatenate([array for _, array in pieces])
    order = jnp.asarray([source for own, _ in pieces for source in own], jnp.int32)
    place = jnp.zeros((net.n,), jnp.int32).at[order].set(jnp.arange(net.n, dtype=jnp.int32))
    return blocks[place[jnp.arange(net.n) ^ me]]


def on_device(
    net,
    inputs,
    timesteps,
    segments,
    cotangent,
    query_weight,
    key_weight,
    value_weight,
    output_weight,
    inner_weight,
    outer_weight,
    time_weight,
    *vectors,
):
    n = net.n
    me = lax.axis_index("fsdp").astype(jnp.int32)
    batch_count, row_count, row_length, model_width = inputs.shape
    rows = batch_count * row_count
    tokens = rows * row_length
    order_a = (net.outer, net.middle, net.near, net.core)
    order_b = (net.outer, net.near, net.middle, net.core)
    back_a = (net.near, net.middle, net.outer)
    back_b = (net.middle, net.near, net.outer)

    feats = features(timesteps.reshape(rows)).astype(BF16)
    sizes = [vector.shape[0] for vector in vectors]
    small = jnp.concatenate(list(vectors) + [feats.reshape(-1)])[None]

    small = in_order(net, me, net.gather(small, order_a))[:, 0]
    flow_tq = net.gather(jnp.stack([time_weight, query_weight]), order_a)
    flow_kv = net.gather(jnp.stack([key_weight, value_weight]), order_b)
    flow_o = net.gather(output_weight[None], order_a)
    flow_i = net.gather(inner_weight[None], order_b)
    flow_u = net.gather(outer_weight[None], order_a)

    gathered, start = [], 0
    for size in sizes:
        gathered.append(small[:, start : start + size].reshape(1, -1).astype(F32))
        start += size
    (query_bias, value_bias, output_bias, inner_bias, outer_bias) = gathered[:5]
    (first_gain, first_shift, second_gain, second_shift) = gathered[5:]
    feats_all = small[:, start:].reshape(n * rows, model_width)

    segments = segments.reshape(rows, row_length)
    x = inputs.reshape(tokens, model_width)
    temb, stream_low, queries, key_rows, values = project(
        net, me, flow_tq, flow_kv, feats, x, query_bias, value_bias, row_length
    )
    context, log_total = attend(queries, key_rows, values, segments)
    (
        layer_output,
        first_low,
        normed_first,
        spread_first,
        active_low,
        slope,
        grad_second,
        grad_second_low,
        second_gain_grad,
        second_shift_grad,
        outer_bias_grad,
    ) = ffn(
        net,
        me,
        (flow_o, flow_i, flow_u),
        context,
        x,
        temb,
        cotangent.reshape(tokens, model_width),
        (output_bias, inner_bias, outer_bias, first_gain, first_shift, second_gain, second_shift),
        row_length,
    )
    outer_halves = product(net, me, active_low, grad_second_low)
    (
        grad_inner_low,
        grad_mixed,
        grad_mixed_low,
        grad_context,
        inner_bias_grad,
        first_gain_grad,
        first_shift_grad,
        output_bias_grad,
    ) = ffn_back(
        net,
        me,
        (flow_o, flow_i, flow_u),
        grad_second,
        grad_second_low,
        slope,
        normed_first,
        spread_first,
        first_gain,
    )
    inner_halves = product(net, me, first_low, grad_inner_low)
    output_halves = product(net, me, context, grad_mixed_low)
    grad_queries, grad_keys, grad_values = attend_back(
        queries, key_rows, values, segments, log_total, grad_context
    )
    query_halves = product(net, me, stream_low, grad_queries)
    key_halves = product(net, me, stream_low, grad_keys)
    value_halves = product(net, me, stream_low, grad_values)
    grad_stream, grad_temb, query_bias_grad, value_bias_grad = stream_back(
        net, me, flow_tq, flow_kv, grad_mixed, grad_queries, grad_keys, grad_values, rows
    )

    outer_weight_grad = net.scatter(outer_halves, back_a, me)
    inner_weight_grad = net.scatter(inner_halves, back_b, me)
    output_weight_grad = net.scatter(output_halves, back_a, me)
    query_weight_grad = net.scatter(query_halves, back_a, me)
    key_weight_grad = net.scatter(key_halves, back_b, me)
    value_weight_grad = net.scatter(value_halves, back_a, me)
    temb_all = in_order(net, me, net.gather(grad_temb, order_a)).reshape(n * rows, model_width)
    own = model_width // n
    feats_own = lax.dynamic_slice_in_dim(feats_all, me * own, own, 1)
    time_weight_grad = lax.dot_general(
        feats_own.astype(F32),
        temb_all,
        (((0,), (0,)), ((), ())),
        precision=lax.Precision.HIGHEST,
    )
    vector_grads = [
        query_bias_grad,
        value_bias_grad,
        output_bias_grad,
        inner_bias_grad,
        outer_bias_grad,
        first_gain_grad,
        first_shift_grad,
        second_gain_grad,
        second_shift_grad,
    ]
    vector_sums = jnp.concatenate([grad.reshape(n, -1) for grad in vector_grads], axis=1)
    vector_sums = net.scatter_whole(vector_sums[:, None], back_a, me)[0]
    vector_outs, start = [], 0
    for size in sizes:
        vector_outs.append(vector_sums[start : start + size])
        start += size

    shape = inputs.shape
    return (
        layer_output.reshape(shape),
        grad_stream.reshape(shape),
        query_weight_grad,
        key_weight_grad,
        value_weight_grad,
        output_weight_grad,
        inner_weight_grad,
        outer_weight_grad,
        time_weight_grad,
    ) + tuple(vector_outs)


def solution(mesh):
    matrix, vector = P("fsdp", None), P("fsdp")
    batch = P(None, "fsdp", None, None)
    return jax.shard_map(
        functools.partial(on_device, Net(mesh.shape["fsdp"])),
        mesh=mesh,
        in_specs=(batch, P(None, "fsdp"), P(None, "fsdp", None), batch)
        + (matrix,) * 7
        + (vector,) * 9,
        out_specs=(batch, batch) + (matrix,) * 7 + (vector,) * 9,
        check_vma=False,
    )
```

time: 1620 us -> 784 us (0.48)
  waiting for transfers between devices: 1030 us -> 294 us
  matrix products: 332 us -> 1.7 us
  Pallas kernels: 0 us -> 264 us
  blocking collectives: 123 us -> 0 us
  starting transfers between devices: 1.31 us -> 102 us
  other arithmetic: 64.5 us -> 34.1 us
  local copies, waits for them, and re-layouts: 47.2 us -> 76.8 us
    reduce_scatter x7 -> x0, waiting for transfers between devices: 827 us -> none  [on_device(): totals = lax.psum_scatter(totals, 'fsdp', scatter_dimension=0, tiled=True)]
    dot_general x50 -> x1, matrix products: 332 us -> 1.7 us  [on_device(): lax.dot_general(feats_own.astype(F32), temb_all, (((0,), (0,)), ((), ()))...]
    ppermute x0 -> x112, waiting for transfers between devices: none -> 294 us  [swap(): return lax.ppermute(array, 'fsdp', [(i, i ^ mask) for i in range(self.n)])]
    pallas_call x0 -> x12, Pallas kernels: none -> 264 us  [call(): pl.pallas_call(body, grid=grid, in_specs=[spec for _, spec in ins], out_s...]
    all_gather x7 -> x0, waiting for transfers between devices: 200 us -> none  [the longest x1 52.6 us: collect(): lax.all_gather(params[2], 'fsdp', axis=0, tiled=True)]
    ppermute x0 -> x112, starting transfers between devices: none -> 102 us  [swap(): return lax.ppermute(array, 'fsdp', [(i, i ^ mask) for i in range(self.n)])]
    unnamed x2 -> x0, blocking collectives: 83.1 us -> none
    all_gather x1 -> x0, blocking collectives: 40.2 us -> none  [collect(): lax.all_gather(params[10], 'fsdp', axis=0, tiled=True)]
  transfers between devices with their start and end apart: 14 -> 112, of which waited for: 12 -> 41; matrix products, arithmetic and copies ran while one was open for 21% -> 9% of each run, Pallas kernels for 0% -> 12%
where the time goes in v1:
time: 784 us; the launch traced here: 775 us
  waiting for transfers between devices  294 us (38%)
  Pallas kernels  264 us (34%)
  starting transfers between devices  102 us (13%)
  local copies, waits for them, and re-layouts  76.8 us (10%)
  other arithmetic  34.1 us (4%)
    ppermute x112, waiting for transfers between devices, swap(): return lax.ppermute(array, 'fsdp', [(i, i ^ mask) for i in range(self.n)])  294 us
    pallas_call x12, Pallas kernels, call(): pl.pallas_call(body, grid=grid, in_specs=[spec for _, spec in ins], out_s...  264 us
    ppermute x112, starting transfers between devices, swap(): return lax.ppermute(array, 'fsdp', [(i, i ^ mask) for i in range(self.n)])  102 us
    unnamed x201, local copies, waits for them, and re-layouts  40.2 us
  transfers between devices with their start and end apart: 112, of which 41 were waited for; matrix products, arithmetic and copies ran while one was open for 9% of the time, Pallas kernels for 12%

profile of v1, /device:TPU:0, one launch (start us, length us, event | category | flops | bytes accessed | tf_op | source)
XLA Modules:
  0.0 774.7 jit_solution(11009155171395409377)
XLA Ops:
  34.5 22.5 %collective-permute-done = bf16[1,32,1024]{2,1,0:T(8,128)(2,1)S(1)} collective-permute-done((bf16[1,32,1024]{2,1,0:T(8,128)(2,1)}, bf16[1,32,1024]{2,1,0:T(8,128)(2,1)S(1)}, u32[]{:S(2)}, u32[]{:S(2)}) %collective-permute-start) | collective-permute-done | bytes 65568 | tf_op jit(solution)/shard_map/ppermute | solution.py:80
  76.5 13.2 %collective-permute-done.10 = bf16[1,32,4096]{2,1,0:T(8,128)(2,1)S(1)} collective-permute-done((bf16[1,32,4096]{2,1,0:T(8,128)(2,1)}, bf16[1,32,4096]{2,1,0:T(8,128)(2,1)S(1)}, u32[]{:S(2)}, u32[]{:S(2)}) %collective-permute-start.10) | collective-permute-done | bytes 262176 | tf_op jit(solution)/shard_map/ppermute | solution.py:80
  91.8 12.9 %collective-permute-done.20 = bf16[1,128,1024]{2,1,0:T(8,128)(2,1)S(1)} collective-permute-done((bf16[1,128,1024]{2,1,0:T(8,128)(2,1)}, bf16[1,128,1024]{2,1,0:T(8,128)(2,1)S(1)}, u32[]{:S(2)}, u32[]{:S(2)}) %collective-permute-start.20) | collective-permute-done | bytes 262176 | tf_op jit(solution)/shard_map/ppermute | solution.py:80
  108.8 6.6 collective-permute-done.5.refs_3_
  117.4 9.3 %collective-permute-done.43.refs_9_ = bf16[4,2,32,1024]{3,2,1,0:T(8,128)(2,1)S(1)} collective-permute-done((bf16[4,2,32,1024]{3,2,1,0:T(8,128)(2,1)S(1)}, bf16[4,2,32,1024]{3,2,1,0:T(8,128)(2,1)S(1)}, u32[]{:S(2)}, u32[]{:S(2)}) %collective-permute-start.43) | collective-permute-done | bytes 524320 | tf_op jit(solution)/shard_map/ppermute | solution.py:80
  127.2 10.2 %collective-permute-done.34.refs_2_ = bf16[4,2,32,1024]{3,2,1,0:T(8,128)(2,1)S(1)} collective-permute-done((bf16[4,2,32,1024]{3,2,1,0:T(8,128)(2,1)S(1)}, bf16[4,2,32,1024]{3,2,1,0:T(8,128)(2,1)S(1)}, u32[]{:S(2)}, u32[]{:S(2)}) %collective-permute-start.34) | collective-permute-done | bytes 524320 | tf_op jit(solution)/shard_map/ppermute | solution.py:80
  143.1 7.9 %collective-permute-done.45.refs_11_ = bf16[4,2,32,1024]{3,2,1,0:T(8,128)(2,1)S(1)} collective-permute-done((bf16[4,2,32,1024]{3,2,1,0:T(8,128)(2,1)S(1)}, bf16[4,2,32,1024]{3,2,1,0:T(8,128)(2,1)S(1)}, u32[]{:S(2)}, u32[]{:S(2)}) %collective-permute-start.45) | collective-permute-done | bytes 524320 | tf_op jit(solution)/shard_map/ppermute | solution.py:80
  155.1 46.0 %collective-permute-done.35.refs_3_ = bf16[4,2,32,1024]{3,2,1,0:T(8,128)(2,1)S(1)} collective-permute-done((bf16[4,2,32,1024]{3,2,1,0:T(8,128)(2,1)S(1)}, bf16[4,2,32,1024]{3,2,1,0:T(8,128)(2,1)S(1)}, u32[]{:S(2)}, u32[]{:S(2)}) %collective-permute-start.35) | collective-permute-done | bytes 524320 | tf_op jit(solution)/shard_map/ppermute | solution.py:80
  206.9 21.3 %collective-permute-done.14.refs_10_ = bf16[4,1,32,4096]{3,2,1,0:T(8,128)(2,1)} collective-permute-done((bf16[4,1,32,4096]{3,2,1,0:T(8,128)(2,1)}, bf16[4,1,32,4096]{3,2,1,0:T(8,128)(2,1)}, u32[]{:S(2)}, u32[]{:S(2)}) %collective-permute-start.14) | collective-permute-done | bytes 1048608 | tf_op jit(solution)/shard_map/ppermute | solution.py:80
  237.9 11.6 %collective-permute-done.15.refs_11_ = bf16[4,1,32,4096]{3,2,1,0:T(8,128)(2,1)} collective-permute-done((bf16[4,1,32,4096]{3,2,1,0:T(8,128)(2,1)}, bf16[4,1,32,4096]{3,2,1,0:T(8,128)(2,1)}, u32[]{:S(2)}, u32[]{:S(2)}) %collective-permute-start.15) | collective-permute-done | bytes 1048608 | tf_op jit(solution)/shard_map/ppermute | solution.py:80
  258.9 23.0 %project.1 = (f32[2,1024]{1,0:T(2,128)S(1)}, bf16[1024,1024]{1,0:T(8,128)(2,1)S(1)}, bf16[1024,1024]{1,0:T(8,128)(2,1)S(1)}, bf16[1024,1024]{1,0:T(8,128)(2,1)}, bf16[1024,1024]{1,0:T(8,128)(2,1)}) custom-call(s32[1]{0:T(128)} %bitcast.me_ref, bf16[4,2,32,1024]{3,2,1,0:T(8,128)(2,1)S(1)} %pad_maximum_fusion.2.refs_0_, ...), custom_call_target="tpu_custom_call" | custom-call | flops 6442450944 | bytes 18874368 | tf_op jit(solution)/shard_map/project/pallas_call | solution.py:193
  287.3 23.5 %attend.1 = (bf16[1024,1024]{1,0:T(8,128)(2,1)S(1)}, f32[2,8,2,512]{3,2,1,0:T(2,128)S(1)}) custom-call(s32[2,512,1]{2,1,0:T(8,128)S(1)} %broadcast_in_dim_reshape.5.segc_ref, s32[2,1,512]{2,1,0:T(1,128)S(1)} %copy-done.7, bf16[1024,1024]{1,0:T(8,128)(2,1)S(1)} %get-tuple-element.63.q_ref, bf16[1024,1024]{1,0:T(8,128)(2,1)S(1)} %copy-done.54, ...), custom_call_target="tpu_custom_call" | custom-call | flops 8589934592 | bytes 8388608 | tf_op jit(solution)/shard_map/attend/pallas_call | solution.py:193
  314.1 49.7 %ffn.1 = (bf16[1024,1024]{1,0:T(8,128)(2,1)}, bf16[1024,1024]{1,0:T(8,128)(2,1)}, f32[1024,1024]{1,0:T(8,128)}, f32[1024,1]{1,0:T(8,128)}, bf16[1024,4096]{1,0:T...) custom-call(s32[1]{0:T(128)} %bitcast.me_ref, ...), custom_call_target="tpu_custom_call" | custom-call | flops 19327352832 | bytes 54525952 | tf_op jit(solution)/shard_map/ffn/pallas_call | solution.py:193
  363.9 45.9 %ffn_back.1 = (bf16[1024,4096]{1,0:T(8,128)(2,1)}, f32[1024,1024]{1,0:T(8,128)}, bf16[1024,1024]{1,0:T(8,128)(2,1)}, bf16[1024,1024]{1,0:T(8,128)(2,1)}, f32[1,4...) custom-call(s32[1]{0:T(128)} %bitcast.me_ref, bf16[4,1,32,1024]{3,2,1,0:T(8,128)(2,1)} %copy-done.77, ...), custom_call_target="tpu_custom_call" | custom-call | flops 19327352832 | bytes 54525952 | tf_op jit(solution)/shard_map/ffn_back/pallas_call | solution.py:193
  414.5 39.2 %attend_back.1 = (bf16[1024,1024]{1,0:T(8,128)(2,1)S(1)}, bf16[1024,1024]{1,0:T(8,128)(2,1)S(1)}, bf16[1024,1024]{1,0:T(8,128)(2,1)S(1)}) custom-call(s32[2,512,1]{2,1,0:T(8,128)S(1)} %broadcast_in_dim_reshape.5.segc_ref, s32[2,1,512]{2,1,0:T(1,128)S(1)} %copy-done.7, bf16[1024,1024]{1,0:T(8,128)(2,1)S(1)} %copy-done.53, bf16[1024,1024]{1,0:T(8,128)(2,1)S(1)} %copy-done.55, ...), custom_call_target="tpu_custom_call" | custom-call | flops 21474836480 | bytes 14680064 | tf_op jit(solution)/shard_map/attend_back/pallas_call | solution.py:193
  468.8 6.3 product.6
  478.9 21.1 %stream_back.1 = (f32[1024,1024]{1,0:T(8,128)}, f32[2,1024]{1,0:T(2,128)S(1)}, f32[1,1024]{1,0:T(1,128)S(1)}, f32[1,1024]{1,0:T(1,128)S(1)}) custom-call(s32[1]{0:T(128)} %bitcast.me_ref, bf16[4,2,32,1024]{3,2,1,0:T(8,128)(2,1)S(1)} %copy-done.6, bf16[4,2,32,1024]{3,2,1,0:T(8,128)(2,1)S(1)} %copy-done.24, bf16[4,2,32,1024]{3,2,1,0:T(8,128)(2,1)S(1)} %copy-done.21, ...), custom_call_target="tpu_custom_call" | custom-call | flops 6442450944 | bytes 20971520 | tf_op jit(solution)/shard_map/stream_back/pallas_call | solution.py:193
  506.1 18.9 %product.11 = (bf16[16,128,1024]{2,1,0:T(8,128)(2,1)}, bf16[16,128,1024]{2,1,0:T(8,128)(2,1)}) custom-call(s32[1]{0:T(128)} %bitcast.me_ref, bf16[1024,4096]{1,0:T(8,128)(2,1)} %get-tuple-element.95.a_ref, bf16[1024,1024]{1,0:T(8,128)(2,1)S(1)} %copy-done.59), custom_call_target="tpu_custom_call" | custom-call | flops 8589934592 | bytes 18874368 | tf_op jit(solution)/shard_map/product/pallas_call | solution.py:193
  543.5 19.7 %product.10 = (bf16[16,32,4096]{2,1,0:T(8,128)(2,1)}, bf16[16,32,4096]{2,1,0:T(8,128)(2,1)}) custom-call(s32[1]{0:T(128)} %bitcast.me_ref, bf16[1024,1024]{1,0:T(8,128)(2,1)S(1)} %copy-done.58, bf16[1024,4096]{1,0:T(8,128)(2,1)} %get-tuple-element.92.b_ref), custom_call_target="tpu_custom_call" | custom-call | flops 8589934592 | bytes 18874368 | tf_op jit(solution)/shard_map/product/pallas_call | solution.py:193
  636.3 10.6 %collective-permute-done.79 = bf16[8,32,1024]{2,1,0:T(8,128)(2,1)S(1)} collective-permute-done((bf16[8,32,1024]{2,1,0:T(8,128)(2,1)S(1)}, bf16[8,32,1024]{2,1,0:T(8,128)(2,1)S(1)}, u32[]{:S(2)}, u32[]{:S(2)}) %collective-permute-start.79) | collective-permute-done | bytes 524320 | tf_op jit(solution)/shard_map/ppermute | solution.py:80
  653.2 30.9 %collective-permute-done.62 = bf16[4,32,1024]{2,1,0:T(8,128)(2,1)S(1)} collective-permute-done((bf16[4,32,1024]{2,1,0:T(8,128)(2,1)S(1)}, bf16[4,32,1024]{2,1,0:T(8,128)(2,1)S(1)}, u32[]{:S(2)}, u32[]{:S(2)}) %collective-permute-start.62) | collective-permute-done | bytes 262176 | tf_op jit(solution)/shard_map/ppermute | solution.py:80
  721.1 13.1 %collective-permute-done.92 = bf16[4,128,1024]{2,1,0:T(8,128)(2,1)S(1)} collective-permute-done((bf16[4,128,1024]{2,1,0:T(8,128)(2,1)S(1)}, bf16[4,128,1024]{2,1,0:T(8,128)(2,1)S(1)}, u32[]{:S(2)}, u32[]{:S(2)}) %collective-permute-start.92) | collective-permute-done | bytes 1048608 | tf_op jit(solution)/shard_map/ppermute | solution.py:80
  744.0 12.3 %collective-permute-done.93 = bf16[1,128,1024]{2,1,0:T(8,128)(2,1)S(1)} collective-permute-done((bf16[1,128,1024]{2,1,0:T(8,128)(2,1)S(1)}, bf16[1,128,1024]{2,1,0:T(8,128)(2,1)S(1)}, u32[]{:S(2)}, u32[]{:S(2)}) %collective-permute-start.93) | collective-permute-done | bytes 262176 | tf_op jit(solution)/shard_map/ppermute | solution.py:80
  758.1 15.1 %collective-permute-done.87 = bf16[1,32,4096]{2,1,0:T(8,128)(2,1)S(1)} collective-permute-done((bf16[1,32,4096]{2,1,0:T(8,128)(2,1)S(1)}, bf16[1,32,4096]{2,1,0:T(8,128)(2,1)S(1)}, u32[]{:S(2)}, u32[]{:S(2)}) %collective-permute-start.87) | collective-permute-done | bytes 262176 | tf_op jit(solution)/shard_map/ppermute | solution.py:80
  (526 shorter events, 281.4 us)
Async XLA Ops:
  29.8 43.6 %collective-permute-start.12 = (bf16[1,32,4096]{2,1,0:T(8,128)(2,1)}, bf16[1,32,4096]{2,1,0:T(8,128)(2,1)S(1)}, u32[]{:S(2)}, u32[]{:S(2)}) collective-permute-start(bf16[1,32,4096]{2,1,0:T(8,128)(2,1)} %bitcast.408), channel_id=1, source_target_pairs={{0,24},{1,25},{2,26},{3,27},{4,28},{5,29},{6,30},{7,31},{8,16},{9,... | collective-permute-start | bytes 786440 | tf_op jit(solution)/shard_map/ppermute | solution.py:80
  139.6 61.5 %collective-permute-start.26 = (bf16[4,1,128,1024]{3,2,1,0:T(8,128)(2,1)}, bf16[4,1,128,1024]{3,2,1,0:T(8,128)(2,1)S(1)}, u32[]{:S(2)}, u32[]{:S(2)}) collective-permute-start(bf16[4,1,128,1024]{3,2,1,0:T(8,128)(2,1)} %pad_maximum_fusion.1.refs_16_), channel_id=1, source_target_pairs={{0,1},{1,0},{2,3},{3,2},{4,5},{5,4},{6,7},{7,6},{8,9},{9,8},{10,11... | collective-permute-start | bytes 3145736 | tf_op jit(solution)/shard_map/ppermute | solution.py:80
  141.6 61.8 %collective-permute-start.24 = (bf16[4,1,128,1024]{3,2,1,0:T(8,128)(2,1)}, bf16[4,1,128,1024]{3,2,1,0:T(8,128)(2,1)}, u32[]{:S(2)}, u32[]{:S(2)}) collective-permute-start(bf16[4,1,128,1024]{3,2,1,0:T(8,128)(2,1)} %pad_maximum_fusion.1.refs_16_), channel_id=1, source_target_pairs={{0,2},{1,3},{2,0},{3,1},{4,6},{5,7},{6,4},{7,5},{8,10},{9,11},{10,... | collective-permute-start | bytes 3145736 | tf_op jit(solution)/shard_map/ppermute | solution.py:80
  150.9 52.5 %collective-permute-start.23 = (bf16[4,1,128,1024]{3,2,1,0:T(8,128)(2,1)}, bf16[4,1,128,1024]{3,2,1,0:T(8,128)(2,1)}, u32[]{:S(2)}, u32[]{:S(2)}) collective-permute-start(bf16[4,1,128,1024]{3,2,1,0:T(8,128)(2,1)} %pad_maximum_fusion.1.refs_16_), channel_id=1, source_target_pairs={{0,4},{1,5},{2,6},{3,7},{4,0},{5,1},{6,2},{7,3},{8,12},{9,13},{10,... | collective-permute-start | bytes 3145736 | tf_op jit(solution)/shard_map/ppermute | solution.py:80
  152.2 52.7 %collective-permute-start.13 = (bf16[4,1,32,4096]{3,2,1,0:T(8,128)(2,1)}, bf16[4,1,32,4096]{3,2,1,0:T(8,128)(2,1)}, u32[]{:S(2)}, u32[]{:S(2)}) collective-permute-start(bf16[4,1,32,4096]{3,2,1,0:T(8,128)(2,1)} %pad_maximum_fusion.refs_8_), channel_id=1, source_target_pairs={{0,2},{1,3},{2,0},{3,1},{4,6},{5,7},{6,4},{7,5},{8,10},{9,11},{10,... | collective-permute-start | bytes 3145736 | tf_op jit(solution)/shard_map/ppermute | solution.py:80
  154.5 46.5 %collective-permute-start.35 = (bf16[4,2,32,1024]{3,2,1,0:T(8,128)(2,1)S(1)}, bf16[4,2,32,1024]{3,2,1,0:T(8,128)(2,1)S(1)}, u32[]{:S(2)}, u32[]{:S(2)}) collective-permute-start(bf16[4,2,32,1024]{3,2,1,0:T(8,128)(2,1)S(1)} %collective-permute-done.33.refs_1_), channel_id=1, source_target_pairs={{0,2},{1,3},{2,0},{3,1},{4,6},{5,7},{6,4},{7,5},{8,10},{9,11},{10,... | collective-permute-start | bytes 1572872 | tf_op jit(solution)/shard_map/ppermute | solution.py:80
  203.4 34.0 %collective-permute-start.28 = (bf16[4,1,128,1024]{3,2,1,0:T(8,128)(2,1)}, bf16[4,1,128,1024]{3,2,1,0:T(8,128)(2,1)}, u32[]{:S(2)}, u32[]{:S(2)}) collective-permute-start(bf16[4,1,128,1024]{3,2,1,0:T(8,128)(2,1)} %collective-permute-done.24.refs_18_), channel_id=1, source_target_pairs={{0,1},{1,0},{2,3},{3,2},{4,5},{5,4},{6,7},{7,6},{8,9},{9,8},{10,11... | collective-permute-start | bytes 3145736 | tf_op jit(solution)/shard_map/ppermute | solution.py:80
  203.4 34.5 %collective-permute-start.25 = (bf16[4,1,128,1024]{3,2,1,0:T(8,128)(2,1)}, bf16[4,1,128,1024]{3,2,1,0:T(8,128)(2,1)}, u32[]{:S(2)}, u32[]{:S(2)}) collective-permute-start(bf16[4,1,128,1024]{3,2,1,0:T(8,128)(2,1)} %collective-permute-done.23.refs_17_), channel_id=1, source_target_pairs={{0,2},{1,3},{2,0},{3,1},{4,6},{5,7},{6,4},{7,5},{8,10},{9,11},{10,... | collective-permute-start | bytes 3145736 | tf_op jit(solution)/shard_map/ppermute | solution.py:80
  204.9 44.6 %collective-permute-start.15 = (bf16[4,1,32,4096]{3,2,1,0:T(8,128)(2,1)}, bf16[4,1,32,4096]{3,2,1,0:T(8,128)(2,1)}, u32[]{:S(2)}, u32[]{:S(2)}) collective-permute-start(bf16[4,1,32,4096]{3,2,1,0:T(8,128)(2,1)} %collective-permute-done.13.refs_9_), channel_id=1, source_target_pairs={{0,4},{1,5},{2,6},{3,7},{4,0},{5,1},{6,2},{7,3},{8,12},{9,13},{10,... | collective-permute-start | bytes 3145736 | tf_op jit(solution)/shard_map/ppermute | solution.py:80
  236.8 75.3 %collective-permute-start.27 = (bf16[4,1,128,1024]{3,2,1,0:T(8,128)(2,1)}, bf16[4,1,128,1024]{3,2,1,0:T(8,128)(2,1)S(1)}, u32[]{:S(2)}, u32[]{:S(2)}) collective-permute-start(bf16[4,1,128,1024]{3,2,1,0:T(8,128)(2,1)} %collective-permute-done.23.refs_17_), channel_id=1, source_target_pairs={{0,1},{1,0},{2,3},{3,2},{4,5},{5,4},{6,7},{7,6},{8,9},{9,8},{10,11... | collective-permute-start | bytes 3145736 | tf_op jit(solution)/shard_map/ppermute | solution.py:80
  237.3 76.8 %collective-permute-start.17 = (bf16[4,1,32,4096]{3,2,1,0:T(8,128)(2,1)}, bf16[4,1,32,4096]{3,2,1,0:T(8,128)(2,1)}, u32[]{:S(2)}, u32[]{:S(2)}) collective-permute-start(bf16[4,1,32,4096]{3,2,1,0:T(8,128)(2,1)} %collective-permute-done.13.refs_9_), channel_id=1, source_target_pairs={{0,1},{1,0},{2,3},{3,2},{4,5},{5,4},{6,7},{7,6},{8,9},{9,8},{10,11... | collective-permute-start | bytes 3145736 | tf_op jit(solution)/shard_map/ppermute | solution.py:80
  237.4 75.7 %collective-permute-start.18 = (bf16[4,1,32,4096]{3,2,1,0:T(8,128)(2,1)}, bf16[4,1,32,4096]{3,2,1,0:T(8,128)(2,1)S(1)}, u32[]{:S(2)}, u32[]{:S(2)}) collective-permute-start(bf16[4,1,32,4096]{3,2,1,0:T(8,128)(2,1)} %collective-permute-done.14.refs_10_), channel_id=1, source_target_pairs={{0,1},{1,0},{2,3},{3,2},{4,5},{5,4},{6,7},{7,6},{8,9},{9,8},{10,11... | collective-permute-start | bytes 3145736 | tf_op jit(solution)/shard_map/ppermute | solution.py:80
  237.8 76.3 %collective-permute-start.29 = (bf16[4,1,128,1024]{3,2,1,0:T(8,128)(2,1)}, bf16[4,1,128,1024]{3,2,1,0:T(8,128)(2,1)}, u32[]{:S(2)}, u32[]{:S(2)}) collective-permute-start(bf16[4,1,128,1024]{3,2,1,0:T(8,128)(2,1)} %collective-permute-done.25.refs_19_), channel_id=1, source_target_pairs={{0,1},{1,0},{2,3},{3,2},{4,5},{5,4},{6,7},{7,6},{8,9},{9,8},{10,11... | collective-permute-start | bytes 3145736 | tf_op jit(solution)/shard_map/ppermute | solution.py:80
  249.5 64.6 %collective-permute-start.19 = (bf16[4,1,32,4096]{3,2,1,0:T(8,128)(2,1)}, bf16[4,1,32,4096]{3,2,1,0:T(8,128)(2,1)}, u32[]{:S(2)}, u32[]{:S(2)}) collective-permute-start(bf16[4,1,32,4096]{3,2,1,0:T(8,128)(2,1)} %collective-permute-done.15.refs_11_), channel_id=1, source_target_pairs={{0,1},{1,0},{2,3},{3,2},{4,5},{5,4},{6,7},{7,6},{8,9},{9,8},{10,11... | collective-permute-start | bytes 3145736 | tf_op jit(solution)/shard_map/ppermute | solution.py:80
  500.0 68.9 %collective-permute-start.98 = (f32[2,1024]{1,0:T(2,128)S(1)}, f32[2,1024]{1,0:T(2,128)}, u32[]{:S(2)}, u32[]{:S(2)}) collective-permute-start(f32[2,1024]{1,0:T(2,128)S(1)} %get-tuple-element.98), channel_id=1, source_target_pairs={{0,24},{1,25},{2,26},{3,27},{4,28},{5,29},{6,30},{7,31},{8,16},{9,... | collective-permute-start | bytes 24584 | tf_op jit(solution)/shard_map/ppermute | solution.py:80
  502.1 67.0 %collective-permute-start.97 = (f32[2,1024]{1,0:T(2,128)S(1)}, f32[2,1024]{1,0:T(2,128)}, u32[]{:S(2)}, u32[]{:S(2)}) collective-permute-start(f32[2,1024]{1,0:T(2,128)S(1)} %get-tuple-element.98), channel_id=1, source_target_pairs={{0,8},{1,9},{2,10},{3,11},{4,12},{5,13},{6,14},{7,15},{8,0},{9,1},... | collective-permute-start | bytes 24584 | tf_op jit(solution)/shard_map/ppermute | solution.py:80
  502.1 67.3 %collective-permute-start.96 = (f32[2,1024]{1,0:T(2,128)S(1)}, f32[2,1024]{1,0:T(2,128)}, u32[]{:S(2)}, u32[]{:S(2)}) collective-permute-start(f32[2,1024]{1,0:T(2,128)S(1)} %get-tuple-element.98), channel_id=1, source_target_pairs={{0,16},{1,17},{2,18},{3,19},{4,20},{5,21},{6,22},{7,23},{8,24},{9,... | collective-permute-start | bytes 24584 | tf_op jit(solution)/shard_map/ppermute | solution.py:80
  567.9 54.6 %collective-permute-start.90 = (bf16[16,128,1024]{2,1,0:T(8,128)(2,1)}, bf16[16,128,1024]{2,1,0:T(8,128)(2,1)}, u32[]{:S(2)}, u32[]{:S(2)}) collective-permute-start(bf16[16,128,1024]{2,1,0:T(8,128)(2,1)} %get-tuple-element.97), channel_id=1, source_target_pairs={{0,1},{1,0},{2,3},{3,2},{4,5},{5,4},{6,7},{7,6},{8,9},{9,8},{10,11... | collective-permute-start | bytes 12582920 | tf_op jit(solution)/shard_map/ppermute | solution.py:80
  569.1 57.6 %collective-permute-start.84 = (bf16[16,32,4096]{2,1,0:T(8,128)(2,1)}, bf16[16,32,4096]{2,1,0:T(8,128)(2,1)}, u32[]{:S(2)}, u32[]{:S(2)}) collective-permute-start(bf16[16,32,4096]{2,1,0:T(8,128)(2,1)} %get-tuple-element.94), channel_id=1, source_target_pairs={{0,1},{1,0},{2,3},{3,2},{4,5},{5,4},{6,7},{7,6},{8,9},{9,8},{10,11... | collective-permute-start | bytes 12582920 | tf_op jit(solution)/shard_map/ppermute | solution.py:80
  626.7 87.7 %collective-permute-start.91 = (bf16[8,128,1024]{2,1,0:T(8,128)(2,1)S(1)}, bf16[8,128,1024]{2,1,0:T(8,128)(2,1)S(1)}, u32[]{:S(2)}, u32[]{:S(2)}) collective-permute-start(bf16[8,128,1024]{2,1,0:T(8,128)(2,1)S(1)} %fusion), channel_id=1, source_target_pairs={{0,2},{1,3},{2,0},{3,1},{4,6},{5,7},{6,4},{7,5},{8,10},{9,11},{10,... | collective-permute-start | bytes 6291464 | tf_op jit(solution)/shard_map/ppermute | solution.py:80
  629.8 87.1 %collective-permute-start.85 = (bf16[8,32,4096]{2,1,0:T(8,128)(2,1)S(1)}, bf16[8,32,4096]{2,1,0:T(8,128)(2,1)S(1)}, u32[]{:S(2)}, u32[]{:S(2)}) collective-permute-start(bf16[8,32,4096]{2,1,0:T(8,128)(2,1)S(1)} %bitcast.343), channel_id=1, source_target_pairs={{0,4},{1,5},{2,6},{3,7},{4,0},{5,1},{6,2},{7,3},{8,12},{9,13},{10,... | collective-permute-start | bytes 6291464 | tf_op jit(solution)/shard_map/ppermute | solution.py:80
  635.7 48.4 %collective-permute-start.62 = (bf16[4,32,1024]{2,1,0:T(8,128)(2,1)S(1)}, bf16[4,32,1024]{2,1,0:T(8,128)(2,1)S(1)}, u32[]{:S(2)}, u32[]{:S(2)}) collective-permute-start(bf16[4,32,1024]{2,1,0:T(8,128)(2,1)S(1)} %fusion.6), channel_id=1, source_target_pairs={{0,4},{1,5},{2,6},{3,7},{4,0},{5,1},{6,2},{7,3},{8,12},{9,13},{10,... | collective-permute-start | bytes 786440 | tf_op jit(solution)/shard_map/ppermute | solution.py:80
  646.9 42.7 %collective-permute-start.74 = (bf16[4,32,1024]{2,1,0:T(8,128)(2,1)S(1)}, bf16[4,32,1024]{2,1,0:T(8,128)(2,1)S(1)}, u32[]{:S(2)}, u32[]{:S(2)}) collective-permute-start(bf16[4,32,1024]{2,1,0:T(8,128)(2,1)S(1)} %fusion.8), channel_id=1, source_target_pairs={{0,4},{1,5},{2,6},{3,7},{4,0},{5,1},{6,2},{7,3},{8,12},{9,13},{10,... | collective-permute-start | bytes 786440 | tf_op jit(solution)/shard_map/ppermute | solution.py:80
  652.5 40.2 %collective-permute-start.80 = (bf16[4,32,1024]{2,1,0:T(8,128)(2,1)S(1)}, bf16[4,32,1024]{2,1,0:T(8,128)(2,1)S(1)}, u32[]{:S(2)}, u32[]{:S(2)}) collective-permute-start(bf16[4,32,1024]{2,1,0:T(8,128)(2,1)S(1)} %fusion.9), channel_id=1, source_target_pairs={{0,4},{1,5},{2,6},{3,7},{4,0},{5,1},{6,2},{7,3},{8,12},{9,13},{10,... | collective-permute-start | bytes 786440 | tf_op jit(solution)/shard_map/ppermute | solution.py:80
  (183 other events, 3227.1 us)

commit v2 on v1

v2 whole, which is shorter than its diff:
```python
import functools
import math

import jax
import jax.numpy as jnp
from jax import lax
from jax.experimental import pallas as pl
from jax.experimental.pallas import tpu as pltpu
from jax.sharding import PartitionSpec as P

D = 1024
H = 16


INV_ROOT_TWO = 0.7071067811865476
INV_ROOT_TAU = 0.3989422804014327
F32 = jnp.float32
BF16 = jnp.bfloat16


def matmul(operand, factor):
    return jnp.dot(operand, factor, preferred_element_type=F32)


def matmul_left(operand, factor):
    return lax.dot_general(
        operand, factor, (((0,), (0,)), ((), ())), preferred_element_type=F32
    )


def matmul_right(operand, factor):
    return lax.dot_general(
        operand, factor, (((1,), (1,)), ((), ())), preferred_element_type=F32
    )


def features(step_ids):
    half_width = D // 2
    freqs = jnp.exp(-math.log(10000.0) * jnp.arange(half_width, dtype=F32) / half_width)
    angles = step_ids.astype(F32)[..., None] * freqs
    return jnp.concatenate([jnp.sin(angles), jnp.cos(angles)], axis=-1)


def normalize(values_in):
    center = values_in - jnp.mean(values_in, axis=-1, keepdims=True)
    spread = lax.rsqrt(jnp.mean(center * center, axis=-1, keepdims=True) + 1e-05)
    return (center * spread, spread)


def norm_back(grad_normed, normed, spread):
    mean_grad = jnp.mean(grad_normed, axis=-1, keepdims=True)
    mean_cross = jnp.mean(grad_normed * normed, axis=-1, keepdims=True)
    return spread * (grad_normed - mean_grad - normed * mean_cross)


class Net:
    def __init__(self, n):
        self.n = n
        self.bits = n.bit_length() - 1
        chip = self.bits - 1
        sizes = [(chip + 2 - i) // 3 for i in range(3)]
        groups, top = [], self.bits - 1
        for size in sizes:
            groups.append(tuple(range(top, top - size, -1)))
            top -= size
        self.outer, self.middle, self.near = groups
        self.core = (0,)

    def masks(self, group):
        found = []
        for pick in range(1, 1 << len(group)):
            mask = 0
            for place, bit in enumerate(group):
                if pick >> place & 1:
                    mask |= 1 << bit
            found.append(mask)
        return found

    def swap(self, array, mask):
        return lax.ppermute(array, "fsdp", [(i, i ^ mask) for i in range(self.n)])

    def gather_far(self, shard):
        return [shard] + [self.swap(shard, mask) for mask in self.masks(self.outer)]

    def stacked(self, parts):
        return ([0] + self.masks(self.outer), jnp.stack(parts))

    def gather_near(self, own):
        sources, array = own
        return [
            [(mask, self.swap(array, mask)) for mask in self.masks(group)]
            for group in (self.near, self.middle)
        ]

    def gather_corner(self, own, near):
        sources, half = own[0], len(own[0]) // 2
        pieces, corners, sent = [own], [], []
        for group in near:
            pieces += [([s ^ mask for s in sources], array) for mask, array in group]
        for mask_x, array_x in near[0]:
            for mask_y, array_y in near[1]:
                low, high = array_y[:half], array_x[half:]
                sent += [low, high]
                corner = mask_x ^ mask_y
                corners.append(([s ^ corner for s in sources[:half]], self.swap(low, mask_x)))
                corners.append(([s ^ corner for s in sources[half:]], self.swap(high, mask_y)))
        return pieces, corners, sent

    def gather_core(self, pieces):
        return pieces + [([s ^ 1 for s in own], self.swap(array, 1)) for own, array in pieces]

    def inner_masks(self):
        near, middle = self.masks(self.near), self.masks(self.middle)
        return near + middle + [x | y for x in near for y in middle]

    def gather_round(self, sources, array, masks):
        array = jnp.concatenate([array] + [self.swap(array, mask) for mask in masks])
        return [source ^ mask for mask in [0] + masks for source in sources], array

    def take(self, term, bits, mask, present, me):
        present = list(present)
        for bit in bits:
            place = present.index(bit)
            low = 1 << (len(present) - 1 - place)
            value = (me >> bit & 1) ^ (mask >> bit & 1)
            rest = term.shape[1:]
            term = term.reshape((1 << place, 2, low) + rest)
            term = lax.dynamic_index_in_dim(term, value, 1, keepdims=False)
            term = term.reshape((low << place,) + rest)
            present.remove(bit)
        return term

    def scatter_core(self, halves):
        keep, send = halves
        return [keep, self.swap(send, 1)], list(range(self.bits - 1, 0, -1))

    def added(self, parts, dtype):
        parts = [part.astype(F32) for part in parts]
        return sum(parts[1:], parts[0]).astype(dtype)

    def scatter_step(self, state, group, me):
        terms, present = state
        sent = []
        for mask in self.masks(group):
            parts = [self.take(term, group, mask, present, me) for term in terms]
            sent.append(self.added(parts, terms[0].dtype))
        received = [self.swap(part, mask) for part, mask in zip(sent, self.masks(group))]
        terms = [self.take(term, group, 0, present, me) for term in terms] + received
        return (terms, [bit for bit in present if bit not in group]), sent

    def scatter_corner(self, state, me):
        terms, present = state
        left = [bit for bit in present if bit not in self.near]
        found, sent = [], []
        for mask_x in self.masks(self.near):
            row = [self.take(term, self.near, mask_x, present, me) for term in terms]
            for mask_y in self.masks(self.middle):
                parts = [self.take(term, self.middle, mask_y, left, me) for term in row]
                half = parts[0].shape[0] // 2
                low = self.added([part[:half] for part in parts], terms[0].dtype)
                high = self.added([part[half:] for part in parts], terms[0].dtype)
                sent += [low, high]
                found.append((mask_x, mask_y, self.swap(low, mask_x), self.swap(high, mask_y)))
        return found, sent

    def scatter_near(self, state, corner, me):
        terms, present = state
        left = [bit for bit in present if bit not in self.near]
        mine, received, sent = [self.take(t, self.near, 0, present, me) for t in terms], [], []
        for mask_x in self.masks(self.near):
            row = [self.take(term, self.near, mask_x, present, me) for term in terms]
            parts = [self.take(term, self.middle, 0, left, me) for term in row]
            for mask, _, _, high in corner:
                if mask == mask_x:
                    parts.append(jnp.concatenate([jnp.zeros_like(high), high]))
            sent.append((self.added(parts, terms[0].dtype), mask_x))
        for mask_y in self.masks(self.middle):
            parts = [self.take(term, self.middle, mask_y, left, me) for term in mine]
            for _, mask, low, _ in corner:
                if mask == mask_y:
                    parts.append(jnp.concatenate([low, jnp.zeros_like(low)]))
            sent.append((self.added(parts, terms[0].dtype), mask_y))
        received = [self.swap(part, mask) for part, mask in sent]
        terms = [self.take(term, self.middle, 0, left, me) for term in mine] + received
        left = [bit for bit in left if bit not in self.middle]
        return (terms, left), [part for part, _ in sent]

    def scatter_far(self, state, me):
        return self.scatter_step(state, self.outer, me)

    def scatter_end(self, state):
        return self.added(state[0], F32)[0]

    def scatter(self, halves, order, me):
        state = self.scatter_core(halves)
        for group in order:
            state, _ = self.scatter_step(state, group, me)
        return self.scatter_end(state)

    def scatter_whole(self, whole, order, me):
        present = list(range(self.bits - 1, -1, -1))
        halves = [self.take(whole, self.core, mask, present, me) for mask in (0, 1)]
        return self.scatter(halves, order, me)


def after(values, others):
    leaves, tree = jax.tree.flatten(values)
    arrays = [leaf for leaf in leaves if not isinstance(leaf, int)]
    others = [leaf for leaf in jax.tree.leaves(others) if not isinstance(leaf, int)]
    tied = iter(lax.optimization_barrier(tuple(arrays + others)))
    return jax.tree.unflatten(
        tree, [leaf if isinstance(leaf, int) else next(tied) for leaf in leaves]
    )


class Weights:
    def __init__(self, net, me, wanted):
        self.arrays, self.plans, self.shapes = [], [], []
        seen = {}
        for pieces, place, rows in wanted:
            columns = pieces[0][1].shape[-1]
            plan = []
            if rows % 16:
                blocks = jnp.concatenate([array[:, place : place + rows] for _, array in pieces])
                order = jnp.asarray([s for own, _ in pieces for s in own], jnp.int32)
                spot = jnp.zeros((net.n,), jnp.int32).at[order ^ me].set(jnp.arange(net.n))
                whole = blocks[spot].reshape(net.n * rows // 16, 16, columns)
                plan.append((len(self.arrays), None, None))
                self.arrays.append(whole)
                self.shapes.append(whole.shape)
            else:
                for own, array in pieces:
                    if id(array) not in seen:
                        seen[id(array)] = len(self.arrays)
                        self.arrays.append(array)
                    for j, source in enumerate(own):
                        plan.append((seen[id(array)], (j, pl.ds(place, rows)), source))
                self.shapes.append((net.n, rows, columns))
            self.plans.append(plan)
        self.slots = max(len(plan) for plan in self.plans)

    def scratch(self):
        return [pltpu.VMEM(shape, BF16) for shape in self.shapes] + [
            pltpu.SemaphoreType.DMA((len(self.plans), self.slots))
        ]

    def copies(self, w, me, array_refs, held_ref, sems):
        found = []
        for slot, (array, index, source) in enumerate(self.plans[w]):
            if index is None:
                pair = (array_refs[array], held_ref)
            else:
                pair = (array_refs[array].at[index], held_ref.at[me ^ source])
            found.append(pltpu.make_async_copy(*pair, sems.at[w, slot]))
        return found

    def start(self, w, *refs):
        for copy in self.copies(w, *refs):
            copy.start()

    def wait(self, w, *refs):
        for copy in self.copies(w, *refs):
            copy.wait()


def flat(held):
    return held.reshape(-1, held.shape[-1])


SMEM_SPEC = pl.BlockSpec(memory_space=pltpu.SMEM)
ANY_SPEC = pl.BlockSpec(memory_space=pltpu.HBM)


def full_spec(shape):
    return pl.BlockSpec(shape, lambda *_: (0,) * len(shape))


def tile_spec(tile, columns):
    return pl.BlockSpec((tile, columns), lambda i: (i, 0))


def call(body, name, grid, ins, outs, scratch, us, bases=()):
    count = len(ins)

    def run(*refs):
        body(*refs[:count], *refs[count + len(bases) :])

    return pl.pallas_call(
        run,
        grid=grid,
        in_specs=[spec for _, spec in ins] + [ANY_SPEC] * len(bases),
        out_specs=[spec for _, _, spec in outs],
        out_shape=[jax.ShapeDtypeStruct(shape, dtype) for shape, dtype, _ in outs],
        scratch_shapes=scratch,
        input_output_aliases={count + i: i for i in range(len(bases))},
        compiler_params=pltpu.CompilerParams(
            vmem_limit_bytes=60 << 20,
            dimension_semantics=("arbitrary",) * len(grid),
        ),
        cost_estimate=pl.CostEstimate(
            flops=int(us * 2e10), bytes_accessed=int(us * 5e7), transcendentals=0
        ),
        name=name,
    )(*[array for array, _ in ins], *bases)


def sum_body(groups, me_ref, *refs):
    step = pl.program_id(0)
    outs = refs[len(refs) - len(groups) :]
    for out_ref, addends in zip(outs, groups):
        total = None
        for place, (low, high) in addends:
            part = refs[place][...].astype(F32)
            if low is not None:
                part = jnp.where((step >= low) & (step < high), part, 0.0)
            total = part if total is None else total + part
        out_ref[...] = total.astype(out_ref.dtype)


def sum_call(me, name, grid, ins, groups, outs, body=None):
    grid_spec = pltpu.PrefetchScalarGridSpec(
        num_scalar_prefetch=1,
        grid=(grid,),
        in_specs=[
            pl.BlockSpec(block, lambda i, me_ref, place=place: place(i, me_ref[0]))
            for _, block, place in ins
        ],
        out_specs=[
            pl.BlockSpec(block, lambda i, me_ref, place=place: place(i, me_ref[0]))
            for _, _, block, place in outs
        ],
    )
    return pl.pallas_call(
        body or functools.partial(sum_body, groups),
        grid_spec=grid_spec,
        out_shape=[jax.ShapeDtypeStruct(shape, dtype) for shape, dtype, _, _ in outs],
        compiler_params=pltpu.CompilerParams(
            vmem_limit_bytes=60 << 20, dimension_semantics=("arbitrary",)
        ),
        cost_estimate=pl.CostEstimate(flops=1000, bytes_accessed=1000, transcendentals=0),
        name=name,
    )(me.reshape(1), *[array for array, _, _ in ins])


class Reduction:
    def __init__(self, net, me, keep, send):
        self.net, self.me = net, me
        self.terms = [keep, net.swap(send, 1)]
        self.rows, self.columns = keep.shape[1:]
        self.plain = len(net.near) == 1 and len(net.middle) == 1 and self.rows % 8 == 0
        self.state = None

    def block(self):
        return (1, self.rows, self.columns)

    def hold(self, others):
        if self.plain:
            self.terms = after(self.terms, others)
        else:
            state = self.state or (self.terms, list(range(self.net.bits - 1, 0, -1)))
            self.state = held(state, others)
            if getattr(self, "corner_pieces", None) is not None:
                self.corner_pieces = after(self.corner_pieces, others)
        return self

    def corner(self):
        net = self.net
        if not self.plain:
            state = self.state or (self.terms, list(range(net.bits - 1, 0, -1)))
            self.state = state
            self.corner_pieces, sent = net.scatter_corner(state, self.me)
            return sent
        far = 1 << (len(net.outer) - 1)

        def place(shift):
            return lambda i, me: ((i + shift) * 4 + (me >> 1 & 3 ^ 3), 0, 0)

        ins = [(term, self.block(), place(shift)) for shift in (0, far) for term in self.terms]
        out = ((far, self.rows, self.columns), BF16, self.block(), lambda i, me: (i, 0, 0))
        always = (None, None)
        groups = [[(0, always), (1, always)], [(2, always), (3, always)]]
        low, high = sum_call(self.me, "corner_sum", far, ins, groups, [out, out])
        self.terms += [net.swap(low, 1 << net.near[0]), net.swap(high, 1 << net.middle[0])]
        return [low, high]

    def near(self):
        net = self.net
        if not self.plain:
            self.state, sent = net.scatter_near(self.state, self.corner_pieces, self.me)
            self.corner_pieces = None
            return sent
        far = 1 << (len(net.outer) - 1)
        keep, other, low, high = self.terms

        def place(flip):
            return lambda i, me: (i * 4 + (me >> 1 & 3 ^ flip), 0, 0)

        ins = [(term, self.block(), place(flip)) for flip in (1, 2) for term in (keep, other)]
        ins.append((high, self.block(), lambda i, me: (jnp.maximum(i - far, 0), 0, 0)))
        ins.append((low, self.block(), lambda i, me: (jnp.minimum(i, far - 1), 0, 0)))
        always = (None, None)
        groups = [
            [(0, always), (1, always), (4, (far, 2 * far))],
            [(2, always), (3, always), (5, (0, far))],
        ]
        out = ((2 * far, self.rows, self.columns), BF16, self.block(), lambda i, me: (i, 0, 0))
        sent = sum_call(self.me, "near_sum", 2 * far, ins, groups, [out, out])
        received = [
            net.swap(part, 1 << group[0]) for part, group in zip(sent, (net.near, net.middle))
        ]
        self.terms = [keep, other] + received
        return sent

    def sources(self, flip, step_block):
        keep, other, row, column = self.terms[:4]
        found = []
        for term in (keep, other):
            found.append((term, lambda me: ((me >> 3 ^ flip) * 4 + (me >> 1 & 3))))
        for term in (row, column):
            found.append((term, lambda me: (me >> 3 ^ flip)))
        return [
            (term, step_block[0], lambda i, me, at=at: step_block[1](i, at(me)))
            for term, at in found
        ]

    def far(self):
        net = self.net
        if not self.plain:
            self.state, sent = net.scatter_step(self.state, net.outer, self.me)
            return sent
        parts = 4
        lanes = self.columns // parts
        step_block = ((1, self.rows, lanes), lambda i, at: (at, 0, i))
        masks = net.masks(net.outer)
        ins, groups = [], []
        for mask in masks:
            groups.append([(len(ins) + j, (None, None)) for j in range(4)])
            ins += self.sources(mask >> 3, step_block)
        out = ((1, self.rows, self.columns), BF16, step_block[0], lambda i, me: (0, 0, i))
        sent = sum_call(self.me, "far_sum", parts, ins, groups, [out] * len(masks))
        self.terms += [net.swap(part, mask) for part, mask in zip(sent, masks)]
        return sent

    def end(self, lots, unit):
        if not self.plain:
            total = self.net.scatter_end(self.state)
            results, start = [], 0
            for count in lots:
                blocks = [
                    total[(start + j) * unit : (start + j + 1) * unit] for j in range(count)
                ]
                results.append(jnp.concatenate(blocks, axis=1))
                start += count
            return results
        step_block = ((1, unit, self.columns), lambda i, at: (at, i, 0))
        ins = self.sources(0, step_block)
        ins += [(term, step_block[0], lambda i, me: (0, i, 0)) for term in self.terms[4:]]
        outs, bounds, start = [], [], 0
        for count in lots:

            def place(i, me, start=start, count=count):
                return (0, jnp.clip(i - start, 0, count - 1))

            outs.append(((unit, count * self.columns), F32, (unit, self.columns), place))
            bounds.append((start, start + count))
            start += count

        def body(me_ref, *refs):
            step, addends = pl.program_id(0), refs[: len(ins)]
            total = addends[0][0].astype(F32)
            for ref in addends[1:]:
                total = total + ref[0].astype(F32)
            for out_ref, (low, high) in zip(refs[len(ins) :], bounds):

                @pl.when((step >= low) & (step < high))
                def _():
                    out_ref[...] = total

        return sum_call(self.me, "end_sum", start, ins, None, outs, body)


def pack_body(step, me_ref, lines_ref, inner_ref, *refs):
    shards, out_ref = refs[:-1], refs[-1]
    start = 0
    for ref in shards:
        out_ref[start : start + ref.shape[0]] = ref[...]
        start += ref.shape[0]
    me, width = me_ref[0], out_ref.shape[1]

    def spread(ref, offset):
        count = ref.shape[1]
        lanes = lax.broadcasted_iota(jnp.int32, (count, width), 1)
        spots = lax.broadcasted_iota(jnp.int32, (count, width), 0) + offset
        return matmul(ref[...], jnp.where(lanes == spots, 1.0, 0.0).astype(BF16))

    vectors = spread(lines_ref, me * step)
    place = me * inner_ref.shape[1]
    inner = spread(inner_ref, lax.rem(place, width))
    row = lax.broadcasted_iota(jnp.int32, inner.shape, 0)
    inner = jnp.where(row == place // width, inner, 0.0)
    out_ref[start:] = jnp.concatenate([vectors, inner]).astype(BF16)


def pack(me, shards, lines, inner):
    step, width = shards[0].shape
    return call(
        functools.partial(pack_body, step),
        "pack",
        (1,),
        [(me.reshape(1), SMEM_SPEC)]
        + [(array, full_spec(array.shape)) for array in (lines, inner, *shards)],
        [((len(shards) * step + 16, width), BF16, full_spec((len(shards) * step + 16, width)))],
        [],
        1,
    )[0]


def project_body(weights, tile, row_length, me_ref, *refs):
    count = len(weights.arrays)
    arrays, refs = refs[:count], refs[count:]
    feats_ref, x_ref = refs[:2]
    temb_ref, lines_ref, low_ref, q_ref, k_ref, v_ref = refs[2:8]
    tw, qw, kw, vw, lw, sems = refs[8:14]
    me, step = me_ref[0], pl.program_id(0)

    @pl.when(step == 0)
    def _():
        for w, held in enumerate((tw, qw, kw, vw, lw)):
            weights.start(w, me, arrays, held, sems)
        weights.wait(0, me, arrays, tw, sems)
        temb_ref[...] = matmul(feats_ref[...], flat(tw[...]))
        weights.wait(4, me, arrays, lw, sems)
        lines_ref[...] = jnp.sum(lw[...].astype(F32), axis=0)
        for w, held in ((1, qw), (2, kw), (3, vw)):
            weights.wait(w, me, arrays, held, sems)

    row = step * tile // row_length
    low = (x_ref[...].astype(F32) + temb_ref[pl.ds(row, 1), :]).astype(BF16)
    low_ref[...] = low
    q_ref[...] = (matmul(low, flat(qw[...])) + lines_ref[0:1]).astype(BF16)
    k_ref[...] = matmul(low, flat(kw[...])).astype(BF16)
    v_ref[...] = (matmul(low, flat(vw[...])) + lines_ref[1:2]).astype(BF16)


def project(net, me, flow, feats, x, row_length):
    tokens, width = x.shape
    tile = min(256, row_length)
    r = width // net.n
    weights = Weights(net, me, [(flow, w * r, r) for w in range(4)] + [(flow, 4 * r, 16)])
    ins = (
        [(me.reshape(1), SMEM_SPEC)]
        + [(array, ANY_SPEC) for array in weights.arrays]
        + [(feats, full_spec(feats.shape)), (x, tile_spec(tile, width))]
    )
    outs = [(feats.shape, F32, full_spec(feats.shape))]
    outs += [((16, width), F32, full_spec((16, width)))]
    outs += [((tokens, width), BF16, tile_spec(tile, width))] * 4
    return call(
        functools.partial(project_body, weights, tile, row_length),
        "project",
        (tokens // tile,),
        ins,
        outs,
        weights.scratch(),
        14,
    )


def same_document(segc_ref, segr_ref, bias_ref, block):
    @pl.when(block == 0)
    def _():
        bias_ref[...] = jnp.where(segc_ref[0] == segr_ref[0], 0.0, -1e30)


def own_lanes(shape, head, head_dim):
    lanes = lax.broadcasted_iota(jnp.int32, shape, len(shape) - 1)
    return (lanes // head_dim) == head


def attend_body(head_dim, segc_ref, segr_ref, q_ref, k_ref, v_ref, out_ref, log_ref, bias_ref):
    same_document(segc_ref, segr_ref, bias_ref, pl.program_id(1))
    queries, key_rows, values = q_ref[...], k_ref[...], v_ref[...]
    scale = 1.0 / math.sqrt(head_dim)
    per = queries.shape[1] // head_dim
    total = None
    for head in range(per):
        mine = own_lanes(queries.shape, head, head_dim)
        keys_own = jnp.where(mine, key_rows * BF16(scale), BF16(0))
        scores = matmul_right(keys_own, queries) + bias_ref[...]
        top = jnp.max(scores, axis=0, keepdims=True)
        raised = jnp.exp(scores - top)
        amount = jnp.sum(raised, axis=0, keepdims=True)
        log_ref[0, 0, pl.ds(head, 1), :] = top + jnp.log(amount)
        soft_low = (raised * (1.0 / amount)).astype(BF16)
        context = matmul_left(soft_low, values)
        total = context if total is None else jnp.where(mine, context, total)
    out_ref[...] = total.astype(BF16)


def attend_back_body(
    head_dim, segc_ref, segr_ref, q_ref, k_ref, v_ref, log_ref, g_ref, gq_ref, gk_ref, gv_ref, sums_ref, bias_ref
):
    same_document(segc_ref, segr_ref, bias_ref, pl.program_id(1))
    queries, key_rows, values, grads = q_ref[...], k_ref[...], v_ref[...], g_ref[...]
    scale = 1.0 / math.sqrt(head_dim)
    per = queries.shape[1] // head_dim
    totals = None
    for head in range(per):
        mine = own_lanes(queries.shape, head, head_dim)
        keys_own = jnp.where(mine, key_rows * BF16(scale), BF16(0))
        scores = matmul_right(keys_own, queries) + bias_ref[...]
        soft = jnp.exp(scores - log_ref[0, 0, pl.ds(head, 1), :])
        grad_soft = matmul_right(jnp.where(mine, values, BF16(0)), grads)
        inner_sum = jnp.sum(soft * grad_soft, axis=0, keepdims=True)
        grad_scores = (soft * (grad_soft - inner_sum)).astype(BF16)
        parts = (
            matmul_left(grad_scores, key_rows),
            matmul(grad_scores, queries),
            matmul(soft.astype(BF16), grads),
        )
        if totals is None:
            totals = parts
        else:
            totals = tuple(jnp.where(mine, part, total) for part, total in zip(parts, totals))
    gq = (totals[0] * scale).astype(BF16)
    gv = totals[2].astype(BF16)
    gq_ref[...] = gq
    gk_ref[...] = (totals[1] * scale).astype(BF16)
    gv_ref[...] = gv
    sums = [jnp.sum(part.astype(F32), axis=0, keepdims=True) for part in (gq, gv)]
    sums_ref[...] = jnp.concatenate(sums + [jnp.zeros_like(sums[0])] * 6)


def attention_args(segments, start, lanes, head_dim):
    row_length, per = segments.shape[1], lanes // head_dim
    segc = pl.BlockSpec((1, row_length, 1), lambda i, j: (start + i, 0, 0))
    segr = pl.BlockSpec((1, 1, row_length), lambda i, j: (start + i, 0, 0))
    block = pl.BlockSpec((row_length, lanes), lambda i, j: (start + i, j))
    log_spec = pl.BlockSpec((1, 1, per, row_length), lambda i, j: (start + i, j, 0, 0))
    return [(segments[:, :, None], segc), (segments[:, None, :], segr)], block, log_spec


def attend(queries, key_rows, values, segments, lanes=128):
    rows, row_length = segments.shape
    tokens, width = queries.shape
    head_dim = width // H
    blocks, per = width // lanes, lanes // head_dim
    masks, block, log_spec = attention_args(segments, 0, lanes, head_dim)
    return call(
        functools.partial(attend_body, head_dim),
        "attend",
        (rows, blocks),
        masks + [(array, block) for array in (queries, key_rows, values)],
        [
            ((tokens, width), BF16, block),
            ((rows, blocks, per, row_length), F32, log_spec),
        ],
        [pltpu.VMEM((row_length, row_length), F32)],
        24,
    )


def attend_back(queries, key_rows, values, segments, log_total, grad_context, row, bases=(), lanes=128):
    rows, row_length = segments.shape
    tokens, width = queries.shape
    head_dim = width // H
    masks, block, log_spec = attention_args(segments, row, lanes, head_dim)
    return call(
        functools.partial(attend_back_body, head_dim),
        "attend_back",
        (1, width // lanes),
        masks
        + [(array, block) for array in (queries, key_rows, values)]
        + [(log_total, log_spec), (grad_context, block)],
        [((tokens, width), BF16, block)] * 3
        + [((8, width), F32, pl.BlockSpec((8, lanes), lambda i, j: (0, j)))],
        [pltpu.VMEM((row_length, row_length), F32)],
        19,
        bases,
    )


def add_to(ref, value, step):
    part = jnp.sum(value, axis=0, keepdims=True)

    @pl.when(step == 0)
    def _():
        ref[...] = part

    @pl.when(step != 0)
    def _():
        ref[...] += part


def add_lines(ref, values, step):
    zero = jnp.zeros((1, ref.shape[1]), F32)
    sums = {line: jnp.sum(value, axis=0, keepdims=True) for line, value in values.items()}
    part = jnp.concatenate([sums.get(line, zero) for line in range(ref.shape[0])])

    @pl.when(step == 0)
    def _():
        ref[...] = part

    @pl.when(step != 0)
    def _():
        ref[...] += part


def ffn_in_body(weights, row, chunk, me_ref, *refs):
    count = len(weights.arrays)
    arrays, refs = refs[:count], refs[count:]
    context_ref, x_ref, temb_ref, lines_ref = refs[:4]
    first_low_ref, normed_ref, spread_ref, active_ref, slope_ref = refs[4:9]
    ow, iws, sems = refs[9], refs[10:14], refs[14]
    me, step = me_ref[0], pl.program_id(0)

    @pl.when(step == 0)
    def _():
        for w, held in enumerate((ow,) + iws):
            weights.start(w, me, arrays, held, sems)
        weights.wait(0, me, arrays, ow, sems)

    stream = x_ref[...].astype(F32) + temb_ref[row : row + 1, :]
    mixed = stream + (matmul(context_ref[...], flat(ow[...])) + lines_ref[2:3])
    normed, spread = normalize(mixed)
    normed_ref[...] = normed
    spread_ref[...] = spread
    first = normed * lines_ref[4:5] + lines_ref[5:6]
    first_low_ref[...] = first.astype(BF16)
    width = ow.shape[2]
    for k, iw in enumerate(iws):

        @pl.when(step == 0)
        def _():
            weights.wait(k + 1, me, arrays, iw, sems)

        @pl.loop(0, width // chunk)
        def _(j):
            inner = pl.ds(pl.multiple_of(j * chunk, chunk), chunk)
            columns = pl.ds(pl.multiple_of(k * width + j * chunk, chunk), chunk)
            pre = matmul(first_low_ref[...], flat(iw[:, :, inner])) + lines_ref[8 + k : 9 + k, inner]
            normal_cdf = 0.5 * (1.0 + lax.erf(pre * INV_ROOT_TWO))
            normal_pdf = jnp.exp(-0.5 * pre * pre) * INV_ROOT_TAU
            active_ref[:, columns] = (pre * normal_cdf).astype(BF16)
            slope_ref[:, columns] = (normal_cdf + pre * normal_pdf).astype(BF16)


def ffn_in(net, me, flow, context, x, temb, lines, hidden, row, row_length, bases=(), tile=256, chunk=512):
    tokens, width = x.shape
    r = width // net.n
    weights = Weights(net, me, [(flow, w * r, r) for w in range(1 + hidden // width)])
    tile = min(tile, row_length)
    start = row * (row_length // tile)
    tiled, wide, thin = (
        pl.BlockSpec((tile, columns), lambda i: (start + i, 0)) for columns in (width, hidden, 1)
    )
    ins = (
        [(me.reshape(1), SMEM_SPEC)]
        + [(array, ANY_SPEC) for array in weights.arrays]
        + [(context, tiled), (x, tiled)]
        + [(array, full_spec(array.shape)) for array in (temb, lines)]
    )
    outs = [
        ((tokens, width), BF16, tiled),
        ((tokens, width), F32, tiled),
        ((tokens, 1), F32, thin),
        ((tokens, hidden), BF16, wide),
        ((tokens, hidden), BF16, wide),
    ]
    return call(
        functools.partial(ffn_in_body, weights, row, chunk),
        "ffn_in",
        (row_length // tile,),
        ins,
        outs,
        weights.scratch(),
        16,
        bases,
    )


def ffn_out_body(weights, me_ref, *refs):
    count = len(weights.arrays)
    arrays, refs = refs[:count], refs[count:]
    active_ref, normed_ref, cot_ref, lines_ref = refs[:4]
    out_ref, gs_ref, gs_low_ref, sums_ref = refs[4:8]
    uw, sems = refs[8:10]
    me, step = me_ref[0], pl.program_id(0)

    @pl.when(step == 0)
    def _():
        weights.start(0, me, arrays, uw, sems)
        weights.wait(0, me, arrays, uw, sems)

    first = normed_ref[...] * lines_ref[4:5] + lines_ref[5:6]
    second = first + (matmul(active_ref[...], flat(uw[...])) + lines_ref[3:4])
    normed_second, spread_second = normalize(second)
    out_ref[...] = (normed_second * lines_ref[6:7] + lines_ref[7:8]).astype(BF16)
    grad_out = cot_ref[...].astype(F32)
    grad_second = norm_back(grad_out * lines_ref[6:7], normed_second, spread_second)
    gs_ref[...] = grad_second
    low = grad_second.astype(BF16)
    gs_low_ref[...] = low
    add_lines(sums_ref, {3: low.astype(F32), 6: grad_out * normed_second, 7: grad_out}, step)


def ffn_out(net, me, flow, active, normed, cotangent, vectors, tile=256):
    tokens, width = normed.shape
    hidden = active.shape[1]
    weights = Weights(net, me, [(flow, 0, hidden // net.n)])
    tiled, wide = tile_spec(tile, width), tile_spec(tile, hidden)
    ins = (
        [(me.reshape(1), SMEM_SPEC)]
        + [(array, ANY_SPEC) for array in weights.arrays]
        + [(active, wide), (normed, tiled), (cotangent, tiled)]
        + [(vector, full_spec(vector.shape)) for vector in vectors]
    )
    outs = [
        ((tokens, width), BF16, tiled),
        ((tokens, width), F32, tiled),
        ((tokens, width), BF16, tiled),
        ((8, width), F32, full_spec((8, width))),
    ]
    return call(
        functools.partial(ffn_out_body, weights),
        "ffn_out",
        (tokens // tile,),
        ins,
        outs,
        weights.scratch(),
        20,
    )


def ffn_back_body(weights, chunk, me_ref, *refs):
    count = len(weights.arrays)
    arrays, refs = refs[:count], refs[count:]
    (gs_ref, gs_low_ref, slope_ref, normed_ref, spread_ref, lines_ref) = refs[:6]
    (gi_ref, gm_ref, gm_low_ref, gc_ref, ibg_ref, sums_ref) = refs[6:12]
    uw, ow, iws, sems, acc_ref = refs[12], refs[13], refs[14:18], refs[18], refs[19]
    me, step = me_ref[0], pl.program_id(0)
    helds = (uw, ow) + iws

    @pl.when(step == 0)
    def _():
        for w in (0, 2, 3, 4, 5, 1):
            weights.start(w, me, arrays, helds[w], sems)
        weights.wait(0, me, arrays, uw, sems)

    acc_ref[...] = gs_ref[...]
    unit = uw.shape[1]
    width = ow.shape[2]
    for k, iw in enumerate(iws):

        @pl.when(step == 0)
        def _():
            weights.wait(k + 2, me, arrays, iw, sems)

        @pl.loop(0, width // chunk)
        def _(j):
            inner = pl.ds(pl.multiple_of(j * chunk, chunk), chunk)
            columns = pl.ds(pl.multiple_of(k * width + j * chunk, chunk), chunk)
            span = chunk // unit
            held = flat(uw[pl.ds(k * (width // unit) + j * span, span)])
            grad_active = matmul_right(gs_low_ref[...], held)
            low = (grad_active * slope_ref[:, columns].astype(F32)).astype(BF16)
            gi_ref[:, columns] = low
            acc_ref[...] += matmul_right(low, flat(iw[:, :, inner]))

    add_to(ibg_ref, gi_ref[...].astype(F32), step)
    grad_first, normed = acc_ref[...], normed_ref[...]
    grad_mixed = norm_back(grad_first * lines_ref[4:5], normed, spread_ref[...])
    gm_ref[...] = grad_mixed
    low = grad_mixed.astype(BF16)
    gm_low_ref[...] = low
    add_lines(sums_ref, {2: low.astype(F32), 4: grad_first * normed, 5: grad_first}, step)

    @pl.when(step == 0)
    def _():
        weights.wait(1, me, arrays, ow, sems)

    gc_ref[...] = matmul_right(low, flat(ow[...])).astype(BF16)


def ffn_back(net, me, flow_u, flow_io, gs, gs_low, slope, normed, spread, lines, tile=256, chunk=512):
    tokens, width = gs.shape
    hidden = slope.shape[1]
    r = width // net.n
    weights = Weights(
        net,
        me,
        [(flow_u, 0, hidden // net.n)]
        + [(flow_io, w * r, r) for w in range(1 + hidden // width)],
    )
    tile = min(tile, tokens)
    tiled, wide = tile_spec(tile, width), tile_spec(tile, hidden)
    ins = (
        [(me.reshape(1), SMEM_SPEC)]
        + [(array, ANY_SPEC) for array in weights.arrays]
        + [(gs, tiled), (gs_low, tiled), (slope, wide), (normed, tiled)]
        + [(spread, tile_spec(tile, 1)), (lines, full_spec(lines.shape))]
    )
    outs = [
        ((tokens, hidden), BF16, wide),
        ((tokens, width), F32, tiled),
        ((tokens, width), BF16, tiled),
        ((tokens, width), BF16, tiled),
        ((1, hidden), F32, full_spec((1, hidden))),
        ((8, width), F32, full_spec((8, width))),
    ]
    return call(
        functools.partial(ffn_back_body, weights, chunk),
        "ffn_back",
        (tokens // tile,),
        ins,
        outs,
        weights.scratch() + [pltpu.VMEM((tile, width), F32)],
        45,
    )


def deal(me_ref, total, rows, keep_ref, send_ref, kind=0):
    core = me_ref[0] & 1
    total = total.reshape(-1, 2, rows, total.shape[-1])
    low, high = total[:, 0], total[:, 1]
    place = slice(kind * rows, (kind + 1) * rows)
    keep_ref[:, place] = jnp.where(core == 0, low, high).astype(BF16)
    send_ref[:, place] = jnp.where(core == 0, high, low).astype(BF16)


def product_body(rows, me_ref, a_ref, b_ref, keep_ref, send_ref):
    deal(me_ref, matmul_left(a_ref[...], b_ref[...]), rows, keep_ref, send_ref)


def product(net, me, left, right, tile=512):
    tokens, width = left.shape
    columns = right.shape[1]
    rows = width // net.n
    shape = (net.n // 2, rows, columns)
    block = pl.BlockSpec((tile // (2 * rows), rows, columns), lambda i: (i, 0, 0))
    return call(
        functools.partial(product_body, rows),
        "product",
        (width // tile,),
        [
            (me.reshape(1), SMEM_SPEC),
            (left, pl.BlockSpec((tokens, tile), lambda i: (0, i))),
            (right, full_spec((tokens, columns))),
        ],
        [(shape, BF16, block), (shape, BF16, block)],
        [],
        15,
    )


def inner_body(rows, me_ref, context_ref, first_ref, gm_ref, gi_ref, keep_ref, send_ref):
    total = matmul_left(first_ref[...], gi_ref[...])
    width = gm_ref.shape[1]
    deal(me_ref, matmul_left(context_ref[...], gm_ref[...]), rows, keep_ref, send_ref, 0)
    for k in range(total.shape[1] // width):
        part = total[:, k * width : (k + 1) * width]
        deal(me_ref, part, rows, keep_ref, send_ref, k + 1)


def inner_product(net, me, context, first_low, gm_low, gi, tile=256):
    tokens, width = context.shape
    hidden = gi.shape[1]
    rows = width // net.n
    kinds = 1 + hidden // width
    shape = (net.n // 2, kinds * rows, width)
    block = pl.BlockSpec((tile // (2 * rows), kinds * rows, width), lambda i: (i, 0, 0))
    left = pl.BlockSpec((tokens, tile), lambda i: (0, i))
    return call(
        functools.partial(inner_body, rows),
        "inner_product",
        (width // tile,),
        [
            (me.reshape(1), SMEM_SPEC),
            (context, left),
            (first_low, left),
            (gm_low, full_spec((tokens, width))),
            (gi, full_spec((tokens, hidden))),
        ],
        [(shape, BF16, block), (shape, BF16, block)],
        [],
        18,
    )


def triple_body(rows, me_ref, lines_ref, a_ref, q_ref, k_ref, v_ref, keep_ref, send_ref):
    for w, ref in enumerate((q_ref, k_ref, v_ref)):
        deal(me_ref, matmul_left(a_ref[...], ref[...]), rows, keep_ref, send_ref, w)
    core = me_ref[0] & 1
    low, high = lines_ref[:, 0:8], lines_ref[:, 8:16]
    place = slice(3 * rows, 3 * rows + 8)
    keep_ref[:, place] = jnp.where(core == 0, low, high).astype(BF16)
    send_ref[:, place] = jnp.where(core == 0, high, low).astype(BF16)


def triple_product(net, me, lines, left, gq, gk, gv, tile=256):
    tokens, width = left.shape
    rows = width // net.n
    shape = (net.n // 2, 3 * rows + 8, width)
    chips = tile // (2 * rows)
    block = pl.BlockSpec((chips, 3 * rows + 8, width), lambda i: (i, 0, 0))
    full = full_spec((tokens, width))
    return call(
        functools.partial(triple_body, rows),
        "triple_product",
        (width // tile,),
        [
            (me.reshape(1), SMEM_SPEC),
            (lines, pl.BlockSpec((chips, 16, width), lambda i: (i, 0, 0))),
            (left, pl.BlockSpec((tokens, tile), lambda i: (0, i))),
            (gq, full),
            (gk, full),
            (gv, full),
        ],
        [(shape, BF16, block), (shape, BF16, block)],
        [],
        13,
    )


def stream_back_body(weights, me_ref, *refs):
    count = len(weights.arrays)
    arrays, refs = refs[:count], refs[count:]
    gm_ref, gq_ref, gk_ref, gv_ref = refs[:4]
    out_ref, gt_ref = refs[4:6]
    qw, kw, vw, sems = refs[6:10]
    me, step = me_ref[0], pl.program_id(0)

    @pl.when(step == 0)
    def _():
        for w, held in enumerate((qw, kw, vw)):
            weights.start(w, me, arrays, held, sems)
        for w, held in enumerate((qw, kw, vw)):
            weights.wait(w, me, arrays, held, sems)

    total = (
        gm_ref[...]
        + matmul_right(gq_ref[...], flat(qw[...]))
        + matmul_right(gk_ref[...], flat(kw[...]))
        + matmul_right(gv_ref[...], flat(vw[...]))
    )
    out_ref[...] = total
    add_to(gt_ref, total, step)


def stream_back(net, me, flow, gm, gq, gk, gv, row, row_length, base=None, tile=256):
    tokens, width = gm.shape
    tile = min(tile, row_length)
    r = width // net.n
    weights = Weights(net, me, [(flow, w * r, r) for w in (1, 2, 3)])
    start = row * (row_length // tile)
    tiled = pl.BlockSpec((tile, width), lambda i: (start + i, 0))
    ins = (
        [(me.reshape(1), SMEM_SPEC)]
        + [(array, ANY_SPEC) for array in weights.arrays]
        + [(array, tiled) for array in (gm, gq, gk, gv)]
    )
    return call(
        functools.partial(stream_back_body, weights),
        "stream_back",
        (row_length // tile,),
        ins,
        [((tokens, width), F32, tiled), ((1, width), F32, full_spec((1, width)))],
        weights.scratch(),
        10,
        () if base is None else (base,),
    )


def in_order(net, me, sources, blocks):
    order = jnp.asarray(sources, jnp.int32)
    spot = jnp.zeros((net.n,), jnp.int32).at[order].set(jnp.arange(net.n, dtype=jnp.int32))
    return blocks[spot[jnp.arange(net.n) ^ me]]


def held(state, others):
    return after(state[0], others), state[1]


def stream_ends(state, unit):
    if not state.plain:
        total = state.net.scatter_end(state.state)
        return [total[w * unit : (w + 1) * unit] for w in range(3)] + [total[3 * unit]]
    rows, columns = state.rows, state.columns
    step_block = ((1, rows, columns), lambda i, at: (at, 0, 0))
    ins = state.sources(0, step_block)
    ins += [(term, step_block[0], lambda i, me: (0, 0, 0)) for term in state.terms[4:]]
    shapes = [(unit, columns)] * 3 + [(8, columns)]
    outs = [(shape, F32, shape, lambda i, me: (0, 0)) for shape in shapes]

    def body(me_ref, *refs):
        total = refs[0][0].astype(F32)
        for ref in refs[1 : len(ins)]:
            total = total + ref[0].astype(F32)
        start = 0
        for out_ref in refs[len(ins) :]:
            count = out_ref.shape[0]
            out_ref[...] = total[start : start + count]
            start += count

    results = sum_call(state.me, "stream_end", 1, ins, None, outs, body)
    return list(results[:3]) + [results[3][0]]


def on_device(
    net,
    inputs,
    timesteps,
    segments,
    cotangent,
    query_weight,
    key_weight,
    value_weight,
    output_weight,
    inner_weight,
    outer_weight,
    time_weight,
    *vectors,
):
    n = net.n
    me = lax.axis_index("fsdp").astype(jnp.int32)
    batch_count, row_count, row_length, model_width = inputs.shape
    rows = batch_count * row_count
    tokens = rows * row_length
    feats = features(timesteps.reshape(rows)).astype(BF16)
    order = (0, 1, 2, 4, 5, 6, 7, 8, 3)
    sizes = [vectors[i].shape[0] for i in order]
    small = sum(
        jnp.pad(vectors[i].astype(F32)[None], ((line, 7 - line), (0, 0)))
        for line, i in enumerate(order[:8])
    )
    inner_line = jnp.broadcast_to(vectors[3][None], (8, sizes[-1]))
    r = model_width // n

    shards = (time_weight, query_weight, key_weight, value_weight)
    far = net.gather_far(pack(me, shards, small.astype(BF16), inner_line))
    hidden = inner_weight.shape[1]
    inner_blocks = [
        inner_weight[:, start : start + model_width] for start in range(0, hidden, model_width)
    ]
    shard_io = after(jnp.concatenate([output_weight] + inner_blocks), far)
    far_io = net.gather_far(shard_io)
    far = net.stacked(far)
    near = net.gather_near(far)
    near, far_io = after((near, far_io), ())
    pieces, corners, _ = net.gather_corner(far, near)
    flow = net.gather_core(pieces)
    far_io, corners = after((net.stacked(far_io), corners), ())
    near_io = net.gather_near(far_io)
    flow += net.gather_core(corners)

    segments = segments.reshape(rows, row_length)
    x = inputs.reshape(tokens, model_width)
    feats_in = after(feats, far_io)
    temb, lines, stream_low, queries, key_rows, values = project(
        net, me, flow, feats_in, x, row_length
    )
    near_io, queries, shard_u = after((near_io, queries, outer_weight), ())
    pieces, corners, sent = net.gather_corner(far_io, near_io)
    flow_io = net.gather_core(pieces[:1])
    far_u = net.gather_far(shard_u)
    queries = after(queries, sent)
    context, log_total = attend(queries, key_rows, values, segments)
    far_u, corners, context = after((far_u, corners, context), ())
    flow_io += net.gather_core(corners) + net.gather_core(pieces[1:])
    far_u = net.stacked(far_u)
    near_u = net.gather_near(far_u)
    context = after(context, far_u)
    fed, sent = (), ()
    for row in range(rows):
        if row == 1:
            near_u, fed = after((near_u, fed), ())
            pieces, corners, sent = net.gather_corner(far_u, near_u)
            fed = after(fed, sent)
        fed = ffn_in(
            net, me, flow_io, context, x, temb, lines, hidden, row, row_length, fed
        )
    first_low, normed_first, spread_first, active_low, slope = fed
    corners, active_low = after((corners, active_low), ())
    flow_u = net.gather_core(pieces) + net.gather_core(corners)
    (
        layer_output,
        grad_second,
        grad_second_low,
        sums_out,
    ) = ffn_out(
        net,
        me,
        flow_u,
        active_low,
        normed_first,
        cotangent.reshape(tokens, model_width),
        (lines,),
    )
    outer_halves = product(net, me, active_low, grad_second_low)
    outer_sum = Reduction(net, me, *outer_halves)
    slope = after(slope, outer_halves)
    (
        grad_inner_low,
        grad_mixed,
        grad_mixed_low,
        grad_context,
        inner_bias_grad,
        sums_back,
    ) = ffn_back(
        net,
        me,
        flow_u,
        flow_io,
        grad_second,
        grad_second_low,
        slope,
        normed_first,
        spread_first,
        lines,
    )
    sent = outer_sum.hold(grad_mixed_low).corner()
    grad_mixed_low = after(grad_mixed_low, sent)
    inner_halves = inner_product(net, me, context, first_low, grad_mixed_low, grad_inner_low)
    inner_sum = Reduction(net, me, *inner_halves)
    sent = outer_sum.hold(inner_halves).near()
    grad_context = after(grad_context, (inner_halves, sent))
    back = (queries, key_rows, values, segments, log_total, grad_context)
    found, sums_rows = None, 0.0
    for row in range(rows):
        if row == 1:
            sent = inner_sum.hold(found[1]).corner() + list(outer_sum.hold(found[1]).far())
            found = after(found, sent)
        found = attend_back(*back, row, found or ())
        sums_rows += found[3]
        found = found[:3]
    grad_queries, grad_keys, grad_values = found
    sent = inner_sum.hold(grad_queries).near()
    (outer_weight_grad,) = outer_sum.hold(grad_queries).end([1], outer_weight.shape[0])
    sums = sums_rows + sums_out + sums_back
    sums = sums.reshape(8, n, r).transpose(1, 0, 2).reshape(n, 8 * r)
    sums = jnp.concatenate([sums, inner_bias_grad.reshape(n, -1)], axis=1)
    sums = jnp.pad(sums, ((0, 0), (0, model_width - sums.shape[1]))).astype(BF16)
    sums = jnp.broadcast_to(sums[:, None], (n, 8, model_width)).reshape(n // 2, 16, model_width)
    stream_low, sums = after((stream_low, sums), (sent, outer_weight_grad))
    stream_halves = triple_product(
        net, me, sums, stream_low, grad_queries, grad_keys, grad_values
    )
    stream_sum = Reduction(net, me, *stream_halves)
    grad_mixed = after(grad_mixed, stream_halves)
    back = (flow, grad_mixed, grad_queries, grad_keys, grad_values)
    grad_stream, part = stream_back(net, me, *back, 0, row_length)
    grad_temb = [part]
    for row in range(1, rows):
        if row == 1:
            sent = stream_sum.hold(part).corner() + list(inner_sum.hold(part).far())
            grad_stream = after(grad_stream, sent)
        grad_stream, part = stream_back(net, me, *back, row, row_length, grad_stream)
        grad_temb.append(part)
    sent = stream_sum.hold(part).near()
    ends = jnp.concatenate([feats.astype(F32), jnp.concatenate(grad_temb)], axis=1)[None]
    output_weight_grad, inner_weight_grad = inner_sum.hold(sent).end([1, hidden // model_width], r)
    ends = after(ends, output_weight_grad)
    sources, ends = net.gather_round([0], ends, net.masks(net.core))
    sources, ends = net.gather_round(sources, ends, net.inner_masks())
    stream_sum.far()
    sources, ends = net.gather_round(sources, ends, net.masks(net.outer))
    ends = in_order(net, me, sources, ends).reshape(n * rows, 2 * model_width)
    query_weight_grad, key_weight_grad, value_weight_grad, vector_sums = stream_ends(
        stream_sum, r
    )
    feats_all, temb_all = ends[:, :model_width], ends[:, model_width:]
    own = model_width // n
    feats_own = lax.dynamic_slice_in_dim(feats_all, me * own, own, 1)
    time_weight_grad = lax.dot_general(
        feats_own,
        temb_all,
        (((0,), (0,)), ((), ())),
        precision=lax.Precision.HIGHEST,
    )
    parts, start = {}, 0
    for i, size in zip(order, sizes):
        parts[i] = vector_sums[start : start + size]
        start += size
    vector_outs = [parts[i] for i in range(len(order))]

    shape = inputs.shape
    return (
        layer_output.reshape(shape),
        grad_stream.reshape(shape),
        query_weight_grad,
        key_weight_grad,
        value_weight_grad,
        output_weight_grad,
        inner_weight_grad,
        outer_weight_grad,
        time_weight_grad,
    ) + tuple(vector_outs)


def solution(mesh):
    matrix, vector = P("fsdp", None), P("fsdp")
    batch = P(None, "fsdp", None, None)
    return jax.shard_map(
        functools.partial(on_device, Net(mesh.shape["fsdp"])),
        mesh=mesh,
        in_specs=(batch, P(None, "fsdp"), P(None, "fsdp", None), batch)
        + (matrix,) * 7
        + (vector,) * 9,
        out_specs=(batch, batch) + (matrix,) * 7 + (vector,) * 9,
        check_vma=False,
    )
```

time: 784 us -> 545 us (0.70)
  the two profiles are of different devices: /device:TPU:0 before, /device:TPU:20 now
where the time goes in v2:
time: 545 us; the launch traced here: 534 us
  Pallas kernels  291 us (53%)
  waiting for transfers between devices  153 us (28%)
  starting transfers between devices  56.5 us (10%)
  local copies, waits for them, and re-layouts  22.4 us (4%)
  other arithmetic  9.3 us (2%)
    pallas_call x14, Pallas kernels, call(): pl.pallas_call(run, grid=grid, in_specs=[spec for _, spec in ins] + [ANY_...  248 us
    ppermute x67, waiting for transfers between devices, swap(): return lax.ppermute(array, 'fsdp', [(i, i ^ mask) for i in range(self.n)])  153 us
    ppermute x67, starting transfers between devices, swap(): return lax.ppermute(array, 'fsdp', [(i, i ^ mask) for i in range(self.n)])  56.5 us
    pallas_call x12, Pallas kernels, sum_call(): pl.pallas_call(body or functools.partial(sum_body, groups), grid_spec=gri...  42.4 us
  transfers between devices with their start and end apart: 67, of which 30 were waited for; matrix products, arithmetic and copies ran while one was open for 4% of the time, Pallas kernels for 44%

profile of v2, /device:TPU:20, one launch (start us, length us, event | category | flops | bytes accessed | tf_op | source)
XLA Modules:
  0.0 534.5 jit_solution(16142438168367530710)
XLA Ops:
  8.7 11.6 %collective-permute-done = bf16[144,1024]{1,0:T(8,128)(2,1)S(1)} collective-permute-done((bf16[144,1024]{1,0:T(8,128)(2,1)}, bf16[144,1024]{1,0:T(8,128)(2,1)S(1)}, u32[]{:S(2)}, u32[]{:S(2)}) %collective-permute-start) | collective-permute-done | bytes 294944 | tf_op jit(solution)/shard_map/ppermute | solution.py:80
  21.5 12.5 %collective-permute-done.2 = bf16[144,1024]{1,0:T(8,128)(2,1)S(1)} collective-permute-done((bf16[144,1024]{1,0:T(8,128)(2,1)}, bf16[144,1024]{1,0:T(8,128)(2,1)S(1)}, u32[]{:S(2)}, u32[]{:S(2)}) %collective-permute-start.2) | collective-permute-done | bytes 294944 | tf_op jit(solution)/shard_map/ppermute | solution.py:80
  40.8 12.0 %collective-permute-done.5 = bf16[160,1024]{1,0:T(8,128)(2,1)S(1)} collective-permute-done((bf16[160,1024]{1,0:T(8,128)(2,1)S(1)}, bf16[160,1024]{1,0:T(8,128)(2,1)S(1)}, u32[]{:S(2)}, u32[]{:S(2)}) %collective-permute-start.5) | collective-permute-done | bytes 327712 | tf_op jit(solution)/shard_map/ppermute | solution.py:80
  54.0 11.3 %collective-permute-done.7 = bf16[160,1024]{1,0:T(8,128)(2,1)S(1)} collective-permute-done((bf16[160,1024]{1,0:T(8,128)(2,1)S(1)}, bf16[160,1024]{1,0:T(8,128)(2,1)S(1)}, u32[]{:S(2)}, u32[]{:S(2)}) %collective-permute-start.7) | collective-permute-done | bytes 327712 | tf_op jit(solution)/shard_map/ppermute | solution.py:80
  69.4 11.0 %collective-permute-done.8.refs_7_ = bf16[2,144,1024]{2,1,0:T(8,128)(2,1)S(1)} collective-permute-done((bf16[2,144,1024]{2,1,0:T(8,128)(2,1)S(1)}, bf16[2,144,1024]{2,1,0:T(8,128)(2,1)S(1)}, u32[]{:S(2)}, u32[]{:S(2)}) %collective-permute-start.8) | collective-permute-done | bytes 589856 | tf_op jit(solution)/shard_map/ppermute | solution.py:80
  87.2 14.6 %project.1 = (f32[2,1024]{1,0:T(2,128)}, f32[16,1024]{1,0:T(8,128)}, bf16[1024,1024]{1,0:T(8,128)(2,1)}, bf16[1024,1024]{1,0:T(8,128)(2,1)}, bf16[1024,1024]{1,0:T(8,128)(2,1)}, /*index=5*/bf16[1024,1024]{1,0:T(8,128)(2,1)}) custom-call(s32[1]{0:T(128)} %bitcast.refs_0_.me_ref, bf16[4,144,1024]{2,1,0:T(8,128)(2,1)} %copy-done.3, ...), custom_call_target="tpu_custom_call" | custom-call | flops 280000004096 | bytes 700000000 | tf_op jit(solution)/shard_map/project/pallas_call | solution.py:288
  101.8 11.3 %collective-permute-done.10.refs_7_.refs_17_ = bf16[4,160,1024]{2,1,0:T(8,128)(2,1)} collective-permute-done((bf16[4,160,1024]{2,1,0:T(8,128)(2,1)}, bf16[4,160,1024]{2,1,0:T(8,128)(2,1)}, u32[]{:S(2)}, u32[]{:S(2)}) %collective-permute-start.10) | collective-permute-done | bytes 1310752 | tf_op jit(solution)/shard_map/ppermute | solution.py:80
  133.5 5.5 %collective-permute-done.19 = bf16[128,1024]{1,0:T(8,128)(2,1)S(1)} collective-permute-done((bf16[128,1024]{1,0:T(8,128)(2,1)S(1)}, bf16[128,1024]{1,0:T(8,128)(2,1)S(1)}, u32[]{:S(2)}, u32[]{:S(2)}) %collective-permute-start.19) | collective-permute-done | bytes 262176 | tf_op jit(solution)/shard_map/ppermute | solution.py:80
  138.9 23.6 %attend.1 = (bf16[1024,1024]{1,0:T(8,128)(2,1)}, f32[2,8,2,512]{3,2,1,0:T(2,128)}) custom-call(s32[2,512,1]{2,1,0:T(8,128)} %broadcast_in_dim_reshape.6.refs_0_, s32[2,1,512]{2,1,0:T(1,128)} %refs_1_.5, bf16[1024,1024]{1,0:T(8,128)(2,1)} %get-tuple-element.197.refs_2_, bf16[1024,1024]{1,0:T(8,128)(2,1)} %get-tuple-element.198.refs_3_, ...), custom_call_target="tpu_custom_call" | custom-call | flops 480000016384 | bytes 1200000000 | tf_op jit(solution)/shard_map/attend/pallas_call | solution.py:288
  168.4 19.1 %ffn_in.2 = (bf16[1024,1024]{1,0:T(8,128)(2,1)}, f32[1024,1024]{1,0:T(8,128)}, f32[1024,1]{1,0:T(8,128)}, bf16[1024,4096]{1,0:T(8,128)(2,1)}, bf16[1024,4096]{1,0:T(8,128)(2,1)}) custom-call(s32[1]{0:T(128)} %bitcast.refs_0_.me_ref, bf16[4,160,1024]{2,1,0:T(8,128)(2,1)} %pad_maximum_fusion.refs_1_.refs_11_, ...), custom_call_target="tpu_custom_call" | custom-call | flops 320000000000 | bytes 800000000 | tf_op jit(solution)/shard_map/ffn_in/pallas_call | solution.py:288
  198.7 19.3 %ffn_in.3 = (bf16[1024,1024]{1,0:T(8,128)(2,1)}, f32[1024,1024]{1,0:T(8,128)}, f32[1024,1]{1,0:T(8,128)}, bf16[1024,4096]{1,0:T(8,128)(2,1)}, bf16[1024,4096]{1,0:T(8,128)(2,1)}) custom-call(s32[1]{0:T(128)} %bitcast.refs_0_.me_ref, ...), custom_call_target="tpu_custom_call", output_to_operand_aliasing={{0}: (15, {}), {1}: (16, {}), {2}: (17, {}), {3}: (18, {}),... | custom-call | flops 320000000000 | bytes 800000000 | tf_op jit(solution)/shard_map/ffn_in/pallas_call | solution.py:288
  221.8 20.9 %ffn_out.1 = (bf16[1024,1024]{1,0:T(8,128)(2,1)}, f32[1024,1024]{1,0:T(8,128)}, bf16[1024,1024]{1,0:T(8,128)(2,1)}, f32[8,1024]{1,0:T(8,128)}) custom-call(s32[1]{0:T(128)} %bitcast.refs_0_.me_ref, bf16[4,128,1024]{2,1,0:T(8,128)(2,1)} %pad_maximum_fusion.2.refs_1_, bf16[4,128,1024]{2,1,0:T(8,128)(2,1)} %collective-permute-done.22.refs_2_, ...), custom_call_target="tpu_custom_call" | custom-call | flops 399999991808 | bytes 1000000000 | tf_op jit(solution)/shard_map/ffn_out/pallas_call | solution.py:288
  242.7 14.4 %product.1 = (bf16[16,128,1024]{2,1,0:T(8,128)(2,1)}, bf16[16,128,1024]{2,1,0:T(8,128)(2,1)}) custom-call(s32[1]{0:T(128)} %bitcast.refs_0_.me_ref, bf16[1024,4096]{1,0:T(8,128)(2,1)} %get-tuple-element.231.refs_11_.refs_1_, bf16[1024,1024]{1,0:T(8,128)(2,1)} %get-tuple-element.235.refs_2_.refs_22_), custom_call_target="tpu_custom_call" | custom-call | flops 299999985664 | bytes 750000000 | tf_op jit(solution)/shard_map/product/pallas_call | solution.py:288
  257.2 45.3 %ffn_back.1 = (bf16[1024,4096]{1,0:T(8,128)(2,1)}, f32[1024,1024]{1,0:T(8,128)}, bf16[1024,1024]{1,0:T(8,128)(2,1)}, bf16[1024,1024]{1,0:T(8,128)(2,1)}, f32[1,4096]{1,0:T(1,128)}, /*index=5*/f32[8,1024]{1,0:T(8,128)}) custom-call(s32[1]{0:T(128)} %bitcast.refs_0_.me_ref, bf16[4,128,1024]{2,1,0:T(8,128)(2,1)} %pad_maximum_fusion.2.refs_1_, ...), custom_call_target="tpu_custom_call" | custom-call | flops 899999989760 | bytes 2249999872 | tf_op jit(solution)/shard_map/ffn_back/pallas_call | solution.py:288
  307.3 17.6 %inner_product.1 = (bf16[16,160,1024]{2,1,0:T(8,128)(2,1)}, bf16[16,160,1024]{2,1,0:T(8,128)(2,1)}) custom-call(s32[1]{0:T(128)} %bitcast.refs_0_.me_ref, bf16[1024,1024]{1,0:T(8,128)(2,1)} %get-tuple-element.208.refs_11_.refs_1_, bf16[1024,1024]{1,0:T(8,128)(2,1)} %get-tuple-element.245.refs_2_, bf16[1024,1024]{1,0:T(8,128)(2,1)} %get-tuple-element.251.refs_3_, ...), custom_call_target="tpu_custom_call" | custom-call | flops 359999995904 | bytes 900000000 | tf_op jit(solution)/shard_map/inner_product/pallas_call | solution.py:288
  332.5 19.8 %attend_back.2 = (bf16[1024,1024]{1,0:T(8,128)(2,1)}, bf16[1024,1024]{1,0:T(8,128)(2,1)}, bf16[1024,1024]{1,0:T(8,128)(2,1)}, f32[8,1024]{1,0:T(8,128)}) custom-call(s32[2,512,1]{2,1,0:T(8,128)} %broadcast_in_dim_reshape.6.refs_0_, s32[2,1,512]{2,1,0:T(1,128)} %refs_1_.5, bf16[1024,1024]{1,0:T(8,128)(2,1)} %get-tuple-element.197.refs_2_, ...), custom_call_target="tpu_custom_call" | custom-call | flops 380000010240 | bytes 950000000 | tf_op jit(solution)/shard_map/attend_back/pallas_call | solution.py:288
  368.8 20.0 %attend_back.3 = (bf16[1024,1024]{1,0:T(8,128)(2,1)}, bf16[1024,1024]{1,0:T(8,128)(2,1)}, bf16[1024,1024]{1,0:T(8,128)(2,1)}, f32[8,1024]{1,0:T(8,128)}) custom-call(s32[2,512,1]{2,1,0:T(8,128)} %broadcast_in_dim_reshape.6.refs_0_, s32[2,1,512]{2,1,0:T(1,128)} %refs_1_.5, ...), custom_call_target="tpu_custom_call", output_to_operand_aliasing={{0}: (7, {}), {1}: (8, {}), {2}: (9, {})} | custom-call | flops 380000010240 | bytes 950000000 | tf_op jit(solution)/shard_map/attend_back/pallas_call | solution.py:288
  399.5 11.8 %triple_product.1 = (bf16[16,104,1024]{2,1,0:T(8,128)(2,1)}, bf16[16,104,1024]{2,1,0:T(8,128)(2,1)}) custom-call(s32[1]{0:T(128)} %bitcast.refs_0_.me_ref, bf16[16,16,1024]{2,1,0:T(8,128)(2,1)} %bitcast.62, bf16[1024,1024]{1,0:T(8,128)(2,1)} %get-tuple-element.299.refs_2_, bf16[1024,1024]{1,0:T(8,128)(2,1)} %get-tuple-element.284.refs_3_.refs_12_, ...), custom_call_target="tpu_custom_call" | custom-call | flops 260000006144 | bytes 650000000 | tf_op jit(solution)/shard_map/triple_product/pallas_call | solution.py:288
  411.3 10.1 %stream_back.2 = (f32[1024,1024]{1,0:T(8,128)}, f32[1,1024]{1,0:T(1,128)}) custom-call(s32[1]{0:T(128)} %bitcast.refs_0_.me_ref, bf16[4,144,1024]{2,1,0:T(8,128)(2,1)} %copy-done.3, bf16[4,144,1024]{2,1,0:T(8,128)(2,1)} %copy-done.4, bf16[4,144,1024]{2,1,0:T(8,128)(2,1)} %copy-done.5, bf16[4,144,1024]{2,1,0:T(8,128)(2,1)} %copy-done.25, ...), custom_call_target="tpu_custom_call" | custom-call | flops 199999995904 | bytes 500000000 | tf_op jit(solution)/shard_map/stream_back/pallas_call | solution.py:288
  438.0 10.1 %stream_back.3 = (f32[1024,1024]{1,0:T(8,128)}, f32[1,1024]{1,0:T(1,128)}) custom-call(s32[1]{0:T(128)} %bitcast.refs_0_.me_ref, bf16[4,144,1024]{2,1,0:T(8,128)(2,1)} %copy-done.3, bf16[4,144,1024]{2,1,0:T(8,128)(2,1)} %copy-done.4, bf16[4,144,1024]{2,1,0:T(8,128)(2,1)} %copy-done.5, ...), custom_call_target="tpu_custom_call", output_to_operand_aliasing={{0}: (15, {})} | custom-call | flops 199999995904 | bytes 500000000 | tf_op jit(solution)/shard_map/stream_back/pallas_call | solution.py:288
  453.3 6.4 %collective-permute-done.59.refs_6_ = bf16[1,160,1024]{2,1,0:T(8,128)(2,1)} collective-permute-done((bf16[1,160,1024]{2,1,0:T(8,128)(2,1)}, bf16[1,160,1024]{2,1,0:T(8,128)(2,1)}, u32[]{:S(2)}, u32[]{:S(2)}) %collective-permute-start.59) | collective-permute-done | bytes 327712 | tf_op jit(solution)/shard_map/ppermute | solution.py:80
  471.0 19.4 %collective-permute-done.62 = f32[2,2,2048]{2,1,0:T(2,128)S(1)} collective-permute-done((f32[2,2,2048]{2,1,0:T(2,128)S(1)}, f32[2,2,2048]{2,1,0:T(2,128)S(1)}, u32[]{:S(2)}, u32[]{:S(2)}) %collective-permute-start.62) | collective-permute-done | bytes 32800 | tf_op jit(solution)/shard_map/ppermute | solution.py:80
  514.2 7.6 %collective-permute-done.54.refs_4_ = bf16[1,104,1024]{2,1,0:T(8,128)(2,1)S(1)} collective-permute-done((bf16[1,104,1024]{2,1,0:T(8,128)(2,1)}, bf16[1,104,1024]{2,1,0:T(8,128)(2,1)S(1)}, u32[]{:S(2)}, u32[]{:S(2)}) %collective-permute-start.54) | collective-permute-done | bytes 213024 | tf_op jit(solution)/shard_map/ppermute | solution.py:80
  522.9 5.7 %collective-permute-done.56.refs_6_ = bf16[1,104,1024]{2,1,0:T(8,128)(2,1)S(1)} collective-permute-done((bf16[1,104,1024]{2,1,0:T(8,128)(2,1)}, bf16[1,104,1024]{2,1,0:T(8,128)(2,1)S(1)}, u32[]{:S(2)}, u32[]{:S(2)}) %collective-permute-start.56) | collective-permute-done | bytes 213024 | tf_op jit(solution)/shard_map/ppermute | solution.py:80
  (259 shorter events, 172.1 us)
Async XLA Ops:
  7.1 26.9 %collective-permute-start.2 = (bf16[144,1024]{1,0:T(8,128)(2,1)}, bf16[144,1024]{1,0:T(8,128)(2,1)S(1)}, u32[]{:S(2)}, u32[]{:S(2)}) collective-permute-start(bf16[144,1024]{1,0:T(8,128)(2,1)} %pack.1), channel_id=1, source_target_pairs={{0,24},{1,25},{2,26},{3,27},{4,28},{5,29},{6,30},{7,31},{8,16},{9,... | collective-permute-start | bytes 884744 | tf_op jit(solution)/shard_map/ppermute | solution.py:80
  35.1 30.2 %collective-permute-start.3 = (bf16[4,144,1024]{2,1,0:T(8,128)(2,1)S(1)}, bf16[4,144,1024]{2,1,0:T(8,128)(2,1)S(1)}, u32[]{:S(2)}, u32[]{:S(2)}) collective-permute-start(bf16[4,144,1024]{2,1,0:T(8,128)(2,1)S(1)} %pad_maximum_fusion.1.refs_1_), channel_id=1, source_target_pairs={{0,2},{1,3},{2,0},{3,1},{4,6},{5,7},{6,4},{7,5},{8,10},{9,11},{10,... | collective-permute-start | bytes 3538952 | tf_op jit(solution)/shard_map/ppermute | solution.py:80
  36.6 28.7 %collective-permute-start.4 = (bf16[4,144,1024]{2,1,0:T(8,128)(2,1)S(1)}, bf16[4,144,1024]{2,1,0:T(8,128)(2,1)S(1)}, u32[]{:S(2)}, u32[]{:S(2)}) collective-permute-start(bf16[4,144,1024]{2,1,0:T(8,128)(2,1)S(1)} %pad_maximum_fusion.1.refs_1_), channel_id=1, source_target_pairs={{0,4},{1,5},{2,6},{3,7},{4,0},{5,1},{6,2},{7,3},{8,12},{9,13},{10,... | collective-permute-start | bytes 3538952 | tf_op jit(solution)/shard_map/ppermute | solution.py:80
  38.4 26.9 %collective-permute-start.7 = (bf16[160,1024]{1,0:T(8,128)(2,1)S(1)}, bf16[160,1024]{1,0:T(8,128)(2,1)S(1)}, u32[]{:S(2)}, u32[]{:S(2)}) collective-permute-start(bf16[160,1024]{1,0:T(8,128)(2,1)S(1)} %slice_dynamic-update-slice_fusion), channel_id=1, source_target_pairs={{0,24},{1,25},{2,26},{3,27},{4,28},{5,29},{6,30},{7,31},{8,16},{9,... | collective-permute-start | bytes 983048 | tf_op jit(solution)/shard_map/ppermute | solution.py:80
  82.0 31.0 %collective-permute-start.10 = (bf16[4,160,1024]{2,1,0:T(8,128)(2,1)}, bf16[4,160,1024]{2,1,0:T(8,128)(2,1)}, u32[]{:S(2)}, u32[]{:S(2)}) collective-permute-start(bf16[4,160,1024]{2,1,0:T(8,128)(2,1)} %pad_maximum_fusion.refs_1_.refs_11_), channel_id=1, source_target_pairs={{0,2},{1,3},{2,0},{3,1},{4,6},{5,7},{6,4},{7,5},{8,10},{9,11},{10,... | collective-permute-start | bytes 3932168 | tf_op jit(solution)/shard_map/ppermute | solution.py:80
  83.5 30.7 %collective-permute-start.11 = (bf16[4,160,1024]{2,1,0:T(8,128)(2,1)}, bf16[4,160,1024]{2,1,0:T(8,128)(2,1)}, u32[]{:S(2)}, u32[]{:S(2)}) collective-permute-start(bf16[4,160,1024]{2,1,0:T(8,128)(2,1)} %pad_maximum_fusion.refs_1_.refs_11_), channel_id=1, source_target_pairs={{0,4},{1,5},{2,6},{3,7},{4,0},{5,1},{6,2},{7,3},{8,12},{9,13},{10,... | collective-permute-start | bytes 3932168 | tf_op jit(solution)/shard_map/ppermute | solution.py:80
  119.2 46.1 %collective-permute-start.24 = (bf16[4,160,1024]{2,1,0:T(8,128)(2,1)}, bf16[4,160,1024]{2,1,0:T(8,128)(2,1)}, u32[]{:S(2)}, u32[]{:S(2)}) collective-permute-start(bf16[4,160,1024]{2,1,0:T(8,128)(2,1)} %pad_maximum_fusion.refs_1_.refs_11_), channel_id=1, source_target_pairs={{0,1},{1,0},{2,3},{3,2},{4,5},{5,4},{6,7},{7,6},{8,9},{9,8},{10,11... | collective-permute-start | bytes 3932168 | tf_op jit(solution)/shard_map/ppermute | solution.py:80
  123.2 39.4 %collective-permute-start.20 = (bf16[2,160,1024]{2,1,0:T(8,128)(2,1)}, bf16[2,160,1024]{2,1,0:T(8,128)(2,1)}, u32[]{:S(2)}, u32[]{:S(2)}) collective-permute-start(bf16[2,160,1024]{2,1,0:T(8,128)(2,1)} %slice.106), channel_id=1, source_target_pairs={{0,2},{1,3},{2,0},{3,1},{4,6},{5,7},{6,4},{7,5},{8,10},{9,11},{10,... | collective-permute-start | bytes 1966088 | tf_op jit(solution)/shard_map/ppermute | solution.py:80
  127.1 35.5 %collective-permute-start.21 = (bf16[2,160,1024]{2,1,0:T(8,128)(2,1)}, bf16[2,160,1024]{2,1,0:T(8,128)(2,1)}, u32[]{:S(2)}, u32[]{:S(2)}) collective-permute-start(bf16[2,160,1024]{2,1,0:T(8,128)(2,1)} %slice.107), channel_id=1, source_target_pairs={{0,4},{1,5},{2,6},{3,7},{4,0},{5,1},{6,2},{7,3},{8,12},{9,13},{10,... | collective-permute-start | bytes 1966088 | tf_op jit(solution)/shard_map/ppermute | solution.py:80
  133.5 34.1 %collective-permute-start.27 = (bf16[4,160,1024]{2,1,0:T(8,128)(2,1)}, bf16[4,160,1024]{2,1,0:T(8,128)(2,1)}, u32[]{:S(2)}, u32[]{:S(2)}) collective-permute-start(bf16[4,160,1024]{2,1,0:T(8,128)(2,1)} %collective-permute-done.10.refs_7_.refs_17_), channel_id=1, source_target_pairs={{0,1},{1,0},{2,3},{3,2},{4,5},{5,4},{6,7},{7,6},{8,9},{9,8},{10,11... | collective-permute-start | bytes 3932168 | tf_op jit(solution)/shard_map/ppermute | solution.py:80
  138.9 28.6 %collective-permute-start.28 = (bf16[4,160,1024]{2,1,0:T(8,128)(2,1)}, bf16[4,160,1024]{2,1,0:T(8,128)(2,1)}, u32[]{:S(2)}, u32[]{:S(2)}) collective-permute-start(bf16[4,160,1024]{2,1,0:T(8,128)(2,1)} %collective-permute-done.11.refs_8_.refs_18_), channel_id=1, source_target_pairs={{0,1},{1,0},{2,3},{3,2},{4,5},{5,4},{6,7},{7,6},{8,9},{9,8},{10,11... | collective-permute-start | bytes 3932168 | tf_op jit(solution)/shard_map/ppermute | solution.py:80
  167.5 51.7 %collective-permute-start.29 = (bf16[4,128,1024]{2,1,0:T(8,128)(2,1)}, bf16[4,128,1024]{2,1,0:T(8,128)(2,1)}, u32[]{:S(2)}, u32[]{:S(2)}) collective-permute-start(bf16[4,128,1024]{2,1,0:T(8,128)(2,1)} %pad_maximum_fusion.2.refs_1_), channel_id=1, source_target_pairs={{0,1},{1,0},{2,3},{3,2},{4,5},{5,4},{6,7},{7,6},{8,9},{9,8},{10,11... | collective-permute-start | bytes 3145736 | tf_op jit(solution)/shard_map/ppermute | solution.py:80
  193.4 27.6 %collective-permute-start.30 = (bf16[4,128,1024]{2,1,0:T(8,128)(2,1)}, bf16[4,128,1024]{2,1,0:T(8,128)(2,1)}, u32[]{:S(2)}, u32[]{:S(2)}) collective-permute-start(bf16[4,128,1024]{2,1,0:T(8,128)(2,1)} %collective-permute-done.22.refs_2_), channel_id=1, source_target_pairs={{0,1},{1,0},{2,3},{3,2},{4,5},{5,4},{6,7},{7,6},{8,9},{9,8},{10,11... | collective-permute-start | bytes 3145736 | tf_op jit(solution)/shard_map/ppermute | solution.py:80
  257.1 46.8 %collective-permute-start.36 = (bf16[16,128,1024]{2,1,0:T(8,128)(2,1)}, bf16[16,128,1024]{2,1,0:T(8,128)(2,1)}, u32[]{:S(2)}, u32[]{:S(2)}) collective-permute-start(bf16[16,128,1024]{2,1,0:T(8,128)(2,1)} %get-tuple-element.238), channel_id=1, source_target_pairs={{0,1},{1,0},{2,3},{3,2},{4,5},{5,4},{6,7},{7,6},{8,9},{9,8},{10,11... | collective-permute-start | bytes 12582920 | tf_op jit(solution)/shard_map/ppermute | solution.py:80
  325.0 39.0 %collective-permute-start.39 = (bf16[16,160,1024]{2,1,0:T(8,128)(2,1)}, bf16[16,160,1024]{2,1,0:T(8,128)(2,1)}, u32[]{:S(2)}, u32[]{:S(2)}) collective-permute-start(bf16[16,160,1024]{2,1,0:T(8,128)(2,1)} %get-tuple-element.254), channel_id=1, source_target_pairs={{0,1},{1,0},{2,3},{3,2},{4,5},{5,4},{6,7},{7,6},{8,9},{9,8},{10,11... | collective-permute-start | bytes 15728648 | tf_op jit(solution)/shard_map/ppermute | solution.py:80
  329.6 25.9 %collective-permute-start.40 = (bf16[4,128,1024]{2,1,0:T(8,128)(2,1)}, bf16[4,128,1024]{2,1,0:T(8,128)(2,1)}, u32[]{:S(2)}, u32[]{:S(2)}) collective-permute-start(bf16[4,128,1024]{2,1,0:T(8,128)(2,1)} %get-tuple-element.259), channel_id=1, source_target_pairs={{0,2},{1,3},{2,0},{3,1},{4,6},{5,7},{6,4},{7,5},{8,10},{9,11},{10,... | collective-permute-start | bytes 3145736 | tf_op jit(solution)/shard_map/ppermute | solution.py:80
  360.5 28.3 %collective-permute-start.44 = (bf16[1,128,1024]{2,1,0:T(8,128)(2,1)}, bf16[1,128,1024]{2,1,0:T(8,128)(2,1)}, u32[]{:S(2)}, u32[]{:S(2)}) collective-permute-start(bf16[1,128,1024]{2,1,0:T(8,128)(2,1)} %get-tuple-element.274), channel_id=1, source_target_pairs={{0,16},{1,17},{2,18},{3,19},{4,20},{5,21},{6,22},{7,23},{8,24},{9,... | collective-permute-start | bytes 786440 | tf_op jit(solution)/shard_map/ppermute | solution.py:80
  360.5 28.3 %collective-permute-start.45 = (bf16[1,128,1024]{2,1,0:T(8,128)(2,1)}, bf16[1,128,1024]{2,1,0:T(8,128)(2,1)}, u32[]{:S(2)}, u32[]{:S(2)}) collective-permute-start(bf16[1,128,1024]{2,1,0:T(8,128)(2,1)} %get-tuple-element.275), channel_id=1, source_target_pairs={{0,8},{1,9},{2,10},{3,11},{4,12},{5,13},{6,14},{7,15},{8,0},{9,1},... | collective-permute-start | bytes 786440 | tf_op jit(solution)/shard_map/ppermute | solution.py:80
  361.5 27.3 %collective-permute-start.46 = (bf16[1,128,1024]{2,1,0:T(8,128)(2,1)}, bf16[1,128,1024]{2,1,0:T(8,128)(2,1)}, u32[]{:S(2)}, u32[]{:S(2)}) collective-permute-start(bf16[1,128,1024]{2,1,0:T(8,128)(2,1)} %get-tuple-element.276), channel_id=1, source_target_pairs={{0,24},{1,25},{2,26},{3,27},{4,28},{5,29},{6,30},{7,31},{8,16},{9,... | collective-permute-start | bytes 786440 | tf_op jit(solution)/shard_map/ppermute | solution.py:80
  396.7 29.0 %collective-permute-start.48 = (bf16[4,160,1024]{2,1,0:T(8,128)(2,1)}, bf16[4,160,1024]{2,1,0:T(8,128)(2,1)}, u32[]{:S(2)}, u32[]{:S(2)}) collective-permute-start(bf16[4,160,1024]{2,1,0:T(8,128)(2,1)} %get-tuple-element.289), channel_id=1, source_target_pairs={{0,2},{1,3},{2,0},{3,1},{4,6},{5,7},{6,4},{7,5},{8,10},{9,11},{10,... | collective-permute-start | bytes 3932168 | tf_op jit(solution)/shard_map/ppermute | solution.py:80
  398.1 28.7 %collective-permute-start.49 = (bf16[4,160,1024]{2,1,0:T(8,128)(2,1)}, bf16[4,160,1024]{2,1,0:T(8,128)(2,1)}, u32[]{:S(2)}, u32[]{:S(2)}) collective-permute-start(bf16[4,160,1024]{2,1,0:T(8,128)(2,1)} %get-tuple-element.290), channel_id=1, source_target_pairs={{0,4},{1,5},{2,6},{3,7},{4,0},{5,1},{6,2},{7,3},{8,12},{9,13},{10,... | collective-permute-start | bytes 3932168 | tf_op jit(solution)/shard_map/ppermute | solution.py:80
  432.8 26.9 %collective-permute-start.59 = (bf16[1,160,1024]{2,1,0:T(8,128)(2,1)}, bf16[1,160,1024]{2,1,0:T(8,128)(2,1)}, u32[]{:S(2)}, u32[]{:S(2)}) collective-permute-start(bf16[1,160,1024]{2,1,0:T(8,128)(2,1)} %get-tuple-element.317), channel_id=1, source_target_pairs={{0,24},{1,25},{2,26},{3,27},{4,28},{5,29},{6,30},{7,31},{8,16},{9,... | collective-permute-start | bytes 983048 | tf_op jit(solution)/shard_map/ppermute | solution.py:80
  466.9 37.2 %collective-permute-start.52 = (bf16[4,104,1024]{2,1,0:T(8,128)(2,1)}, bf16[4,104,1024]{2,1,0:T(8,128)(2,1)S(1)}, u32[]{:S(2)}, u32[]{:S(2)}) collective-permute-start(bf16[4,104,1024]{2,1,0:T(8,128)(2,1)} %get-tuple-element.325), channel_id=1, source_target_pairs={{0,2},{1,3},{2,0},{3,1},{4,6},{5,7},{6,4},{7,5},{8,10},{9,11},{10,... | collective-permute-start | bytes 2555912 | tf_op jit(solution)/shard_map/ppermute | solution.py:80
  468.3 35.7 %collective-permute-start.53 = (bf16[4,104,1024]{2,1,0:T(8,128)(2,1)}, bf16[4,104,1024]{2,1,0:T(8,128)(2,1)S(1)}, u32[]{:S(2)}, u32[]{:S(2)}) collective-permute-start(bf16[4,104,1024]{2,1,0:T(8,128)(2,1)} %get-tuple-element.326), channel_id=1, source_target_pairs={{0,4},{1,5},{2,6},{3,7},{4,0},{5,1},{6,2},{7,3},{8,12},{9,13},{10,... | collective-permute-start | bytes 2555912 | tf_op jit(solution)/shard_map/ppermute | solution.py:80
  (80 other events, 1006.7 us)

commit v3 on v2

--- a/solution.py
+++ b/solution.py
@@ -51,6 +51,29 @@
     mean_grad = jnp.mean(grad_normed, axis=-1, keepdims=True)
     mean_cross = jnp.mean(grad_normed * normed, axis=-1, keepdims=True)
     return spread * (grad_normed - mean_grad - normed * mean_cross)
+
+
+def halves_body(low_in, high_in, low_out, high_out):
+    low_out[...] = low_in[...]
+    high_out[...] = high_in[...]
+
+
+def halves(low_of, high_of):
+    count, half = low_of.shape[0], low_of.shape[0] // 2
+    block = (1,) + low_of.shape[1:]
+    return pl.pallas_call(
+        halves_body,
+        grid=(half,),
+        in_specs=[
+            pl.BlockSpec(block, lambda i: (i, 0, 0)),
+            pl.BlockSpec(block, lambda i: (half + i, 0, 0)),
+        ],
+        out_specs=[pl.BlockSpec(block, lambda i: (i, 0, 0))] * 2,
+        out_shape=[jax.ShapeDtypeStruct((half,) + low_of.shape[1:], low_of.dtype)] * 2,
+        compiler_params=pltpu.CompilerParams(vmem_limit_bytes=60 << 20),
+        cost_estimate=pl.CostEstimate(flops=1000, bytes_accessed=1000, transcendentals=0),
+        name="halves",
+    )(low_of, high_of)
 
 
 class Net:
@@ -99,7 +122,7 @@
             pieces += [([s ^ mask for s in sources], array) for mask, array in group]
         for mask_x, array_x in near[0]:
             for mask_y, array_y in near[1]:
-                low, high = array_y[:half], array_x[half:]
+                low, high = halves(array_y, array_x)
                 sent += [low, high]
                 corner = mask_x ^ mask_y
                 corners.append(([s ^ corner for s in sources[:half]], self.swap(low, mask_x)))
@@ -217,15 +240,20 @@
     def __init__(self, net, me, wanted):
         self.arrays, self.plans, self.shapes = [], [], []
         seen = {}
-        for pieces, place, rows in wanted:
+        for pieces, places, rows in wanted:
+            places = (places,) if isinstance(places, int) else tuple(places)
             columns = pieces[0][1].shape[-1]
             plan = []
             if rows % 16:
-                blocks = jnp.concatenate([array[:, place : place + rows] for _, array in pieces])
+                blocks = [
+                    jnp.concatenate([array[:, place : place + rows] for _, array in pieces])
+                    for place in places
+                ]
+                blocks = jnp.concatenate(blocks, axis=2)
                 order = jnp.asarray([s for own, _ in pieces for s in own], jnp.int32)
                 spot = jnp.zeros((net.n,), jnp.int32).at[order ^ me].set(jnp.arange(net.n))
-                whole = blocks[spot].reshape(net.n * rows // 16, 16, columns)
-                plan.append((len(self.arrays), None, None))
+                whole = blocks[spot].reshape(net.n * rows // 16, 16, len(places) * columns)
+                plan.append((len(self.arrays), None, None, None))
                 self.arrays.append(whole)
                 self.shapes.append(whole.shape)
             else:
@@ -234,8 +262,10 @@
                         seen[id(array)] = len(self.arrays)
                         self.arrays.append(array)
                     for j, source in enumerate(own):
-                        plan.append((seen[id(array)], (j, pl.ds(place, rows)), source))
-                self.shapes.append((net.n, rows, columns))
+                        for k, place in enumerate(places):
+                            aim = pl.ds(k * columns, columns)
+                            plan.append((seen[id(array)], (j, pl.ds(place, rows)), source, aim))
+                self.shapes.append((net.n, rows, len(places) * columns))
             self.plans.append(plan)
         self.slots = max(len(plan) for plan in self.plans)
 
@@ -246,11 +276,11 @@
 
     def copies(self, w, me, array_refs, held_ref, sems):
         found = []
-        for slot, (array, index, source) in enumerate(self.plans[w]):
+        for slot, (array, index, source, aim) in enumerate(self.plans[w]):
             if index is None:
                 pair = (array_refs[array], held_ref)
             else:
-                pair = (array_refs[array].at[index], held_ref.at[me ^ source])
+                pair = (array_refs[array].at[index], held_ref.at[me ^ source, :, aim])
             found.append(pltpu.make_async_copy(*pair, sems.at[w, slot]))
         return found
 
@@ -317,7 +347,7 @@
         out_ref[...] = total.astype(out_ref.dtype)
 
 
-def sum_call(me, name, grid, ins, groups, outs, body=None):
+def sum_call(me, name, grid, ins, groups, outs, body=None, us=0.01):
     grid_spec = pltpu.PrefetchScalarGridSpec(
         num_scalar_prefetch=1,
         grid=(grid,),
@@ -337,7 +367,7 @@
         compiler_params=pltpu.CompilerParams(
             vmem_limit_bytes=60 << 20, dimension_semantics=("arbitrary",)
         ),
-        cost_estimate=pl.CostEstimate(flops=1000, bytes_accessed=1000, transcendentals=0),
+        cost_estimate=pl.CostEstimate(flops=int(us * 2e10), bytes_accessed=int(us * 5e7), transcendentals=0),
         name=name,
     )(me.reshape(1), *[array for array, _, _ in ins])
 
@@ -441,6 +471,9 @@
         self.terms += [net.swap(part, mask) for part, mask in zip(sent, masks)]
         return sent
 
+    def received(self):
+        return self.terms[-1] if self.plain else self.state[0][-1]
+
     def end(self, lots, unit):
         if not self.plain:
             total = self.net.scatter_end(self.state)
@@ -476,7 +509,7 @@
                 def _():
                     out_ref[...] = total
 
-        return sum_call(self.me, "end_sum", start, ins, None, outs, body)
+        return sum_call(self.me, "end_sum", start, ins, None, outs, body, 4)
 
 
 def pack_body(step, me_ref, lines_ref, inner_ref, *refs):
@@ -598,7 +631,7 @@
 
 
 def attend_back_body(
-    head_dim, segc_ref, segr_ref, q_ref, k_ref, v_ref, log_ref, g_ref, gq_ref, gk_ref, gv_ref, sums_ref, bias_ref
+    head_dim, segc_ref, segr_ref, q_ref, k_ref, v_ref, log_ref, g_ref, gq_ref, gk_ref, gv_ref, sums_ref, rows_ref, bias_ref
 ):
     same_document(segc_ref, segr_ref, bias_ref, pl.program_id(1))
     queries, key_rows, values, grads = q_ref[...], k_ref[...], v_ref[...], g_ref[...]
@@ -625,10 +658,13 @@
     gq = (totals[0] * scale).astype(BF16)
     gv = totals[2].astype(BF16)
     gq_ref[...] = gq
-    gk_ref[...] = (totals[1] * scale).astype(BF16)
+    gk = (totals[1] * scale).astype(BF16)
+    gk_ref[...] = gk
     gv_ref[...] = gv
-    sums = [jnp.sum(part.astype(F32), axis=0, keepdims=True) for part in (gq, gv)]
-    sums_ref[...] = jnp.concatenate(sums + [jnp.zeros_like(sums[0])] * 6)
+    sums = [jnp.sum(part.astype(F32), axis=0, keepdims=True) for part in (gq, gk, gv)]
+    zero = jnp.zeros_like(sums[0])
+    sums_ref[...] = jnp.concatenate([sums[0], sums[2]] + [zero] * 6)
+    rows_ref[...] = jnp.concatenate(sums + [zero] * 5)
 
 
 def attention_args(segments, start, lanes, head_dim):
@@ -640,7 +676,7 @@
     return [(segments[:, :, None], segc), (segments[:, None, :], segr)], block, log_spec
 
 
-def attend(queries, key_rows, values, segments, lanes=128):
+def attend(queries, key_rows, values, segments, lanes=256):
     rows, row_length = segments.shape
     tokens, width = queries.shape
     head_dim = width // H
@@ -660,7 +696,7 @@
     )
 
 
-def attend_back(queries, key_rows, values, segments, log_total, grad_context, row, bases=(), lanes=128):
+def attend_back(queries, key_rows, values, segments, log_total, grad_context, row, bases=(), lanes=256):
     rows, row_length = segments.shape
     tokens, width = queries.shape
     head_dim = width // H
@@ -673,7 +709,7 @@
         + [(array, block) for array in (queries, key_rows, values)]
         + [(log_total, log_spec), (grad_context, block)],
         [((tokens, width), BF16, block)] * 3
-        + [((8, width), F32, pl.BlockSpec((8, lanes), lambda i, j: (0, j)))],
+        + [((8, width), F32, pl.BlockSpec((8, lanes), lambda i, j: (0, j)))] * 2,
         [pltpu.VMEM((row_length, row_length), F32)],
         19,
         bases,
@@ -706,54 +742,60 @@
         ref[...] += part
 
 
-def ffn_in_body(weights, row, chunk, me_ref, *refs):
+def ffn_in_body(weights, tile, row_length, chunk, me_ref, *refs):
     count = len(weights.arrays)
     arrays, refs = refs[:count], refs[count:]
     context_ref, x_ref, temb_ref, lines_ref = refs[:4]
     first_low_ref, normed_ref, spread_ref, active_ref, slope_ref = refs[4:9]
-    ow, iws, sems = refs[9], refs[10:14], refs[14]
+    ow, iw, sems = refs[9:12]
     me, step = me_ref[0], pl.program_id(0)
 
     @pl.when(step == 0)
     def _():
-        for w, held in enumerate((ow,) + iws):
+        for w, held in enumerate((ow, iw)):
             weights.start(w, me, arrays, held, sems)
         weights.wait(0, me, arrays, ow, sems)
 
-    stream = x_ref[...].astype(F32) + temb_ref[row : row + 1, :]
+    row = step * tile // row_length
+    stream = x_ref[...].astype(F32) + temb_ref[pl.ds(row, 1), :]
     mixed = stream + (matmul(context_ref[...], flat(ow[...])) + lines_ref[2:3])
     normed, spread = normalize(mixed)
     normed_ref[...] = normed
     spread_ref[...] = spread
     first = normed * lines_ref[4:5] + lines_ref[5:6]
-    first_low_ref[...] = first.astype(BF16)
-    width = ow.shape[2]
-    for k, iw in enumerate(iws):
-
-        @pl.when(step == 0)
-        def _():
-            weights.wait(k + 1, me, arrays, iw, sems)
-
-        @pl.loop(0, width // chunk)
-        def _(j):
-            inner = pl.ds(pl.multiple_of(j * chunk, chunk), chunk)
-            columns = pl.ds(pl.multiple_of(k * width + j * chunk, chunk), chunk)
-            pre = matmul(first_low_ref[...], flat(iw[:, :, inner])) + lines_ref[8 + k : 9 + k, inner]
-            normal_cdf = 0.5 * (1.0 + lax.erf(pre * INV_ROOT_TWO))
-            normal_pdf = jnp.exp(-0.5 * pre * pre) * INV_ROOT_TAU
-            active_ref[:, columns] = (pre * normal_cdf).astype(BF16)
-            slope_ref[:, columns] = (normal_cdf + pre * normal_pdf).astype(BF16)
-
-
-def ffn_in(net, me, flow, context, x, temb, lines, hidden, row, row_length, bases=(), tile=256, chunk=512):
+    low = first.astype(BF16)
+    first_low_ref[...] = low
+
+    @pl.when(step == 0)
+    def _():
+        weights.wait(1, me, arrays, iw, sems)
+
+    width, hidden = ow.shape[2], iw.shape[2]
+
+    def inner(start):
+        pre = matmul(low, flat(iw[:, :, start : start + chunk]))
+        line, place = 8 + start // width, start % width
+        return pre + lines_ref[line : line + 1, place : place + chunk]
+
+    later = inner(0)
+    for start in range(0, hidden, chunk):
+        pre = later
+        if start + chunk < hidden:
+            later = inner(start + chunk)
+        columns = slice(start, start + chunk)
+        normal_cdf = 0.5 * (1.0 + lax.erf(pre * INV_ROOT_TWO))
+        normal_pdf = jnp.exp(-0.5 * pre * pre) * INV_ROOT_TAU
+        active_ref[:, columns] = (pre * normal_cdf).astype(BF16)
+        slope_ref[:, columns] = (normal_cdf + pre * normal_pdf).astype(BF16)
+
+
+def ffn_in(net, me, flow, context, x, temb, lines, hidden, row_length, tile=256, chunk=512):
     tokens, width = x.shape
     r = width // net.n
-    weights = Weights(net, me, [(flow, w * r, r) for w in range(1 + hidden // width)])
+    blocks = range(r, r + hidden // width * r, r)
+    weights = Weights(net, me, [(flow, 0, r), (flow, blocks, r)])
     tile = min(tile, row_length)
-    start = row * (row_length // tile)
-    tiled, wide, thin = (
-        pl.BlockSpec((tile, columns), lambda i: (start + i, 0)) for columns in (width, hidden, 1)
-    )
+    tiled, wide, thin = (tile_spec(tile, columns) for columns in (width, hidden, 1))
     ins = (
         [(me.reshape(1), SMEM_SPEC)]
         + [(array, ANY_SPEC) for array in weights.arrays]
@@ -768,14 +810,13 @@
         ((tokens, hidden), BF16, wide),
     ]
     return call(
-        functools.partial(ffn_in_body, weights, row, chunk),
+        functools.partial(ffn_in_body, weights, tile, row_length, chunk),
         "ffn_in",
-        (row_length // tile,),
+        (tokens // tile,),
         ins,
         outs,
         weights.scratch(),
-        16,
-        bases,
+        30,
     )
 
 
@@ -832,45 +873,44 @@
     )
 
 
-def ffn_back_body(weights, chunk, me_ref, *refs):
+def ffn_back_body(weights, tile, row_length, chunk, me_ref, *refs):
     count = len(weights.arrays)
     arrays, refs = refs[:count], refs[count:]
     (gs_ref, gs_low_ref, slope_ref, normed_ref, spread_ref, lines_ref) = refs[:6]
-    (gi_ref, gm_ref, gm_low_ref, gc_ref, ibg_ref, sums_ref) = refs[6:12]
-    uw, ow, iws, sems, acc_ref = refs[12], refs[13], refs[14:18], refs[18], refs[19]
+    (gi_ref, gm_ref, gm_low_ref, gc_ref, ibg_ref, sums_ref, rows_ref) = refs[6:13]
+    uw, ow, iw, sems = refs[13:17]
     me, step = me_ref[0], pl.program_id(0)
-    helds = (uw, ow) + iws
 
     @pl.when(step == 0)
     def _():
-        for w in (0, 2, 3, 4, 5, 1):
-            weights.start(w, me, arrays, helds[w], sems)
+        for w, held in ((0, uw), (2, iw), (1, ow)):
+            weights.start(w, me, arrays, held, sems)
         weights.wait(0, me, arrays, uw, sems)
 
-    acc_ref[...] = gs_ref[...]
     unit = uw.shape[1]
-    width = ow.shape[2]
-    for k, iw in enumerate(iws):
-
-        @pl.when(step == 0)
-        def _():
-            weights.wait(k + 2, me, arrays, iw, sems)
-
-        @pl.loop(0, width // chunk)
-        def _(j):
-            inner = pl.ds(pl.multiple_of(j * chunk, chunk), chunk)
-            columns = pl.ds(pl.multiple_of(k * width + j * chunk, chunk), chunk)
-            span = chunk // unit
-            held = flat(uw[pl.ds(k * (width // unit) + j * span, span)])
-            grad_active = matmul_right(gs_low_ref[...], held)
-            low = (grad_active * slope_ref[:, columns].astype(F32)).astype(BF16)
-            gi_ref[:, columns] = low
-            acc_ref[...] += matmul_right(low, flat(iw[:, :, inner]))
-
+    hidden = iw.shape[2]
+    for start in range(0, hidden, chunk):
+        columns = slice(start, start + chunk)
+        held = flat(uw[start // unit : (start + chunk) // unit])
+        grad_active = matmul_right(gs_low_ref[...], held)
+        gi_ref[:, columns] = (grad_active * slope_ref[:, columns].astype(F32)).astype(BF16)
+
+    @pl.when(step == 0)
+    def _():
+        weights.wait(2, me, arrays, iw, sems)
+
+    grad_first = gs_ref[...] + matmul_right(gi_ref[...], flat(iw[...]))
     add_to(ibg_ref, gi_ref[...].astype(F32), step)
-    grad_first, normed = acc_ref[...], normed_ref[...]
+    normed = normed_ref[...]
     grad_mixed = norm_back(grad_first * lines_ref[4:5], normed, spread_ref[...])
     gm_ref[...] = grad_mixed
+
+    @pl.when(step == 0)
+    def _():
+        rows_ref[...] = jnp.zeros_like(rows_ref)
+
+    row = pl.ds(step * tile // row_length, 1)
+    rows_ref[row, :] += jnp.sum(grad_mixed, axis=0, keepdims=True)
     low = grad_mixed.astype(BF16)
     gm_low_ref[...] = low
     add_lines(sums_ref, {2: low.astype(F32), 4: grad_first * normed, 5: grad_first}, step)
@@ -882,17 +922,20 @@
     gc_ref[...] = matmul_right(low, flat(ow[...])).astype(BF16)
 
 
-def ffn_back(net, me, flow_u, flow_io, gs, gs_low, slope, normed, spread, lines, tile=256, chunk=512):
+def ffn_back(net, me, flow_u, flow_io, gs, gs_low, slope, normed, spread, lines, row_length, tile=256, chunk=1024):
     tokens, width = gs.shape
     hidden = slope.shape[1]
     r = width // net.n
     weights = Weights(
         net,
         me,
-        [(flow_u, 0, hidden // net.n)]
-        + [(flow_io, w * r, r) for w in range(1 + hidden // width)],
-    )
-    tile = min(tile, tokens)
+        [
+            (flow_u, 0, hidden // net.n),
+            (flow_io, 0, r),
+            (flow_io, range(r, r + hidden // width * r, r), r),
+        ],
+    )
+    tile = min(tile, row_length)
     tiled, wide = tile_spec(tile, width), tile_spec(tile, hidden)
     ins = (
         [(me.reshape(1), SMEM_SPEC)]
@@ -907,15 +950,16 @@
         ((tokens, width), BF16, tiled),
         ((1, hidden), F32, full_spec((1, hidden))),
         ((8, width), F32, full_spec((8, width))),
+        ((8, width), F32, full_spec((8, width))),
     ]
     return call(
-        functools.partial(ffn_back_body, weights, chunk),
+        functools.partial(ffn_back_body, weights, tile, row_length, chunk),
         "ffn_back",
         (tokens // tile,),
         ins,
         outs,
-        weights.scratch() + [pltpu.VMEM((tile, width), F32)],
-        45,
+        weights.scratch(),
+        38,
     )
 
 
@@ -932,7 +976,7 @@
     deal(me_ref, matmul_left(a_ref[...], b_ref[...]), rows, keep_ref, send_ref)
 
 
-def product(net, me, left, right, tile=512):
+def product(net, me, left, right, tile=1024):
     tokens, width = left.shape
     columns = right.shape[1]
     rows = width // net.n
@@ -1022,12 +1066,13 @@
     )
 
 
-def stream_back_body(weights, me_ref, *refs):
+def stream_back_body(weights, rows, me_ref, *refs):
     count = len(weights.arrays)
     arrays, refs = refs[:count], refs[count:]
     gm_ref, gq_ref, gk_ref, gv_ref = refs[:4]
-    out_ref, gt_ref = refs[4:6]
-    qw, kw, vw, sems = refs[6:10]
+    sum_refs, refs = refs[4 : 4 + rows], refs[4 + rows :]
+    out_ref, outs = refs[0], refs[1:]
+    qw, kw, vw, sems = outs[-4:]
     me, step = me_ref[0], pl.program_id(0)
 
     @pl.when(step == 0)
@@ -1036,18 +1081,23 @@
             weights.start(w, me, arrays, held, sems)
         for w, held in enumerate((qw, kw, vw)):
             weights.wait(w, me, arrays, held, sems)
-
-    total = (
+        if sum_refs:
+            total = sum_refs[0][...]
+            for w, held in enumerate((qw, kw, vw)):
+                lines = [ref[w : w + 1] for ref in sum_refs[1:]]
+                lines += [jnp.zeros_like(lines[0])] * (8 - len(lines))
+                total += matmul_right(jnp.concatenate(lines).astype(BF16), flat(held[...]))
+            outs[0][...] = total
+
+    out_ref[...] = (
         gm_ref[...]
         + matmul_right(gq_ref[...], flat(qw[...]))
         + matmul_right(gk_ref[...], flat(kw[...]))
         + matmul_right(gv_ref[...], flat(vw[...]))
     )
-    out_ref[...] = total
-    add_to(gt_ref, total, step)
-
-
-def stream_back(net, me, flow, gm, gq, gk, gv, row, row_length, base=None, tile=256):
+
+
+def stream_back(net, me, flow, gm, gq, gk, gv, row, row_length, base=None, sums=(), tile=256):
     tokens, width = gm.shape
     tile = min(tile, row_length)
     r = width // net.n
@@ -1058,13 +1108,17 @@
         [(me.reshape(1), SMEM_SPEC)]
         + [(array, ANY_SPEC) for array in weights.arrays]
         + [(array, tiled) for array in (gm, gq, gk, gv)]
-    )
+        + [(array, full_spec((8, width))) for array in sums]
+    )
+    outs = [((tokens, width), F32, tiled)]
+    if sums:
+        outs.append(((8, width), F32, full_spec((8, width))))
     return call(
-        functools.partial(stream_back_body, weights),
+        functools.partial(stream_back_body, weights, len(sums)),
         "stream_back",
         (row_length // tile,),
         ins,
-        [((tokens, width), F32, tiled), ((1, width), F32, full_spec((1, width)))],
+        outs,
         weights.scratch(),
         10,
         () if base is None else (base,),
@@ -1146,12 +1200,12 @@
     far_io = net.gather_far(shard_io)
     far = net.stacked(far)
     near = net.gather_near(far)
-    near, far_io = after((near, far_io), ())
     pieces, corners, _ = net.gather_corner(far, near)
     flow = net.gather_core(pieces)
-    far_io, corners = after((net.stacked(far_io), corners), ())
+    far_io, corners, shard_u = after((net.stacked(far_io), corners, outer_weight), ())
     near_io = net.gather_near(far_io)
     flow += net.gather_core(corners)
+    far_u = net.gather_far(after(shard_u, flow))
 
     segments = segments.reshape(rows, row_length)
     x = inputs.reshape(tokens, model_width)
@@ -1159,27 +1213,21 @@
     temb, lines, stream_low, queries, key_rows, values = project(
         net, me, flow, feats_in, x, row_length
     )
-    near_io, queries, shard_u = after((near_io, queries, outer_weight), ())
+    far_u = net.stacked(after(far_u, queries))
+    near_io, queries = after((near_io, queries), far_u)
     pieces, corners, sent = net.gather_corner(far_io, near_io)
-    flow_io = net.gather_core(pieces[:1])
-    far_u = net.gather_far(shard_u)
-    queries = after(queries, sent)
+    far_u = after(far_u, sent)
+    near_u = net.gather_near(far_u)
+    queries = after(queries, (sent, far_u))
     context, log_total = attend(queries, key_rows, values, segments)
-    far_u, corners, context = after((far_u, corners, context), ())
-    flow_io += net.gather_core(corners) + net.gather_core(pieces[1:])
-    far_u = net.stacked(far_u)
-    near_u = net.gather_near(far_u)
-    context = after(context, far_u)
-    fed, sent = (), ()
-    for row in range(rows):
-        if row == 1:
-            near_u, fed = after((near_u, fed), ())
-            pieces, corners, sent = net.gather_corner(far_u, near_u)
-            fed = after(fed, sent)
-        fed = ffn_in(
-            net, me, flow_io, context, x, temb, lines, hidden, row, row_length, fed
-        )
-    first_low, normed_first, spread_first, active_low, slope = fed
+    corners, context, pieces = after((corners, context, pieces), ())
+    flow_io = net.gather_core(pieces) + net.gather_core(corners)
+    near_u, flow_io = after((near_u, flow_io), ())
+    pieces, corners, sent = net.gather_corner(far_u, near_u)
+    context = after(context, sent)
+    first_low, normed_first, spread_first, active_low, slope = ffn_in(
+        net, me, flow_io, context, x, temb, lines, hidden, row_length
+    )
     corners, active_low = after((corners, active_low), ())
     flow_u = net.gather_core(pieces) + net.gather_core(corners)
     (
@@ -1206,6 +1254,7 @@
         grad_context,
         inner_bias_grad,
         sums_back,
+        mixed_rows,
     ) = ffn_back(
         net,
         me,
@@ -1217,6 +1266,7 @@
         normed_first,
         spread_first,
         lines,
+        row_length,
     )
     sent = outer_sum.hold(grad_mixed_low).corner()
     grad_mixed_low = after(grad_mixed_low, sent)
@@ -1225,13 +1275,14 @@
     sent = outer_sum.hold(inner_halves).near()
     grad_context = after(grad_context, (inner_halves, sent))
     back = (queries, key_rows, values, segments, log_total, grad_context)
-    found, sums_rows = None, 0.0
+    found, sums_rows, row_sums = None, 0.0, [mixed_rows]
     for row in range(rows):
         if row == 1:
             sent = inner_sum.hold(found[1]).corner() + list(outer_sum.hold(found[1]).far())
             found = after(found, sent)
         found = attend_back(*back, row, found or ())
         sums_rows += found[3]
+        row_sums.append(found[4])
         found = found[:3]
     grad_queries, grad_keys, grad_values = found
     sent = inner_sum.hold(grad_queries).near()
@@ -1248,22 +1299,22 @@
     stream_sum = Reduction(net, me, *stream_halves)
     grad_mixed = after(grad_mixed, stream_halves)
     back = (flow, grad_mixed, grad_queries, grad_keys, grad_values)
-    grad_stream, part = stream_back(net, me, *back, 0, row_length)
-    grad_temb = [part]
+    grad_stream, grad_temb = stream_back(net, me, *back, 0, row_length, sums=row_sums)
+    ends = jnp.concatenate([feats.astype(F32), grad_temb[:rows]], axis=1)[None]
+    sources, ends = net.gather_round([0], ends, net.masks(net.core))
+    sent = inner_sum.hold(grad_temb).far()
+    sent = list(sent) + stream_sum.hold((grad_temb, sent)).corner()
+    ends, grad_stream = after((ends, grad_stream), sent)
     for row in range(1, rows):
-        if row == 1:
-            sent = stream_sum.hold(part).corner() + list(inner_sum.hold(part).far())
-            grad_stream = after(grad_stream, sent)
-        grad_stream, part = stream_back(net, me, *back, row, row_length, grad_stream)
-        grad_temb.append(part)
-    sent = stream_sum.hold(part).near()
-    ends = jnp.concatenate([feats.astype(F32), jnp.concatenate(grad_temb)], axis=1)[None]
+        (grad_stream,) = stream_back(net, me, *back, row, row_length, grad_stream)
+    sent = stream_sum.hold(grad_stream).near()
     output_weight_grad, inner_weight_grad = inner_sum.hold(sent).end([1, hidden // model_width], r)
-    ends = after(ends, output_weight_grad)
-    sources, ends = net.gather_round([0], ends, net.masks(net.core))
+    ends = after(ends, (sent, output_weight_grad))
     sources, ends = net.gather_round(sources, ends, net.inner_masks())
-    stream_sum.far()
-    sources, ends = net.gather_round(sources, ends, net.masks(net.outer))
+    stream_sum.hold(ends).far()
+    sources, ends = net.gather_round(
+        sources, after(ends, stream_sum.received()), net.masks(net.outer)
+    )
     ends = in_order(net, me, sources, ends).reshape(n * rows, 2 * model_width)
     query_weight_grad, key_weight_grad, value_weight_grad, vector_sums = stream_ends(
         stream_sum, r

time: 545 us -> 494 us (0.906)
  the two profiles are of different devices: /device:TPU:20 before, /device:TPU:0 now
where the time goes in v3:
time: 494 us; the launch traced here: 486 us
  Pallas kernels  275 us (56%)
  waiting for transfers between devices  93 us (19%)
  starting transfers between devices  89 us (18%)
  local copies, waits for them, and re-layouts  15.5 us (3%)
  other arithmetic  10.8 us (2%)
    pallas_call x13, Pallas kernels, call(): pl.pallas_call(run, grid=grid, in_specs=[spec for _, spec in ins] + [ANY_...  226 us
    ppermute x67, waiting for transfers between devices, swap(): return lax.ppermute(array, 'fsdp', [(i, i ^ mask) for i in range(self.n)])  93 us
    ppermute x67, starting transfers between devices, swap(): return lax.ppermute(array, 'fsdp', [(i, i ^ mask) for i in range(self.n)])  89 us
    pallas_call x12, Pallas kernels, sum_call(): pl.pallas_call(body or functools.partial(sum_body, groups), grid_spec=gri...  42.1 us
  transfers between devices with their start and end apart: 67, of which 21 were waited for; matrix products, arithmetic and copies ran while one was open for 3% of the time, Pallas kernels for 46%

profile of v3, /device:TPU:0, one launch (start us, length us, event | category | flops | bytes accessed | tf_op | source)
XLA Modules:
  0.0 485.9 jit_solution(8967683948040429205)
XLA Ops:
  10.7 13.7 %collective-permute-done = bf16[144,1024]{1,0:T(8,128)(2,1)S(1)} collective-permute-done((bf16[144,1024]{1,0:T(8,128)(2,1)}, bf16[144,1024]{1,0:T(8,128)(2,1)S(1)}, u32[]{:S(2)}, u32[]{:S(2)}) %collective-permute-start) | collective-permute-done | bytes 294944 | tf_op jit(solution)/shard_map/ppermute | solution.py:103
  24.4 5.8 %collective-permute-done.2 = bf16[144,1024]{1,0:T(8,128)(2,1)S(1)} collective-permute-done((bf16[144,1024]{1,0:T(8,128)(2,1)}, bf16[144,1024]{1,0:T(8,128)(2,1)S(1)}, u32[]{:S(2)}, u32[]{:S(2)}) %collective-permute-start.2) | collective-permute-done | bytes 294944 | tf_op jit(solution)/shard_map/ppermute | solution.py:103
  34.5 7.8 %collective-permute-start.3 = (bf16[160,1024]{1,0:T(8,128)(2,1)S(1)}, bf16[160,1024]{1,0:T(8,128)(2,1)}, u32[]{:S(2)}, u32[]{:S(2)}) collective-permute-start(bf16[160,1024]{1,0:T(8,128)(2,1)S(1)} %slice_dynamic-update-slice_fusion), channel_id=1, source_target_pairs={{0,16},{1,17},{2,18},{3,19},{4,20},{5,21},{6,22},{7,23},{8,24},{9,... | collective-permute-start | bytes 983048 | tf_op jit(solution)/shard_map/ppermute | solution.py:103
  43.9 14.4 %collective-permute-done.6.low_in.refs_3_ = bf16[4,144,1024]{2,1,0:T(8,128)(2,1)S(1)} collective-permute-done((bf16[4,144,1024]{2,1,0:T(8,128)(2,1)S(1)}, bf16[4,144,1024]{2,1,0:T(8,128)(2,1)S(1)}, u32[]{:S(2)}, u32[]{:S(2)}) %collective-permute-start.6) | collective-permute-done | bytes 1179680 | tf_op jit(solution)/shard_map/ppermute | solution.py:103
  68.4 7.7 %collective-permute-done.8.refs_7_ = bf16[2,144,1024]{2,1,0:T(8,128)(2,1)} collective-permute-done((bf16[2,144,1024]{2,1,0:T(8,128)(2,1)}, bf16[2,144,1024]{2,1,0:T(8,128)(2,1)}, u32[]{:S(2)}, u32[]{:S(2)}) %collective-permute-start.8) | collective-permute-done | bytes 589856 | tf_op jit(solution)/shard_map/ppermute | solution.py:103
  81.7 10.0 %collective-permute-start.15 = (bf16[128,1024]{1,0:T(8,128)(2,1)}, bf16[128,1024]{1,0:T(8,128)(2,1)}, u32[]{:S(2)}, u32[]{:S(2)}) collective-permute-start(bf16[128,1024]{1,0:T(8,128)(2,1)} %param.30), channel_id=1, source_target_pairs={{0,16},{1,17},{2,18},{3,19},{4,20},{5,21},{6,22},{7,23},{8,24},{9,... | collective-permute-start | bytes 786440 | tf_op jit(solution)/shard_map/ppermute | solution.py:103
  93.3 14.5 %project.1 = (f32[2,1024]{1,0:T(2,128)}, f32[16,1024]{1,0:T(8,128)}, bf16[1024,1024]{1,0:T(8,128)(2,1)}, bf16[1024,1024]{1,0:T(8,128)(2,1)}, bf16[1024,1024]{1,0:T(8,128)(2,1)}, /*index=5*/bf16[1024,1024]{1,0:T(8,128)(2,1)}) custom-call(s32[1]{0:T(128)} %bitcast.refs_0_.me_ref, bf16[4,144,1024]{2,1,0:T(8,128)(2,1)} %copy-done.3, ...), custom_call_target="tpu_custom_call" | custom-call | flops 280000004096 | bytes 700000000 | tf_op jit(solution)/shard_map/project/pallas_call | solution.py:318
  118.8 19.9 %attend.1 = (bf16[1024,1024]{1,0:T(8,128)(2,1)}, f32[2,4,4,512]{3,2,1,0:T(4,128)}) custom-call(s32[2,512,1]{2,1,0:T(8,128)} %broadcast_in_dim_reshape.6.refs_0_, s32[2,1,512]{2,1,0:T(1,128)} %refs_1_.5, bf16[1024,1024]{1,0:T(8,128)(2,1)} %get-tuple-element.208.refs_2_, bf16[1024,1024]{1,0:T(8,128)(2,1)} %get-tuple-element.209.refs_3_, ...), custom_call_target="tpu_custom_call" | custom-call | flops 480000016384 | bytes 1200000000 | tf_op jit(solution)/shard_map/attend/pallas_call | solution.py:318
  139.4 12.6 %collective-permute-done.20.high_in.refs_2_ = bf16[4,128,1024]{2,1,0:T(8,128)(2,1)} collective-permute-done((bf16[4,128,1024]{2,1,0:T(8,128)(2,1)}, bf16[4,128,1024]{2,1,0:T(8,128)(2,1)}, u32[]{:S(2)}, u32[]{:S(2)}) %collective-permute-start.20) | collective-permute-done | bytes 1048608 | tf_op jit(solution)/shard_map/ppermute | solution.py:103
  161.4 29.1 %ffn_in.1 = (bf16[1024,1024]{1,0:T(8,128)(2,1)}, f32[1024,1024]{1,0:T(8,128)}, f32[1024,1]{1,0:T(8,128)}, bf16[1024,4096]{1,0:T(8,128)(2,1)}, bf16[1024,4096]{1,0:T(8,128)(2,1)}) custom-call(s32[1]{0:T(128)} %bitcast.refs_0_.me_ref, bf16[4,160,1024]{2,1,0:T(8,128)(2,1)} %pad_maximum_fusion.refs_1_.refs_11_, ...), custom_call_target="tpu_custom_call" | custom-call | flops 599999971328 | bytes 1500000000 | tf_op jit(solution)/shard_map/ffn_in/pallas_call | solution.py:318
  194.2 20.9 %ffn_out.1 = (bf16[1024,1024]{1,0:T(8,128)(2,1)}, f32[1024,1024]{1,0:T(8,128)}, bf16[1024,1024]{1,0:T(8,128)(2,1)}, f32[8,1024]{1,0:T(8,128)}) custom-call(s32[1]{0:T(128)} %bitcast.refs_0_.me_ref, bf16[4,128,1024]{2,1,0:T(8,128)(2,1)} %pad_maximum_fusion.2.refs_1_, bf16[4,128,1024]{2,1,0:T(8,128)(2,1)} %collective-permute-done.20.high_in.refs_2_, ...), custom_call_target="tpu_custom_call" | custom-call | flops 399999991808 | bytes 1000000000 | tf_op jit(solution)/shard_map/ffn_out/pallas_call | solution.py:318
  215.1 13.1 %product.1 = (bf16[16,128,1024]{2,1,0:T(8,128)(2,1)}, bf16[16,128,1024]{2,1,0:T(8,128)(2,1)}) custom-call(s32[1]{0:T(128)} %bitcast.refs_0_.me_ref, bf16[1024,4096]{1,0:T(8,128)(2,1)} %get-tuple-element.238.refs_11_.refs_1_, bf16[1024,1024]{1,0:T(8,128)(2,1)} %get-tuple-element.242.refs_2_.refs_22_), custom_call_target="tpu_custom_call" | custom-call | flops 299999985664 | bytes 750000000 | tf_op jit(solution)/shard_map/product/pallas_call | solution.py:318
  228.4 37.5 %ffn_back.1 = (bf16[1024,4096]{1,0:T(8,128)(2,1)}, f32[1024,1024]{1,0:T(8,128)}, bf16[1024,1024]{1,0:T(8,128)(2,1)}, bf16[1024,1024]{1,0:T(8,128)(2,1)}, f32[1,4...) custom-call(s32[1]{0:T(128)} %bitcast.refs_0_.me_ref, bf16[4,128,1024]{2,1,0:T(8,128)(2,1)} %pad_maximum_fusion.2.refs_1_, ...), custom_call_target="tpu_custom_call" | custom-call | flops 760000020480 | bytes 1900000000 | tf_op jit(solution)/shard_map/ffn_back/pallas_call | solution.py:318
  271.7 17.6 %inner_product.1 = (bf16[16,160,1024]{2,1,0:T(8,128)(2,1)}, bf16[16,160,1024]{2,1,0:T(8,128)(2,1)}) custom-call(s32[1]{0:T(128)} %bitcast.refs_0_.me_ref, bf16[1024,1024]{1,0:T(8,128)(2,1)} %get-tuple-element.232.refs_11_.refs_1_, bf16[1024,1024]{1,0:T(8,128)(2,1)} %get-tuple-element.252.refs_2_, bf16[1024,1024]{1,0:T(8,128)(2,1)} %get-tuple-element.258.refs_3_, ...), custom_call_target="tpu_custom_call" | custom-call | flops 359999995904 | bytes 900000000 | tf_op jit(solution)/shard_map/inner_product/pallas_call | solution.py:318
  296.0 18.8 %attend_back.2 = (bf16[1024,1024]{1,0:T(8,128)(2,1)}, bf16[1024,1024]{1,0:T(8,128)(2,1)}, bf16[1024,1024]{1,0:T(8,128)(2,1)}, f32[8,1024]{1,0:T(8,128)}, f32[8,1024]{1,0:T(8,128)}) custom-call(s32[2,512,1]{2,1,0:T(8,128)} %broadcast_in_dim_reshape.6.refs_0_, s32[2,1,512]{2,1,0:T(1,128)} %refs_1_.5, bf16[1024,1024]{1,0:T(8,128)(2,1)} %get-tuple-element.208.refs_2_, ...), custom_call_target="tpu_custom_call" | custom-call | flops 380000010240 | bytes 950000000 | tf_op jit(solution)/shard_map/attend_back/pallas_call | solution.py:318
  324.6 9.3 %collective-permute-start.44 = (bf16[1,128,1024]{2,1,0:T(8,128)(2,1)}, bf16[1,128,1024]{2,1,0:T(8,128)(2,1)}, u32[]{:S(2)}, u32[]{:S(2)}) collective-permute-start(bf16[1,128,1024]{2,1,0:T(8,128)(2,1)} %get-tuple-element.281), channel_id=1, source_target_pairs={{0,16},{1,17},{2,18},{3,19},{4,20},{5,21},{6,22},{7,23},{8,24},{9,... | collective-permute-start | bytes 786440 | tf_op jit(solution)/shard_map/ppermute | solution.py:103
  340.4 18.6 %attend_back.3 = (bf16[1024,1024]{1,0:T(8,128)(2,1)}, bf16[1024,1024]{1,0:T(8,128)(2,1)}, bf16[1024,1024]{1,0:T(8,128)(2,1)}, f32[8,1024]{1,0:T(8,128)}, f32[8,1024]{1,0:T(8,128)}) custom-call(s32[2,512,1]{2,1,0:T(8,128)} %broadcast_in_dim_reshape.6.refs_0_, s32[2,1,512]{2,1,0:T(1,128)} %refs_1_.5, ...), custom_call_target="tpu_custom_call", output_to_operand_aliasing={{0}: (7, {}), {1}: (8, {}), {2}: (9, {})} | custom-call | flops 380000010240 | bytes 950000000 | tf_op jit(solution)/shard_map/attend_back/pallas_call | solution.py:318
  361.9 5.0 %near_sum.4 = (bf16[4,160,1024]{2,1,0:T(8,128)(2,1)}, bf16[4,160,1024]{2,1,0:T(8,128)(2,1)}) custom-call(s32[1]{0:T(128)} %bitcast.refs_0_.me_ref, bf16[16,160,1024]{2,1,0:T(8,128)(2,1)} %get-tuple-element.336.refs_0_.refs_2_.refs_4_.refs_8_, bf16[16,160,1024]{2,1,0:T(8,128)(2,1)} %collective-permute-done.39.refs_1_.refs_3_.refs_5_.refs_9_, ...), custom_call_target="tpu_custom_call" | custom-call | flops 200000000 | bytes 500000 | tf_op jit(solution)/shard_map/near_sum/pallas_call | solution.py:363
  369.5 11.8 %triple_product.1 = (bf16[16,104,1024]{2,1,0:T(8,128)(2,1)}, bf16[16,104,1024]{2,1,0:T(8,128)(2,1)}) custom-call(s32[1]{0:T(128)} %bitcast.refs_0_.me_ref, bf16[16,16,1024]{2,1,0:T(8,128)(2,1)} %bitcast.62, bf16[1024,1024]{1,0:T(8,128)(2,1)} %get-tuple-element.306.refs_2_, bf16[1024,1024]{1,0:T(8,128)(2,1)} %get-tuple-element.291.refs_3_.refs_12_, ...), custom_call_target="tpu_custom_call" | custom-call | flops 260000006144 | bytes 650000000 | tf_op jit(solution)/shard_map/triple_product/pallas_call | solution.py:318
  381.3 12.1 %stream_back.2 = (f32[1024,1024]{1,0:T(8,128)}, f32[8,1024]{1,0:T(8,128)}) custom-call(s32[1]{0:T(128)} %bitcast.refs_0_.me_ref, bf16[4,144,1024]{2,1,0:T(8,128)(2,1)} %copy-done.3, bf16[4,144,1024]{2,1,0:T(8,128)(2,1)} %copy-done.5, bf16[4,144,1024]{2,1,0:T(8,128)(2,1)} %copy-done.4, bf16[4,144,1024]{2,1,0:T(8,128)(2,1)} %copy-done.24, ...), custom_call_target="tpu_custom_call" | custom-call | flops 199999995904 | bytes 500000000 | tf_op jit(solution)/shard_map/stream_back/pallas_call | solution.py:318
  410.0 10.0 %stream_back.3 = f32[1024,1024]{1,0:T(8,128)} custom-call(s32[1]{0:T(128)} %bitcast.refs_0_.me_ref, bf16[4,144,1024]{2,1,0:T(8,128)(2,1)} %copy-done.3, bf16[4,144,1024]{2,1,0:T(8,128)(2,1)} %copy-done.5, bf16[4,144,1024]{2,1,0:T(8,128)(2,1)} %copy-done.4, bf16[4,144,1024]{2,1,0:T(8,128)(2,1)} %copy-done.24, ...), custom_call_target="tpu_custom_call", output_to_operand_aliasing={{}: (15, {})} | custom-call | flops 199999995904 | bytes 500000000 | tf_op jit(solution)/shard_map/stream_back/pallas_call | solution.py:318
  434.5 10.7 %collective-permute-done.58 = f32[2,2,2048]{2,1,0:T(2,128)S(1)} collective-permute-done((f32[2,2,2048]{2,1,0:T(2,128)S(1)}, f32[2,2,2048]{2,1,0:T(2,128)S(1)}, u32[]{:S(2)}, u32[]{:S(2)}) %collective-permute-start.58) | collective-permute-done | bytes 32800 | tf_op jit(solution)/shard_map/ppermute | solution.py:103
  456.5 5.8 %collective-permute-done.63.refs_6_ = bf16[1,104,1024]{2,1,0:T(8,128)(2,1)S(1)} collective-permute-done((bf16[1,104,1024]{2,1,0:T(8,128)(2,1)}, bf16[1,104,1024]{2,1,0:T(8,128)(2,1)S(1)}, u32[]{:S(2)}, u32[]{:S(2)}) %collective-permute-start.63) | collective-permute-done | bytes 213024 | tf_op jit(solution)/shard_map/ppermute | solution.py:103
  462.3 8.1 %collective-permute-start.64 = (f32[8,2,2048]{2,1,0:T(2,128)S(1)}, f32[8,2,2048]{2,1,0:T(2,128)S(1)}, u32[]{:S(2)}, u32[]{:S(2)}) collective-permute-start(f32[8,2,2048]{2,1,0:T(2,128)S(1)} %constant_dynamic-update-slice_fusion.1), channel_id=1, source_target_pairs={{0,16},{1,17},{2,18},{3,19},{4,20},{5,21},{6,22},{7,23},{8,24},{9,... | collective-permute-start | bytes 393224 | tf_op jit(solution)/shard_map/ppermute | solution.py:103
  (242 shorter events, 149.2 us)
Async XLA Ops:
  31.4 26.9 %collective-permute-start.6 = (bf16[4,144,1024]{2,1,0:T(8,128)(2,1)S(1)}, bf16[4,144,1024]{2,1,0:T(8,128)(2,1)S(1)}, u32[]{:S(2)}, u32[]{:S(2)}) collective-permute-start(bf16[4,144,1024]{2,1,0:T(8,128)(2,1)S(1)} %pad_maximum_fusion.1.refs_1_), channel_id=1, source_target_pairs={{0,4},{1,5},{2,6},{3,7},{4,0},{5,1},{6,2},{7,3},{8,12},{9,13},{10,... | collective-permute-start | bytes 3538952 | tf_op jit(solution)/shard_map/ppermute | solution.py:103
  32.9 26.5 %collective-permute-start.7 = (bf16[4,144,1024]{2,1,0:T(8,128)(2,1)S(1)}, bf16[4,144,1024]{2,1,0:T(8,128)(2,1)S(1)}, u32[]{:S(2)}, u32[]{:S(2)}) collective-permute-start(bf16[4,144,1024]{2,1,0:T(8,128)(2,1)S(1)} %pad_maximum_fusion.1.refs_1_), channel_id=1, source_target_pairs={{0,2},{1,3},{2,0},{3,1},{4,6},{5,7},{6,4},{7,5},{8,10},{9,11},{10,... | collective-permute-start | bytes 3538952 | tf_op jit(solution)/shard_map/ppermute | solution.py:103
  34.5 30.9 %collective-permute-start.3 = (bf16[160,1024]{1,0:T(8,128)(2,1)S(1)}, bf16[160,1024]{1,0:T(8,128)(2,1)}, u32[]{:S(2)}, u32[]{:S(2)}) collective-permute-start(bf16[160,1024]{1,0:T(8,128)(2,1)S(1)} %slice_dynamic-update-slice_fusion), channel_id=1, source_target_pairs={{0,16},{1,17},{2,18},{3,19},{4,20},{5,21},{6,22},{7,23},{8,24},{9,... | collective-permute-start | bytes 983048 | tf_op jit(solution)/shard_map/ppermute | solution.py:103
  79.6 33.0 %collective-permute-start.18 = (bf16[4,160,1024]{2,1,0:T(8,128)(2,1)}, bf16[4,160,1024]{2,1,0:T(8,128)(2,1)}, u32[]{:S(2)}, u32[]{:S(2)}) collective-permute-start(bf16[4,160,1024]{2,1,0:T(8,128)(2,1)} %pad_maximum_fusion.refs_1_.refs_11_), channel_id=1, source_target_pairs={{0,2},{1,3},{2,0},{3,1},{4,6},{5,7},{6,4},{7,5},{8,10},{9,11},{10,... | collective-permute-start | bytes 3932168 | tf_op jit(solution)/shard_map/ppermute | solution.py:103
  80.2 32.4 %collective-permute-start.19 = (bf16[4,160,1024]{2,1,0:T(8,128)(2,1)}, bf16[4,160,1024]{2,1,0:T(8,128)(2,1)}, u32[]{:S(2)}, u32[]{:S(2)}) collective-permute-start(bf16[4,160,1024]{2,1,0:T(8,128)(2,1)} %pad_maximum_fusion.refs_1_.refs_11_), channel_id=1, source_target_pairs={{0,4},{1,5},{2,6},{3,7},{4,0},{5,1},{6,2},{7,3},{8,12},{9,13},{10,... | collective-permute-start | bytes 3932168 | tf_op jit(solution)/shard_map/ppermute | solution.py:103
  81.7 28.0 %collective-permute-start.15 = (bf16[128,1024]{1,0:T(8,128)(2,1)}, bf16[128,1024]{1,0:T(8,128)(2,1)}, u32[]{:S(2)}, u32[]{:S(2)}) collective-permute-start(bf16[128,1024]{1,0:T(8,128)(2,1)} %param.30), channel_id=1, source_target_pairs={{0,16},{1,17},{2,18},{3,19},{4,20},{5,21},{6,22},{7,23},{8,24},{9,... | collective-permute-start | bytes 786440 | tf_op jit(solution)/shard_map/ppermute | solution.py:103
  116.8 35.2 %collective-permute-start.20 = (bf16[4,128,1024]{2,1,0:T(8,128)(2,1)}, bf16[4,128,1024]{2,1,0:T(8,128)(2,1)}, u32[]{:S(2)}, u32[]{:S(2)}) collective-permute-start(bf16[4,128,1024]{2,1,0:T(8,128)(2,1)} %pad_maximum_fusion.2.refs_1_), channel_id=1, source_target_pairs={{0,2},{1,3},{2,0},{3,1},{4,6},{5,7},{6,4},{7,5},{8,10},{9,11},{10,... | collective-permute-start | bytes 3145736 | tf_op jit(solution)/shard_map/ppermute | solution.py:103
  117.7 35.5 %collective-permute-start.21 = (bf16[4,128,1024]{2,1,0:T(8,128)(2,1)}, bf16[4,128,1024]{2,1,0:T(8,128)(2,1)}, u32[]{:S(2)}, u32[]{:S(2)}) collective-permute-start(bf16[4,128,1024]{2,1,0:T(8,128)(2,1)} %pad_maximum_fusion.2.refs_1_), channel_id=1, source_target_pairs={{0,4},{1,5},{2,6},{3,7},{4,0},{5,1},{6,2},{7,3},{8,12},{9,13},{10,... | collective-permute-start | bytes 3145736 | tf_op jit(solution)/shard_map/ppermute | solution.py:103
  154.3 37.2 %collective-permute-start.29 = (bf16[4,128,1024]{2,1,0:T(8,128)(2,1)}, bf16[4,128,1024]{2,1,0:T(8,128)(2,1)}, u32[]{:S(2)}, u32[]{:S(2)}) collective-permute-start(bf16[4,128,1024]{2,1,0:T(8,128)(2,1)} %pad_maximum_fusion.2.refs_1_), channel_id=1, source_target_pairs={{0,1},{1,0},{2,3},{3,2},{4,5},{5,4},{6,7},{7,6},{8,9},{9,8},{10,11... | collective-permute-start | bytes 3145736 | tf_op jit(solution)/shard_map/ppermute | solution.py:103
  156.4 37.0 %collective-permute-start.30 = (bf16[4,128,1024]{2,1,0:T(8,128)(2,1)}, bf16[4,128,1024]{2,1,0:T(8,128)(2,1)}, u32[]{:S(2)}, u32[]{:S(2)}) collective-permute-start(bf16[4,128,1024]{2,1,0:T(8,128)(2,1)} %collective-permute-done.20.high_in.refs_2_), channel_id=1, source_target_pairs={{0,1},{1,0},{2,3},{3,2},{4,5},{5,4},{6,7},{7,6},{8,9},{9,8},{10,11... | collective-permute-start | bytes 3145736 | tf_op jit(solution)/shard_map/ppermute | solution.py:103
  159.2 34.3 %collective-permute-start.31 = (bf16[4,128,1024]{2,1,0:T(8,128)(2,1)}, bf16[4,128,1024]{2,1,0:T(8,128)(2,1)}, u32[]{:S(2)}, u32[]{:S(2)}) collective-permute-start(bf16[4,128,1024]{2,1,0:T(8,128)(2,1)} %collective-permute-done.21.low_in.refs_3_), channel_id=1, source_target_pairs={{0,1},{1,0},{2,3},{3,2},{4,5},{5,4},{6,7},{7,6},{8,9},{9,8},{10,11... | collective-permute-start | bytes 3145736 | tf_op jit(solution)/shard_map/ppermute | solution.py:103
  159.3 31.2 %collective-permute-start.32 = (bf16[2,128,1024]{2,1,0:T(8,128)(2,1)}, bf16[2,128,1024]{2,1,0:T(8,128)(2,1)}, u32[]{:S(2)}, u32[]{:S(2)}) collective-permute-start(bf16[2,128,1024]{2,1,0:T(8,128)(2,1)} %get-tuple-element.219), channel_id=1, source_target_pairs={{0,2},{1,3},{2,0},{3,1},{4,6},{5,7},{6,4},{7,5},{8,10},{9,11},{10,... | collective-permute-start | bytes 1572872 | tf_op jit(solution)/shard_map/ppermute | solution.py:103
  160.5 30.0 %collective-permute-start.33 = (bf16[2,128,1024]{2,1,0:T(8,128)(2,1)}, bf16[2,128,1024]{2,1,0:T(8,128)(2,1)}, u32[]{:S(2)}, u32[]{:S(2)}) collective-permute-start(bf16[2,128,1024]{2,1,0:T(8,128)(2,1)} %get-tuple-element.220), channel_id=1, source_target_pairs={{0,4},{1,5},{2,6},{3,7},{4,0},{5,1},{6,2},{7,3},{8,12},{9,13},{10,... | collective-permute-start | bytes 1572872 | tf_op jit(solution)/shard_map/ppermute | solution.py:103
  228.2 39.1 %collective-permute-start.36 = (bf16[16,128,1024]{2,1,0:T(8,128)(2,1)}, bf16[16,128,1024]{2,1,0:T(8,128)(2,1)}, u32[]{:S(2)}, u32[]{:S(2)}) collective-permute-start(bf16[16,128,1024]{2,1,0:T(8,128)(2,1)} %get-tuple-element.245), channel_id=1, source_target_pairs={{0,1},{1,0},{2,3},{3,2},{4,5},{5,4},{6,7},{7,6},{8,9},{9,8},{10,11... | collective-permute-start | bytes 12582920 | tf_op jit(solution)/shard_map/ppermute | solution.py:103
  289.3 46.1 %collective-permute-start.39 = (bf16[16,160,1024]{2,1,0:T(8,128)(2,1)}, bf16[16,160,1024]{2,1,0:T(8,128)(2,1)}, u32[]{:S(2)}, u32[]{:S(2)}) collective-permute-start(bf16[16,160,1024]{2,1,0:T(8,128)(2,1)} %get-tuple-element.261), channel_id=1, source_target_pairs={{0,1},{1,0},{2,3},{3,2},{4,5},{5,4},{6,7},{7,6},{8,9},{9,8},{10,11... | collective-permute-start | bytes 15728648 | tf_op jit(solution)/shard_map/ppermute | solution.py:103
  293.9 25.9 %collective-permute-start.40 = (bf16[4,128,1024]{2,1,0:T(8,128)(2,1)}, bf16[4,128,1024]{2,1,0:T(8,128)(2,1)}, u32[]{:S(2)}, u32[]{:S(2)}) collective-permute-start(bf16[4,128,1024]{2,1,0:T(8,128)(2,1)} %get-tuple-element.266), channel_id=1, source_target_pairs={{0,2},{1,3},{2,0},{3,1},{4,6},{5,7},{6,4},{7,5},{8,10},{9,11},{10,... | collective-permute-start | bytes 3145736 | tf_op jit(solution)/shard_map/ppermute | solution.py:103
  295.1 25.6 %collective-permute-start.41 = (bf16[4,128,1024]{2,1,0:T(8,128)(2,1)}, bf16[4,128,1024]{2,1,0:T(8,128)(2,1)}, u32[]{:S(2)}, u32[]{:S(2)}) collective-permute-start(bf16[4,128,1024]{2,1,0:T(8,128)(2,1)} %get-tuple-element.267), channel_id=1, source_target_pairs={{0,4},{1,5},{2,6},{3,7},{4,0},{5,1},{6,2},{7,3},{8,12},{9,13},{10,... | collective-permute-start | bytes 3145736 | tf_op jit(solution)/shard_map/ppermute | solution.py:103
  324.6 34.4 %collective-permute-start.44 = (bf16[1,128,1024]{2,1,0:T(8,128)(2,1)}, bf16[1,128,1024]{2,1,0:T(8,128)(2,1)}, u32[]{:S(2)}, u32[]{:S(2)}) collective-permute-start(bf16[1,128,1024]{2,1,0:T(8,128)(2,1)} %get-tuple-element.281), channel_id=1, source_target_pairs={{0,16},{1,17},{2,18},{3,19},{4,20},{5,21},{6,22},{7,23},{8,24},{9,... | collective-permute-start | bytes 786440 | tf_op jit(solution)/shard_map/ppermute | solution.py:103
  333.9 25.1 %collective-permute-start.45 = (bf16[1,128,1024]{2,1,0:T(8,128)(2,1)}, bf16[1,128,1024]{2,1,0:T(8,128)(2,1)}, u32[]{:S(2)}, u32[]{:S(2)}) collective-permute-start(bf16[1,128,1024]{2,1,0:T(8,128)(2,1)} %get-tuple-element.282), channel_id=1, source_target_pairs={{0,8},{1,9},{2,10},{3,11},{4,12},{5,13},{6,14},{7,15},{8,0},{9,1},... | collective-permute-start | bytes 786440 | tf_op jit(solution)/shard_map/ppermute | solution.py:103
  333.9 25.1 %collective-permute-start.46 = (bf16[1,128,1024]{2,1,0:T(8,128)(2,1)}, bf16[1,128,1024]{2,1,0:T(8,128)(2,1)}, u32[]{:S(2)}, u32[]{:S(2)}) collective-permute-start(bf16[1,128,1024]{2,1,0:T(8,128)(2,1)} %get-tuple-element.283), channel_id=1, source_target_pairs={{0,24},{1,25},{2,26},{3,27},{4,28},{5,29},{6,30},{7,31},{8,16},{9,... | collective-permute-start | bytes 786440 | tf_op jit(solution)/shard_map/ppermute | solution.py:103
  366.9 29.7 %collective-permute-start.48 = (bf16[4,160,1024]{2,1,0:T(8,128)(2,1)}, bf16[4,160,1024]{2,1,0:T(8,128)(2,1)}, u32[]{:S(2)}, u32[]{:S(2)}) collective-permute-start(bf16[4,160,1024]{2,1,0:T(8,128)(2,1)} %get-tuple-element.296), channel_id=1, source_target_pairs={{0,2},{1,3},{2,0},{3,1},{4,6},{5,7},{6,4},{7,5},{8,10},{9,11},{10,... | collective-permute-start | bytes 3932168 | tf_op jit(solution)/shard_map/ppermute | solution.py:103
  368.1 29.0 %collective-permute-start.49 = (bf16[4,160,1024]{2,1,0:T(8,128)(2,1)}, bf16[4,160,1024]{2,1,0:T(8,128)(2,1)}, u32[]{:S(2)}, u32[]{:S(2)}) collective-permute-start(bf16[4,160,1024]{2,1,0:T(8,128)(2,1)} %get-tuple-element.297), channel_id=1, source_target_pairs={{0,4},{1,5},{2,6},{3,7},{4,0},{5,1},{6,2},{7,3},{8,12},{9,13},{10,... | collective-permute-start | bytes 3932168 | tf_op jit(solution)/shard_map/ppermute | solution.py:103
  381.3 24.5 %collective-permute-start.50 = (bf16[16,104,1024]{2,1,0:T(8,128)(2,1)}, bf16[16,104,1024]{2,1,0:T(8,128)(2,1)}, u32[]{:S(2)}, u32[]{:S(2)}) collective-permute-start(bf16[16,104,1024]{2,1,0:T(8,128)(2,1)} %get-tuple-element.310), channel_id=1, source_target_pairs={{0,1},{1,0},{2,3},{3,2},{4,5},{5,4},{6,7},{7,6},{8,9},{9,8},{10,11... | collective-permute-start | bytes 10223624 | tf_op jit(solution)/shard_map/ppermute | solution.py:103
  401.3 25.3 %collective-permute-start.55 = (bf16[1,160,1024]{2,1,0:T(8,128)(2,1)}, bf16[1,160,1024]{2,1,0:T(8,128)(2,1)}, u32[]{:S(2)}, u32[]{:S(2)}) collective-permute-start(bf16[1,160,1024]{2,1,0:T(8,128)(2,1)} %get-tuple-element.321), channel_id=1, source_target_pairs={{0,16},{1,17},{2,18},{3,19},{4,20},{5,21},{6,22},{7,23},{8,24},{9,... | collective-permute-start | bytes 983048 | tf_op jit(solution)/shard_map/ppermute | solution.py:103
  (74 other events, 953.0 us)

commit v4 on v3

--- a/solution.py
+++ b/solution.py
@@ -39,6 +39,15 @@
     freqs = jnp.exp(-math.log(10000.0) * jnp.arange(half_width, dtype=F32) / half_width)
     angles = step_ids.astype(F32)[..., None] * freqs
     return jnp.concatenate([jnp.sin(angles), jnp.cos(angles)], axis=-1)
+
+
+def own_features(step_ids, first, count):
+    half_width = D // 2
+    columns = first + jnp.arange(count, dtype=jnp.int32)
+    places = (columns % half_width).astype(F32)
+    freqs = jnp.exp(-math.log(10000.0) * places / half_width)
+    angles = step_ids[:, None] * freqs
+    return jnp.where(columns < half_width, jnp.sin(angles), jnp.cos(angles))
 
 
 def normalize(values_in):
@@ -70,7 +79,7 @@
         ],
         out_specs=[pl.BlockSpec(block, lambda i: (i, 0, 0))] * 2,
         out_shape=[jax.ShapeDtypeStruct((half,) + low_of.shape[1:], low_of.dtype)] * 2,
-        compiler_params=pltpu.CompilerParams(vmem_limit_bytes=60 << 20),
+        compiler_params=pltpu.CompilerParams(vmem_limit_bytes=16 << 20),
         cost_estimate=pl.CostEstimate(flops=1000, bytes_accessed=1000, transcendentals=0),
         name="halves",
     )(low_of, high_of)
@@ -458,15 +467,14 @@
         if not self.plain:
             self.state, sent = net.scatter_step(self.state, net.outer, self.me)
             return sent
-        parts = 4
-        lanes = self.columns // parts
-        step_block = ((1, self.rows, lanes), lambda i, at: (at, 0, i))
+        parts = 2 if self.rows % 32 == 0 else 1
+        step_block = ((1, self.rows // parts, self.columns), lambda i, at: (at, i, 0))
         masks = net.masks(net.outer)
         ins, groups = [], []
         for mask in masks:
             groups.append([(len(ins) + j, (None, None)) for j in range(4)])
             ins += self.sources(mask >> 3, step_block)
-        out = ((1, self.rows, self.columns), BF16, step_block[0], lambda i, me: (0, 0, i))
+        out = ((1, self.rows, self.columns), BF16, step_block[0], lambda i, me: (0, i, 0))
         sent = sum_call(self.me, "far_sum", parts, ins, groups, [out] * len(masks))
         self.terms += [net.swap(part, mask) for part, mask in zip(sent, masks)]
         return sent
@@ -512,7 +520,7 @@
         return sum_call(self.me, "end_sum", start, ins, None, outs, body, 4)
 
 
-def pack_body(step, me_ref, lines_ref, inner_ref, *refs):
+def pack_body(sizes, me_ref, small_ref, *refs):
     shards, out_ref = refs[:-1], refs[-1]
     start = 0
     for ref in shards:
@@ -520,29 +528,45 @@
         start += ref.shape[0]
     me, width = me_ref[0], out_ref.shape[1]
 
-    def spread(ref, offset):
-        count = ref.shape[1]
-        lanes = lax.broadcasted_iota(jnp.int32, (count, width), 1)
-        spots = lax.broadcasted_iota(jnp.int32, (count, width), 0) + offset
-        return matmul(ref[...], jnp.where(lanes == spots, 1.0, 0.0).astype(BF16))
-
-    vectors = spread(lines_ref, me * step)
-    place = me * inner_ref.shape[1]
-    inner = spread(inner_ref, lax.rem(place, width))
+    small = small_ref[...]
+    step, inner_size, steps = sizes
+
+    def spread(first, count, offset):
+        spots = lax.broadcasted_iota(jnp.int32, (small.shape[1], width), 0) - first
+        lanes = lax.broadcasted_iota(jnp.int32, (small.shape[1], width), 1)
+        hits = (spots >= 0) & (spots < count) & (lanes == spots + offset)
+        return matmul(small, jnp.where(hits, 1.0, 0.0).astype(BF16))
+
+    vectors = spread(0, step, me * step)
+    place = me * inner_size
+    inner = spread(step, inner_size, lax.rem(place, width))
     row = lax.broadcasted_iota(jnp.int32, inner.shape, 0)
     inner = jnp.where(row == place // width, inner, 0.0)
-    out_ref[start:] = jnp.concatenate([vectors, inner]).astype(BF16)
-
-
-def pack(me, shards, lines, inner):
+    times = spread(step + inner_size, steps, me * steps)
+    out_ref[start:] = jnp.concatenate([vectors, inner + times]).astype(BF16)
+
+
+def pack(me, shards, vectors, inner, times):
     step, width = shards[0].shape
+    sizes = (step, inner.shape[0], times.shape[0])
+    small = 0.0
+    for line, vector in enumerate(vectors):
+        small += jnp.pad(vector.astype(F32)[None], ((line, 7 - line), (0, 256 - step)))
+    rest = 256 - sizes[1] - step
+    small += jnp.pad(inner.astype(F32)[None], ((0, 0), (step, rest)))
+    for line, digits in ((4, times // 64), (5, times % 64)):
+        left = step + sizes[1]
+        right = 256 - left - sizes[2]
+        small += jnp.pad(digits.astype(F32)[None], ((line, 7 - line), (left, right)))
+    small = small.astype(BF16)
+    rows = len(shards) * step + 16
     return call(
-        functools.partial(pack_body, step),
+        functools.partial(pack_body, sizes),
         "pack",
         (1,),
         [(me.reshape(1), SMEM_SPEC)]
-        + [(array, full_spec(array.shape)) for array in (lines, inner, *shards)],
-        [((len(shards) * step + 16, width), BF16, full_spec((len(shards) * step + 16, width)))],
+        + [(array, full_spec(array.shape)) for array in (small, *shards)],
+        [((rows, width), BF16, full_spec((rows, width)))],
         [],
         1,
     )[0]
@@ -1135,29 +1159,35 @@
     return after(state[0], others), state[1]
 
 
-def stream_ends(state, unit):
+def stream_ends(state, unit, sizes):
     if not state.plain:
         total = state.net.scatter_end(state.state)
-        return [total[w * unit : (w + 1) * unit] for w in range(3)] + [total[3 * unit]]
+        found, start = [total[w * unit : (w + 1) * unit] for w in range(3)], 0
+        for size in sizes:
+            found.append(total[3 * unit, start : start + size])
+            start += size
+        return found
     rows, columns = state.rows, state.columns
     step_block = ((1, rows, columns), lambda i, at: (at, 0, 0))
     ins = state.sources(0, step_block)
     ins += [(term, step_block[0], lambda i, me: (0, 0, 0)) for term in state.terms[4:]]
-    shapes = [(unit, columns)] * 3 + [(8, columns)]
+    shapes = [(unit, columns)] * 3 + [(1, size) for size in sizes]
     outs = [(shape, F32, shape, lambda i, me: (0, 0)) for shape in shapes]
 
     def body(me_ref, *refs):
         total = refs[0][0].astype(F32)
         for ref in refs[1 : len(ins)]:
             total = total + ref[0].astype(F32)
+        outs = refs[len(ins) :]
+        for w in range(3):
+            outs[w][...] = total[w * unit : (w + 1) * unit]
         start = 0
-        for out_ref in refs[len(ins) :]:
-            count = out_ref.shape[0]
-            out_ref[...] = total[start : start + count]
-            start += count
+        for out_ref, size in zip(outs[3:], sizes):
+            out_ref[...] = total[3 * unit : 3 * unit + 1, start : start + size]
+            start += size
 
     results = sum_call(state.me, "stream_end", 1, ins, None, outs, body)
-    return list(results[:3]) + [results[3][0]]
+    return list(results[:3]) + [result[0] for result in results[3:]]
 
 
 def on_device(
@@ -1183,15 +1213,11 @@
     feats = features(timesteps.reshape(rows)).astype(BF16)
     order = (0, 1, 2, 4, 5, 6, 7, 8, 3)
     sizes = [vectors[i].shape[0] for i in order]
-    small = sum(
-        jnp.pad(vectors[i].astype(F32)[None], ((line, 7 - line), (0, 0)))
-        for line, i in enumerate(order[:8])
-    )
-    inner_line = jnp.broadcast_to(vectors[3][None], (8, sizes[-1]))
     r = model_width // n
 
     shards = (time_weight, query_weight, key_weight, value_weight)
-    far = net.gather_far(pack(me, shards, small.astype(BF16), inner_line))
+    lines = [vectors[i] for i in order[:8]]
+    far = net.gather_far(pack(me, shards, lines, vectors[3], timesteps.reshape(rows)))
     hidden = inner_weight.shape[1]
     inner_blocks = [
         inner_weight[:, start : start + model_width] for start in range(0, hidden, model_width)
@@ -1214,17 +1240,17 @@
         net, me, flow, feats_in, x, row_length
     )
     far_u = net.stacked(after(far_u, queries))
+    near_u = net.gather_near(far_u)
     near_io, queries = after((near_io, queries), far_u)
     pieces, corners, sent = net.gather_corner(far_io, near_io)
-    far_u = after(far_u, sent)
-    near_u = net.gather_near(far_u)
-    queries = after(queries, (sent, far_u))
+    queries = after(queries, sent)
     context, log_total = attend(queries, key_rows, values, segments)
-    corners, context, pieces = after((corners, context, pieces), ())
-    flow_io = net.gather_core(pieces) + net.gather_core(corners)
-    near_u, flow_io = after((near_u, flow_io), ())
-    pieces, corners, sent = net.gather_corner(far_u, near_u)
-    context = after(context, sent)
+    near_u, context, pieces = after((near_u, context, pieces), ())
+    flow_io = net.gather_core(pieces)
+    pieces, corners_u, sent = net.gather_corner(far_u, near_u)
+    context, corners = after((context, corners), sent)
+    flow_io += net.gather_core(corners)
+    corners = corners_u
     first_low, normed_first, spread_first, active_low, slope = ffn_in(
         net, me, flow_io, context, x, temb, lines, hidden, row_length
     )
@@ -1278,7 +1304,8 @@
     found, sums_rows, row_sums = None, 0.0, [mixed_rows]
     for row in range(rows):
         if row == 1:
-            sent = inner_sum.hold(found[1]).corner() + list(outer_sum.hold(found[1]).far())
+            sent = list(inner_sum.hold(found[1]).corner())
+            sent += list(outer_sum.hold((found[1], sent)).far())
             found = after(found, sent)
         found = attend_back(*back, row, found or ())
         sums_rows += found[3]
@@ -1286,13 +1313,13 @@
         found = found[:3]
     grad_queries, grad_keys, grad_values = found
     sent = inner_sum.hold(grad_queries).near()
-    (outer_weight_grad,) = outer_sum.hold(grad_queries).end([1], outer_weight.shape[0])
+    outer_sum.hold(grad_queries)
     sums = sums_rows + sums_out + sums_back
     sums = sums.reshape(8, n, r).transpose(1, 0, 2).reshape(n, 8 * r)
     sums = jnp.concatenate([sums, inner_bias_grad.reshape(n, -1)], axis=1)
     sums = jnp.pad(sums, ((0, 0), (0, model_width - sums.shape[1]))).astype(BF16)
     sums = jnp.broadcast_to(sums[:, None], (n, 8, model_width)).reshape(n // 2, 16, model_width)
-    stream_low, sums = after((stream_low, sums), (sent, outer_weight_grad))
+    stream_low, sums = after((stream_low, sums), (sent, outer_sum.received()))
     stream_halves = triple_product(
         net, me, sums, stream_low, grad_queries, grad_keys, grad_values
     )
@@ -1300,38 +1327,39 @@
     grad_mixed = after(grad_mixed, stream_halves)
     back = (flow, grad_mixed, grad_queries, grad_keys, grad_values)
     grad_stream, grad_temb = stream_back(net, me, *back, 0, row_length, sums=row_sums)
-    ends = jnp.concatenate([feats.astype(F32), grad_temb[:rows]], axis=1)[None]
+    ends = grad_temb[:rows][None]
     sources, ends = net.gather_round([0], ends, net.masks(net.core))
-    sent = inner_sum.hold(grad_temb).far()
-    sent = list(sent) + stream_sum.hold((grad_temb, sent)).corner()
-    ends, grad_stream = after((ends, grad_stream), sent)
+    sent = list(stream_sum.hold(grad_temb).corner())
+    sent += list(inner_sum.hold((grad_temb, sent)).far())
+    ends = after(ends, sent)
+    sent = stream_sum.hold(sent).near()
+    grad_stream = after(grad_stream, sent)
     for row in range(1, rows):
         (grad_stream,) = stream_back(net, me, *back, row, row_length, grad_stream)
-    sent = stream_sum.hold(grad_stream).near()
-    output_weight_grad, inner_weight_grad = inner_sum.hold(sent).end([1, hidden // model_width], r)
-    ends = after(ends, (sent, output_weight_grad))
-    sources, ends = net.gather_round(sources, ends, net.inner_masks())
-    stream_sum.hold(ends).far()
+    inner_sum.hold(grad_stream), outer_sum.hold(grad_stream)
+    output_weight_grad, inner_weight_grad = inner_sum.end([1, hidden // model_width], r)
+    (outer_weight_grad,) = outer_sum.end([1], outer_weight.shape[0])
+    ends = after(ends, (grad_stream, inner_sum.received()))
+    sources, ends = net.gather_round(sources, ends, net.masks(net.near))
+    sent = stream_sum.hold(grad_stream).far()
+    sources, ends = net.gather_round(sources, after(ends, sent), net.masks(net.middle))
     sources, ends = net.gather_round(
         sources, after(ends, stream_sum.received()), net.masks(net.outer)
     )
-    ends = in_order(net, me, sources, ends).reshape(n * rows, 2 * model_width)
-    query_weight_grad, key_weight_grad, value_weight_grad, vector_sums = stream_ends(
-        stream_sum, r
-    )
-    feats_all, temb_all = ends[:, :model_width], ends[:, model_width:]
+    temb_all = in_order(net, me, sources, ends).reshape(n * rows, model_width)
+    query_weight_grad, key_weight_grad, value_weight_grad, *parts = stream_ends(
+        stream_sum, r, sizes
+    )
     own = model_width // n
-    feats_own = lax.dynamic_slice_in_dim(feats_all, me * own, own, 1)
+    steps_all = (lines[12] * 64.0 + lines[13])[: n * rows]
+    feats_own = own_features(steps_all, me * own, own).astype(BF16).astype(F32)
     time_weight_grad = lax.dot_general(
         feats_own,
         temb_all,
         (((0,), (0,)), ((), ())),
         precision=lax.Precision.HIGHEST,
     )
-    parts, start = {}, 0
-    for i, size in zip(order, sizes):
-        parts[i] = vector_sums[start : start + size]
-        start += size
+    parts = dict(zip(order, parts))
     vector_outs = [parts[i] for i in range(len(order))]
 
     shape = inputs.shape

time: 494 us -> 459 us (0.929)
  waiting for transfers between devices: 93 us -> 71.3 us
  starting transfers between devices: 89 us -> 83.4 us
  local copies, waits for them, and re-layouts: 15.5 us -> 10.2 us
  Pallas kernels: 275 us -> 270 us
    ppermute x67 -> x66, waiting for transfers between devices: 93 us -> 71.3 us  [swap(): return lax.ppermute(array, 'fsdp', [(i, i ^ mask) for i in range(self.n)])]
    ppermute x67 -> x66, starting transfers between devices: 89 us -> 83.4 us  [swap(): return lax.ppermute(array, 'fsdp', [(i, i ^ mask) for i in range(self.n)])]
  transfers between devices with their start and end apart: 67 -> 66, of which waited for: 21 -> 22; matrix products, arithmetic and copies ran while one was open for 3% -> 3% of each run, Pallas kernels for 46% -> 50%
where the time goes in v4:
time: 459 us; the launch traced here: 452 us
  Pallas kernels  270 us (59%)
  starting transfers between devices  83.4 us (18%)
  waiting for transfers between devices  71.3 us (16%)
  other arithmetic  14 us (3%)
  local copies, waits for them, and re-layouts  10.2 us (2%)
    pallas_call x13, Pallas kernels, call(): pl.pallas_call(run, grid=grid, in_specs=[spec for _, spec in ins] + [ANY_...  226 us
    ppermute x66, starting transfers between devices, swap(): return lax.ppermute(array, 'fsdp', [(i, i ^ mask) for i in range(self.n)])  83.4 us
    ppermute x66, waiting for transfers between devices, swap(): return lax.ppermute(array, 'fsdp', [(i, i ^ mask) for i in range(self.n)])  71.3 us
    pallas_call x12, Pallas kernels, sum_call(): pl.pallas_call(body or functools.partial(sum_body, groups), grid_spec=gri...  39.4 us
  transfers between devices with their start and end apart: 66, of which 22 were waited for; matrix products, arithmetic and copies ran while one was open for 3% of the time, Pallas kernels for 50%

profile of v4, /device:TPU:0, one launch (start us, length us, event | category | flops | bytes accessed | tf_op | source)
XLA Modules:
  0.0 451.6 jit_solution(3306286737051977086)
XLA Ops:
  11.0 13.7 %collective-permute-done = bf16[144,1024]{1,0:T(8,128)(2,1)S(1)} collective-permute-done((bf16[144,1024]{1,0:T(8,128)(2,1)}, bf16[144,1024]{1,0:T(8,128)(2,1)S(1)}, u32[]{:S(2)}, u32[]{:S(2)}) %collective-permute-start) | collective-permute-done | bytes 294944 | tf_op jit(solution)/shard_map/ppermute | solution.py:112
  24.7 5.8 %collective-permute-done.2 = bf16[144,1024]{1,0:T(8,128)(2,1)S(1)} collective-permute-done((bf16[144,1024]{1,0:T(8,128)(2,1)}, bf16[144,1024]{1,0:T(8,128)(2,1)S(1)}, u32[]{:S(2)}, u32[]{:S(2)}) %collective-permute-start.2) | collective-permute-done | bytes 294944 | tf_op jit(solution)/shard_map/ppermute | solution.py:112
  34.8 7.8 %collective-permute-start.3 = (bf16[160,1024]{1,0:T(8,128)(2,1)S(1)}, bf16[160,1024]{1,0:T(8,128)(2,1)S(1)}, u32[]{:S(2)}, u32[]{:S(2)}) collective-permute-start(bf16[160,1024]{1,0:T(8,128)(2,1)S(1)} %slice_dynamic-update-slice_fusion), channel_id=1, source_target_pairs={{0,16},{1,17},{2,18},{3,19},{4,20},{5,21},{6,22},{7,23},{8,24},{9,... | collective-permute-start | bytes 983048 | tf_op jit(solution)/shard_map/ppermute | solution.py:112
  44.1 14.4 %collective-permute-done.6.low_in.refs_3_ = bf16[4,144,1024]{2,1,0:T(8,128)(2,1)S(1)} collective-permute-done((bf16[4,144,1024]{2,1,0:T(8,128)(2,1)S(1)}, bf16[4,144,1024]{2,1,0:T(8,128)(2,1)S(1)}, u32[]{:S(2)}, u32[]{:S(2)}) %collective-permute-start.6) | collective-permute-done | bytes 1179680 | tf_op jit(solution)/shard_map/ppermute | solution.py:112
  66.9 6.1 %collective-permute-done.8.refs_7_ = bf16[2,144,1024]{2,1,0:T(8,128)(2,1)} collective-permute-done((bf16[2,144,1024]{2,1,0:T(8,128)(2,1)S(1)}, bf16[2,144,1024]{2,1,0:T(8,128)(2,1)}, u32[]{:S(2)}, u32[]{:S(2)}) %collective-permute-start.8) | collective-permute-done | bytes 589856 | tf_op jit(solution)/shard_map/ppermute | solution.py:112
  77.7 10.0 %collective-permute-start.15 = (bf16[128,1024]{1,0:T(8,128)(2,1)}, bf16[128,1024]{1,0:T(8,128)(2,1)}, u32[]{:S(2)}, u32[]{:S(2)}) collective-permute-start(bf16[128,1024]{1,0:T(8,128)(2,1)} %param.30), channel_id=1, source_target_pairs={{0,16},{1,17},{2,18},{3,19},{4,20},{5,21},{6,22},{7,23},{8,24},{9,... | collective-permute-start | bytes 786440 | tf_op jit(solution)/shard_map/ppermute | solution.py:112
  89.2 14.5 %project.1 = (f32[2,1024]{1,0:T(2,128)}, f32[16,1024]{1,0:T(8,128)}, bf16[1024,1024]{1,0:T(8,128)(2,1)}, bf16[1024,1024]{1,0:T(8,128)(2,1)}, bf16[1024,1024]{1,0:T(8,128)(2,1)}, /*index=5*/bf16[1024,1024]{1,0:T(8,128)(2,1)}) custom-call(s32[1]{0:T(128)} %bitcast.refs_0_.me_ref, bf16[4,144,1024]{2,1,0:T(8,128)(2,1)} %copy-done.4, ...), custom_call_target="tpu_custom_call" | custom-call | flops 280000004096 | bytes 700000000 | tf_op jit(solution)/shard_map/project/pallas_call | solution.py:327
  115.1 20.0 %attend.1 = (bf16[1024,1024]{1,0:T(8,128)(2,1)}, f32[2,4,4,512]{3,2,1,0:T(4,128)}) custom-call(s32[2,512,1]{2,1,0:T(8,128)} %broadcast_in_dim_reshape.6.refs_0_, s32[2,1,512]{2,1,0:T(1,128)} %refs_1_.5, bf16[1024,1024]{1,0:T(8,128)(2,1)} %get-tuple-element.212.refs_2_, bf16[1024,1024]{1,0:T(8,128)(2,1)} %get-tuple-element.213.refs_3_, ...), custom_call_target="tpu_custom_call" | custom-call | flops 480000016384 | bytes 1200000000 | tf_op jit(solution)/shard_map/attend/pallas_call | solution.py:327
  139.0 7.5 %collective-permute-done.30.refs_7_.refs_17_ = bf16[2,160,1024]{2,1,0:T(8,128)(2,1)} collective-permute-done((bf16[2,160,1024]{2,1,0:T(8,128)(2,1)}, bf16[2,160,1024]{2,1,0:T(8,128)(2,1)}, u32[]{:S(2)}, u32[]{:S(2)}) %collective-permute-start.30) | collective-permute-done | bytes 655392 | tf_op jit(solution)/shard_map/ppermute | solution.py:112
  152.8 29.1 %ffn_in.1 = (bf16[1024,1024]{1,0:T(8,128)(2,1)}, f32[1024,1024]{1,0:T(8,128)}, f32[1024,1]{1,0:T(8,128)}, bf16[1024,4096]{1,0:T(8,128)(2,1)}, bf16[1024,4096]{1,0:T(8,128)(2,1)}) custom-call(s32[1]{0:T(128)} %bitcast.refs_0_.me_ref, bf16[4,160,1024]{2,1,0:T(8,128)(2,1)} %pad_maximum_fusion.refs_1_.refs_11_, ...), custom_call_target="tpu_custom_call" | custom-call | flops 599999971328 | bytes 1500000000 | tf_op jit(solution)/shard_map/ffn_in/pallas_call | solution.py:327
  185.7 20.9 %ffn_out.1 = (bf16[1024,1024]{1,0:T(8,128)(2,1)}, f32[1024,1024]{1,0:T(8,128)}, bf16[1024,1024]{1,0:T(8,128)(2,1)}, f32[8,1024]{1,0:T(8,128)}) custom-call(s32[1]{0:T(128)} %bitcast.refs_0_.me_ref, bf16[4,128,1024]{2,1,0:T(8,128)(2,1)} %pad_maximum_fusion.2.refs_1_, bf16[4,128,1024]{2,1,0:T(8,128)(2,1)} %collective-permute-done.18.high_in.refs_2_, ...), custom_call_target="tpu_custom_call" | custom-call | flops 399999991808 | bytes 1000000000 | tf_op jit(solution)/shard_map/ffn_out/pallas_call | solution.py:327
  206.7 13.2 %product.1 = (bf16[16,128,1024]{2,1,0:T(8,128)(2,1)}, bf16[16,128,1024]{2,1,0:T(8,128)(2,1)}) custom-call(s32[1]{0:T(128)} %bitcast.refs_0_.me_ref, bf16[1024,4096]{1,0:T(8,128)(2,1)} %get-tuple-element.232.refs_11_.refs_1_, bf16[1024,1024]{1,0:T(8,128)(2,1)} %get-tuple-element.236.refs_2_.refs_22_), custom_call_target="tpu_custom_call" | custom-call | flops 299999985664 | bytes 750000000 | tf_op jit(solution)/shard_map/product/pallas_call | solution.py:327
  219.9 37.6 %ffn_back.1 = (bf16[1024,4096]{1,0:T(8,128)(2,1)}, f32[1024,1024]{1,0:T(8,128)}, bf16[1024,1024]{1,0:T(8,128)(2,1)}, bf16[1024,1024]{1,0:T(8,128)(2,1)}, f32[1,4...) custom-call(s32[1]{0:T(128)} %bitcast.refs_0_.me_ref, bf16[4,128,1024]{2,1,0:T(8,128)(2,1)} %pad_maximum_fusion.2.refs_1_, ...), custom_call_target="tpu_custom_call" | custom-call | flops 760000020480 | bytes 1900000000 | tf_op jit(solution)/shard_map/ffn_back/pallas_call | solution.py:327
  263.4 17.7 %inner_product.1 = (bf16[16,160,1024]{2,1,0:T(8,128)(2,1)}, bf16[16,160,1024]{2,1,0:T(8,128)(2,1)}) custom-call(s32[1]{0:T(128)} %bitcast.refs_0_.me_ref, bf16[1024,1024]{1,0:T(8,128)(2,1)} %get-tuple-element.226.refs_11_.refs_1_, bf16[1024,1024]{1,0:T(8,128)(2,1)} %get-tuple-element.246.refs_2_, bf16[1024,1024]{1,0:T(8,128)(2,1)} %get-tuple-element.252.refs_3_, ...), custom_call_target="tpu_custom_call" | custom-call | flops 359999995904 | bytes 900000000 | tf_op jit(solution)/shard_map/inner_product/pallas_call | solution.py:327
  281.1 4.6 %near_sum.3 = (bf16[4,128,1024]{2,1,0:T(8,128)(2,1)}, bf16[4,128,1024]{2,1,0:T(8,128)(2,1)}) custom-call(s32[1]{0:T(128)} %bitcast.refs_0_.me_ref, bf16[16,128,1024]{2,1,0:T(8,128)(2,1)} %get-tuple-element.348.refs_0_.refs_2_.refs_4_.refs_8_, bf16[16,128,1024]{2,1,0:T(8,128)(2,1)} %collective-permute-done.36.refs_1_.refs_3_.refs_5_.refs_9_, ...), custom_call_target="tpu_custom_call" | custom-call | flops 200000000 | bytes 500000 | tf_op jit(solution)/shard_map/near_sum/pallas_call | solution.py:372
  287.7 18.8 %attend_back.2 = (bf16[1024,1024]{1,0:T(8,128)(2,1)}, bf16[1024,1024]{1,0:T(8,128)(2,1)}, bf16[1024,1024]{1,0:T(8,128)(2,1)}, f32[8,1024]{1,0:T(8,128)}, f32[8,1024]{1,0:T(8,128)}) custom-call(s32[2,512,1]{2,1,0:T(8,128)} %broadcast_in_dim_reshape.6.refs_0_, s32[2,1,512]{2,1,0:T(1,128)} %refs_1_.5, bf16[1024,1024]{1,0:T(8,128)(2,1)} %get-tuple-element.212.refs_2_, ...), custom_call_target="tpu_custom_call" | custom-call | flops 380000010240 | bytes 950000000 | tf_op jit(solution)/shard_map/attend_back/pallas_call | solution.py:327
  315.5 7.9 %collective-permute-start.44 = (bf16[1,128,1024]{2,1,0:T(8,128)(2,1)}, bf16[1,128,1024]{2,1,0:T(8,128)(2,1)}, u32[]{:S(2)}, u32[]{:S(2)}) collective-permute-start(bf16[1,128,1024]{2,1,0:T(8,128)(2,1)} %get-tuple-element.275), channel_id=1, source_target_pairs={{0,16},{1,17},{2,18},{3,19},{4,20},{5,21},{6,22},{7,23},{8,24},{9,... | collective-permute-start | bytes 786440 | tf_op jit(solution)/shard_map/ppermute | solution.py:112
  324.9 18.7 %attend_back.3 = (bf16[1024,1024]{1,0:T(8,128)(2,1)}, bf16[1024,1024]{1,0:T(8,128)(2,1)}, bf16[1024,1024]{1,0:T(8,128)(2,1)}, f32[8,1024]{1,0:T(8,128)}, f32[8,1024]{1,0:T(8,128)}) custom-call(s32[2,512,1]{2,1,0:T(8,128)} %broadcast_in_dim_reshape.6.refs_0_, s32[2,1,512]{2,1,0:T(1,128)} %refs_1_.5, ...), custom_call_target="tpu_custom_call", output_to_operand_aliasing={{0}: (7, {}), {1}: (8, {}), {2}: (9, {})} | custom-call | flops 380000010240 | bytes 950000000 | tf_op jit(solution)/shard_map/attend_back/pallas_call | solution.py:327
  344.7 5.0 %near_sum.4 = (bf16[4,160,1024]{2,1,0:T(8,128)(2,1)}, bf16[4,160,1024]{2,1,0:T(8,128)(2,1)}) custom-call(s32[1]{0:T(128)} %bitcast.refs_0_.me_ref, bf16[16,160,1024]{2,1,0:T(8,128)(2,1)} %get-tuple-element.333.refs_0_.refs_2_.refs_4_.refs_8_, bf16[16,160,1024]{2,1,0:T(8,128)(2,1)} %collective-permute-done.39.refs_1_.refs_3_.refs_5_.refs_9_, ...), custom_call_target="tpu_custom_call" | custom-call | flops 200000000 | bytes 500000 | tf_op jit(solution)/shard_map/near_sum/pallas_call | solution.py:372
  352.8 11.8 %triple_product.1 = (bf16[16,104,1024]{2,1,0:T(8,128)(2,1)}, bf16[16,104,1024]{2,1,0:T(8,128)(2,1)}) custom-call(s32[1]{0:T(128)} %bitcast.refs_0_.me_ref, bf16[16,16,1024]{2,1,0:T(8,128)(2,1)} %bitcast.75, bf16[1024,1024]{1,0:T(8,128)(2,1)} %get-tuple-element.294.refs_2_, bf16[1024,1024]{1,0:T(8,128)(2,1)} %get-tuple-element.285.refs_3_.refs_12_, ...), custom_call_target="tpu_custom_call" | custom-call | flops 260000006144 | bytes 650000000 | tf_op jit(solution)/shard_map/triple_product/pallas_call | solution.py:327
  364.6 12.1 %stream_back.2 = (f32[1024,1024]{1,0:T(8,128)}, f32[8,1024]{1,0:T(8,128)}) custom-call(s32[1]{0:T(128)} %bitcast.refs_0_.me_ref, bf16[4,144,1024]{2,1,0:T(8,128)(2,1)} %copy-done.4, bf16[4,144,1024]{2,1,0:T(8,128)(2,1)} %copy-done.1, bf16[4,144,1024]{2,1,0:T(8,128)(2,1)} %copy-done, bf16[4,144,1024]{2,1,0:T(8,128)(2,1)} %collective-permute-done.10.refs_4_, ...), custom_call_target="tpu_custom_call" | custom-call | flops 199999995904 | bytes 500000000 | tf_op jit(solution)/shard_map/stream_back/pallas_call | solution.py:327
  393.0 4.4 near_sum.5
  399.6 10.0 %stream_back.3 = f32[1024,1024]{1,0:T(8,128)} custom-call(s32[1]{0:T(128)} %bitcast.refs_0_.me_ref, bf16[4,144,1024]{2,1,0:T(8,128)(2,1)} %copy-done.4, bf16[4,144,1024]{2,1,0:T(8,128)(2,1)} %copy-done.1, bf16[4,144,1024]{2,1,0:T(8,128)(2,1)} %copy-done, bf16[4,144,1024]{2,1,0:T(8,128)(2,1)} %collective-permute-done.10.refs_4_, ...), custom_call_target="tpu_custom_call", output_to_operand_aliasing={{}: (15, {})} | custom-call | flops 199999995904 | bytes 500000000 | tf_op jit(solution)/shard_map/stream_back/pallas_call | solution.py:327
  433.2 5.4 %collective-permute-start.63 = (f32[8,2,1024]{2,1,0:T(2,128)S(1)}, f32[8,2,1024]{2,1,0:T(2,128)S(1)}, u32[]{:S(2)}, u32[]{:S(2)}) collective-permute-start(f32[8,2,1024]{2,1,0:T(2,128)S(1)} %pad_maximum_fusion.4), channel_id=1, source_target_pairs={{0,16},{1,17},{2,18},{3,19},{4,20},{5,21},{6,22},{7,23},{8,24},{9,... | collective-permute-start | bytes 196616 | tf_op jit(solution)/shard_map/ppermute | solution.py:112
  (237 shorter events, 133.0 us)
Async XLA Ops:
  31.6 26.9 %collective-permute-start.6 = (bf16[4,144,1024]{2,1,0:T(8,128)(2,1)S(1)}, bf16[4,144,1024]{2,1,0:T(8,128)(2,1)S(1)}, u32[]{:S(2)}, u32[]{:S(2)}) collective-permute-start(bf16[4,144,1024]{2,1,0:T(8,128)(2,1)S(1)} %pad_maximum_fusion.1.refs_1_), channel_id=1, source_target_pairs={{0,4},{1,5},{2,6},{3,7},{4,0},{5,1},{6,2},{7,3},{8,12},{9,13},{10,... | collective-permute-start | bytes 3538952 | tf_op jit(solution)/shard_map/ppermute | solution.py:112
  33.2 26.5 %collective-permute-start.7 = (bf16[4,144,1024]{2,1,0:T(8,128)(2,1)S(1)}, bf16[4,144,1024]{2,1,0:T(8,128)(2,1)S(1)}, u32[]{:S(2)}, u32[]{:S(2)}) collective-permute-start(bf16[4,144,1024]{2,1,0:T(8,128)(2,1)S(1)} %pad_maximum_fusion.1.refs_1_), channel_id=1, source_target_pairs={{0,2},{1,3},{2,0},{3,1},{4,6},{5,7},{6,4},{7,5},{8,10},{9,11},{10,... | collective-permute-start | bytes 3538952 | tf_op jit(solution)/shard_map/ppermute | solution.py:112
  34.8 29.7 %collective-permute-start.3 = (bf16[160,1024]{1,0:T(8,128)(2,1)S(1)}, bf16[160,1024]{1,0:T(8,128)(2,1)S(1)}, u32[]{:S(2)}, u32[]{:S(2)}) collective-permute-start(bf16[160,1024]{1,0:T(8,128)(2,1)S(1)} %slice_dynamic-update-slice_fusion), channel_id=1, source_target_pairs={{0,16},{1,17},{2,18},{3,19},{4,20},{5,21},{6,22},{7,23},{8,24},{9,... | collective-permute-start | bytes 983048 | tf_op jit(solution)/shard_map/ppermute | solution.py:112
  76.5 34.9 %collective-permute-start.20 = (bf16[4,160,1024]{2,1,0:T(8,128)(2,1)}, bf16[4,160,1024]{2,1,0:T(8,128)(2,1)}, u32[]{:S(2)}, u32[]{:S(2)}) collective-permute-start(bf16[4,160,1024]{2,1,0:T(8,128)(2,1)} %pad_maximum_fusion.refs_1_.refs_11_), channel_id=1, source_target_pairs={{0,2},{1,3},{2,0},{3,1},{4,6},{5,7},{6,4},{7,5},{8,10},{9,11},{10,... | collective-permute-start | bytes 3932168 | tf_op jit(solution)/shard_map/ppermute | solution.py:112
  77.1 34.4 %collective-permute-start.21 = (bf16[4,160,1024]{2,1,0:T(8,128)(2,1)}, bf16[4,160,1024]{2,1,0:T(8,128)(2,1)}, u32[]{:S(2)}, u32[]{:S(2)}) collective-permute-start(bf16[4,160,1024]{2,1,0:T(8,128)(2,1)} %pad_maximum_fusion.refs_1_.refs_11_), channel_id=1, source_target_pairs={{0,4},{1,5},{2,6},{3,7},{4,0},{5,1},{6,2},{7,3},{8,12},{9,13},{10,... | collective-permute-start | bytes 3932168 | tf_op jit(solution)/shard_map/ppermute | solution.py:112
  77.7 26.1 %collective-permute-start.15 = (bf16[128,1024]{1,0:T(8,128)(2,1)}, bf16[128,1024]{1,0:T(8,128)(2,1)}, u32[]{:S(2)}, u32[]{:S(2)}) collective-permute-start(bf16[128,1024]{1,0:T(8,128)(2,1)} %param.30), channel_id=1, source_target_pairs={{0,16},{1,17},{2,18},{3,19},{4,20},{5,21},{6,22},{7,23},{8,24},{9,... | collective-permute-start | bytes 786440 | tf_op jit(solution)/shard_map/ppermute | solution.py:112
  108.8 26.4 %collective-permute-start.18 = (bf16[4,128,1024]{2,1,0:T(8,128)(2,1)}, bf16[4,128,1024]{2,1,0:T(8,128)(2,1)}, u32[]{:S(2)}, u32[]{:S(2)}) collective-permute-start(bf16[4,128,1024]{2,1,0:T(8,128)(2,1)} %pad_maximum_fusion.2.refs_1_), channel_id=1, source_target_pairs={{0,2},{1,3},{2,0},{3,1},{4,6},{5,7},{6,4},{7,5},{8,10},{9,11},{10,... | collective-permute-start | bytes 3145736 | tf_op jit(solution)/shard_map/ppermute | solution.py:112
  110.0 26.4 %collective-permute-start.19 = (bf16[4,128,1024]{2,1,0:T(8,128)(2,1)}, bf16[4,128,1024]{2,1,0:T(8,128)(2,1)}, u32[]{:S(2)}, u32[]{:S(2)}) collective-permute-start(bf16[4,128,1024]{2,1,0:T(8,128)(2,1)} %pad_maximum_fusion.2.refs_1_), channel_id=1, source_target_pairs={{0,4},{1,5},{2,6},{3,7},{4,0},{5,1},{6,2},{7,3},{8,12},{9,13},{10,... | collective-permute-start | bytes 3145736 | tf_op jit(solution)/shard_map/ppermute | solution.py:112
  113.6 32.9 %collective-permute-start.30 = (bf16[2,160,1024]{2,1,0:T(8,128)(2,1)}, bf16[2,160,1024]{2,1,0:T(8,128)(2,1)}, u32[]{:S(2)}, u32[]{:S(2)}) collective-permute-start(bf16[2,160,1024]{2,1,0:T(8,128)(2,1)} %get-tuple-element.210), channel_id=1, source_target_pairs={{0,2},{1,3},{2,0},{3,1},{4,6},{5,7},{6,4},{7,5},{8,10},{9,11},{10,... | collective-permute-start | bytes 1966088 | tf_op jit(solution)/shard_map/ppermute | solution.py:112
  114.1 32.9 %collective-permute-start.31 = (bf16[2,160,1024]{2,1,0:T(8,128)(2,1)}, bf16[2,160,1024]{2,1,0:T(8,128)(2,1)}, u32[]{:S(2)}, u32[]{:S(2)}) collective-permute-start(bf16[2,160,1024]{2,1,0:T(8,128)(2,1)} %get-tuple-element.211), channel_id=1, source_target_pairs={{0,4},{1,5},{2,6},{3,7},{4,0},{5,1},{6,2},{7,3},{8,12},{9,13},{10,... | collective-permute-start | bytes 1966088 | tf_op jit(solution)/shard_map/ppermute | solution.py:112
  150.2 34.0 %collective-permute-start.22 = (bf16[4,128,1024]{2,1,0:T(8,128)(2,1)}, bf16[4,128,1024]{2,1,0:T(8,128)(2,1)}, u32[]{:S(2)}, u32[]{:S(2)}) collective-permute-start(bf16[4,128,1024]{2,1,0:T(8,128)(2,1)} %pad_maximum_fusion.2.refs_1_), channel_id=1, source_target_pairs={{0,1},{1,0},{2,3},{3,2},{4,5},{5,4},{6,7},{7,6},{8,9},{9,8},{10,11... | collective-permute-start | bytes 3145736 | tf_op jit(solution)/shard_map/ppermute | solution.py:112
  150.4 31.6 %collective-permute-start.25 = (bf16[2,128,1024]{2,1,0:T(8,128)(2,1)}, bf16[2,128,1024]{2,1,0:T(8,128)(2,1)}, u32[]{:S(2)}, u32[]{:S(2)}) collective-permute-start(bf16[2,128,1024]{2,1,0:T(8,128)(2,1)} %get-tuple-element.218), channel_id=1, source_target_pairs={{0,2},{1,3},{2,0},{3,1},{4,6},{5,7},{6,4},{7,5},{8,10},{9,11},{10,... | collective-permute-start | bytes 1572872 | tf_op jit(solution)/shard_map/ppermute | solution.py:112
  151.6 30.4 %collective-permute-start.26 = (bf16[2,128,1024]{2,1,0:T(8,128)(2,1)}, bf16[2,128,1024]{2,1,0:T(8,128)(2,1)}, u32[]{:S(2)}, u32[]{:S(2)}) collective-permute-start(bf16[2,128,1024]{2,1,0:T(8,128)(2,1)} %get-tuple-element.219), channel_id=1, source_target_pairs={{0,4},{1,5},{2,6},{3,7},{4,0},{5,1},{6,2},{7,3},{8,12},{9,13},{10,... | collective-permute-start | bytes 1572872 | tf_op jit(solution)/shard_map/ppermute | solution.py:112
  152.3 31.9 %collective-permute-start.23 = (bf16[4,128,1024]{2,1,0:T(8,128)(2,1)}, bf16[4,128,1024]{2,1,0:T(8,128)(2,1)}, u32[]{:S(2)}, u32[]{:S(2)}) collective-permute-start(bf16[4,128,1024]{2,1,0:T(8,128)(2,1)} %collective-permute-done.18.high_in.refs_2_), channel_id=1, source_target_pairs={{0,1},{1,0},{2,3},{3,2},{4,5},{5,4},{6,7},{7,6},{8,9},{9,8},{10,11... | collective-permute-start | bytes 3145736 | tf_op jit(solution)/shard_map/ppermute | solution.py:112
  152.3 31.9 %collective-permute-start.24 = (bf16[4,128,1024]{2,1,0:T(8,128)(2,1)}, bf16[4,128,1024]{2,1,0:T(8,128)(2,1)}, u32[]{:S(2)}, u32[]{:S(2)}) collective-permute-start(bf16[4,128,1024]{2,1,0:T(8,128)(2,1)} %collective-permute-done.19.low_in.refs_3_), channel_id=1, source_target_pairs={{0,1},{1,0},{2,3},{3,2},{4,5},{5,4},{6,7},{7,6},{8,9},{9,8},{10,11... | collective-permute-start | bytes 3145736 | tf_op jit(solution)/shard_map/ppermute | solution.py:112
  219.8 39.1 %collective-permute-start.36 = (bf16[16,128,1024]{2,1,0:T(8,128)(2,1)}, bf16[16,128,1024]{2,1,0:T(8,128)(2,1)}, u32[]{:S(2)}, u32[]{:S(2)}) collective-permute-start(bf16[16,128,1024]{2,1,0:T(8,128)(2,1)} %get-tuple-element.239), channel_id=1, source_target_pairs={{0,1},{1,0},{2,3},{3,2},{4,5},{5,4},{6,7},{7,6},{8,9},{9,8},{10,11... | collective-permute-start | bytes 12582920 | tf_op jit(solution)/shard_map/ppermute | solution.py:112
  281.1 25.4 %collective-permute-start.39 = (bf16[16,160,1024]{2,1,0:T(8,128)(2,1)}, bf16[16,160,1024]{2,1,0:T(8,128)(2,1)}, u32[]{:S(2)}, u32[]{:S(2)}) collective-permute-start(bf16[16,160,1024]{2,1,0:T(8,128)(2,1)} %get-tuple-element.255), channel_id=1, source_target_pairs={{0,1},{1,0},{2,3},{3,2},{4,5},{5,4},{6,7},{7,6},{8,9},{9,8},{10,11... | collective-permute-start | bytes 15728648 | tf_op jit(solution)/shard_map/ppermute | solution.py:112
  285.8 25.9 %collective-permute-start.40 = (bf16[4,128,1024]{2,1,0:T(8,128)(2,1)}, bf16[4,128,1024]{2,1,0:T(8,128)(2,1)}, u32[]{:S(2)}, u32[]{:S(2)}) collective-permute-start(bf16[4,128,1024]{2,1,0:T(8,128)(2,1)} %get-tuple-element.260), channel_id=1, source_target_pairs={{0,2},{1,3},{2,0},{3,1},{4,6},{5,7},{6,4},{7,5},{8,10},{9,11},{10,... | collective-permute-start | bytes 3145736 | tf_op jit(solution)/shard_map/ppermute | solution.py:112
  287.0 25.6 %collective-permute-start.41 = (bf16[4,128,1024]{2,1,0:T(8,128)(2,1)}, bf16[4,128,1024]{2,1,0:T(8,128)(2,1)}, u32[]{:S(2)}, u32[]{:S(2)}) collective-permute-start(bf16[4,128,1024]{2,1,0:T(8,128)(2,1)} %get-tuple-element.261), channel_id=1, source_target_pairs={{0,4},{1,5},{2,6},{3,7},{4,0},{5,1},{6,2},{7,3},{8,12},{9,13},{10,... | collective-permute-start | bytes 3145736 | tf_op jit(solution)/shard_map/ppermute | solution.py:112
  309.2 35.6 %collective-permute-start.42 = (bf16[2,160,1024]{2,1,0:T(8,128)(2,1)}, bf16[2,160,1024]{2,1,0:T(8,128)(2,1)}, u32[]{:S(2)}, u32[]{:S(2)}) collective-permute-start(bf16[2,160,1024]{2,1,0:T(8,128)(2,1)} %get-tuple-element.269), channel_id=1, source_target_pairs={{0,2},{1,3},{2,0},{3,1},{4,6},{5,7},{6,4},{7,5},{8,10},{9,11},{10,... | collective-permute-start | bytes 1966088 | tf_op jit(solution)/shard_map/ppermute | solution.py:112
  310.7 34.0 %collective-permute-start.43 = (bf16[2,160,1024]{2,1,0:T(8,128)(2,1)}, bf16[2,160,1024]{2,1,0:T(8,128)(2,1)}, u32[]{:S(2)}, u32[]{:S(2)}) collective-permute-start(bf16[2,160,1024]{2,1,0:T(8,128)(2,1)} %get-tuple-element.270), channel_id=1, source_target_pairs={{0,4},{1,5},{2,6},{3,7},{4,0},{5,1},{6,2},{7,3},{8,12},{9,13},{10,... | collective-permute-start | bytes 1966088 | tf_op jit(solution)/shard_map/ppermute | solution.py:112
  315.5 29.2 %collective-permute-start.44 = (bf16[1,128,1024]{2,1,0:T(8,128)(2,1)}, bf16[1,128,1024]{2,1,0:T(8,128)(2,1)}, u32[]{:S(2)}, u32[]{:S(2)}) collective-permute-start(bf16[1,128,1024]{2,1,0:T(8,128)(2,1)} %get-tuple-element.275), channel_id=1, source_target_pairs={{0,16},{1,17},{2,18},{3,19},{4,20},{5,21},{6,22},{7,23},{8,24},{9,... | collective-permute-start | bytes 786440 | tf_op jit(solution)/shard_map/ppermute | solution.py:112
  349.8 34.0 %collective-permute-start.50 = (bf16[4,160,1024]{2,1,0:T(8,128)(2,1)}, bf16[4,160,1024]{2,1,0:T(8,128)(2,1)}, u32[]{:S(2)}, u32[]{:S(2)}) collective-permute-start(bf16[4,160,1024]{2,1,0:T(8,128)(2,1)} %get-tuple-element.290), channel_id=1, source_target_pairs={{0,2},{1,3},{2,0},{3,1},{4,6},{5,7},{6,4},{7,5},{8,10},{9,11},{10,... | collective-permute-start | bytes 3932168 | tf_op jit(solution)/shard_map/ppermute | solution.py:112
  350.6 33.2 %collective-permute-start.51 = (bf16[4,160,1024]{2,1,0:T(8,128)(2,1)}, bf16[4,160,1024]{2,1,0:T(8,128)(2,1)}, u32[]{:S(2)}, u32[]{:S(2)}) collective-permute-start(bf16[4,160,1024]{2,1,0:T(8,128)(2,1)} %get-tuple-element.291), channel_id=1, source_target_pairs={{0,4},{1,5},{2,6},{3,7},{4,0},{5,1},{6,2},{7,3},{8,12},{9,13},{10,... | collective-permute-start | bytes 3932168 | tf_op jit(solution)/shard_map/ppermute | solution.py:112
  (72 other events, 974.2 us)

commit v5 on v4

--- a/solution.py
+++ b/solution.py
@@ -114,32 +114,52 @@
     def gather_far(self, shard):
         return [shard] + [self.swap(shard, mask) for mask in self.masks(self.outer)]
 
-    def stacked(self, parts):
-        return ([0] + self.masks(self.outer), jnp.stack(parts))
+    def stacked(self, parts, me):
+        low = self.bits - len(self.outer)
+        masks = [mask >> low for mask in [0] + self.masks(self.outer)]
+        count, shape = len(parts), parts[0].shape
+
+        def body(me_ref, *refs):
+            step, out_ref = pl.program_id(0), refs[-1]
+            for mask, ref in zip(masks, refs):
+
+                @pl.when(step == me_ref[0] >> low ^ mask)
+                def _():
+                    out_ref[0] = ref[...]
+
+        whole = pl.BlockSpec(shape, lambda i: (0, 0))
+        return pl.pallas_call(
+            body,
+            grid=(count,),
+            in_specs=[pl.BlockSpec(memory_space=pltpu.SMEM)] + [whole] * count,
+            out_specs=pl.BlockSpec((1,) + shape, lambda i: (i, 0, 0)),
+            out_shape=jax.ShapeDtypeStruct((count,) + shape, parts[0].dtype),
+            compiler_params=pltpu.CompilerParams(vmem_limit_bytes=16 << 20),
+            cost_estimate=pl.CostEstimate(flops=1000, bytes_accessed=1000, transcendentals=0),
+            name="stacked",
+        )(me.reshape(1), *parts)
 
     def gather_near(self, own):
-        sources, array = own
         return [
-            [(mask, self.swap(array, mask)) for mask in self.masks(group)]
+            [(mask, self.swap(own, mask)) for mask in self.masks(group)]
             for group in (self.near, self.middle)
         ]
 
     def gather_corner(self, own, near):
-        sources, half = own[0], len(own[0]) // 2
-        pieces, corners, sent = [own], [], []
+        half = own.shape[0] // 2
+        pieces, corners, sent = [(0, 0, own)], [], []
         for group in near:
-            pieces += [([s ^ mask for s in sources], array) for mask, array in group]
+            pieces += [(0, mask, array) for mask, array in group]
         for mask_x, array_x in near[0]:
             for mask_y, array_y in near[1]:
                 low, high = halves(array_y, array_x)
                 sent += [low, high]
-                corner = mask_x ^ mask_y
-                corners.append(([s ^ corner for s in sources[:half]], self.swap(low, mask_x)))
-                corners.append(([s ^ corner for s in sources[half:]], self.swap(high, mask_y)))
+                corners.append((0, mask_x ^ mask_y, self.swap(low, mask_x)))
+                corners.append((half, mask_x ^ mask_y, self.swap(high, mask_y)))
         return pieces, corners, sent
 
     def gather_core(self, pieces):
-        return pieces + [([s ^ 1 for s in own], self.swap(array, 1)) for own, array in pieces]
+        return pieces + [(first, mask ^ 1, self.swap(array, 1)) for first, mask, array in pieces]
 
     def inner_masks(self):
         near, middle = self.masks(self.near), self.masks(self.middle)
@@ -249,32 +269,39 @@
     def __init__(self, net, me, wanted):
         self.arrays, self.plans, self.shapes = [], [], []
         seen = {}
+        outer = 1 << len(net.outer)
+        low = net.n // outer
+        self.low = low
         for pieces, places, rows in wanted:
             places = (places,) if isinstance(places, int) else tuple(places)
-            columns = pieces[0][1].shape[-1]
+            columns = pieces[0][2].shape[-1]
             plan = []
             if rows % 16:
                 blocks = [
-                    jnp.concatenate([array[:, place : place + rows] for _, array in pieces])
+                    jnp.concatenate([array[:, place : place + rows] for _, _, array in pieces])
                     for place in places
                 ]
                 blocks = jnp.concatenate(blocks, axis=2)
-                order = jnp.asarray([s for own, _ in pieces for s in own], jnp.int32)
-                spot = jnp.zeros((net.n,), jnp.int32).at[order ^ me].set(jnp.arange(net.n))
-                whole = blocks[spot].reshape(net.n * rows // 16, 16, len(places) * columns)
+                order = [
+                    (first + j) * low + (me % low ^ mask)
+                    for first, mask, array in pieces
+                    for j in range(array.shape[0])
+                ]
+                spot = jnp.zeros((net.n,), jnp.int32).at[jnp.stack(order)].set(jnp.arange(net.n))
+                whole = blocks[spot].reshape(outer, low * rows // 16, 16, len(places) * columns)
                 plan.append((len(self.arrays), None, None, None))
                 self.arrays.append(whole)
                 self.shapes.append(whole.shape)
             else:
-                for own, array in pieces:
+                for first, mask, array in pieces:
                     if id(array) not in seen:
                         seen[id(array)] = len(self.arrays)
                         self.arrays.append(array)
-                    for j, source in enumerate(own):
-                        for k, place in enumerate(places):
-                            aim = pl.ds(k * columns, columns)
-                            plan.append((seen[id(array)], (j, pl.ds(place, rows)), source, aim))
-                self.shapes.append((net.n, rows, len(places) * columns))
+                    for k, place in enumerate(places):
+                        own = (slice(None), pl.ds(place, rows))
+                        aim = (pl.ds(first, array.shape[0]), pl.ds(k * columns, columns))
+                        plan.append((seen[id(array)], own, mask, aim))
+                self.shapes.append((outer, low, rows, len(places) * columns))
             self.plans.append(plan)
         self.slots = max(len(plan) for plan in self.plans)
 
@@ -285,11 +312,12 @@
 
     def copies(self, w, me, array_refs, held_ref, sems):
         found = []
-        for slot, (array, index, source, aim) in enumerate(self.plans[w]):
-            if index is None:
+        for slot, (array, own, mask, aim) in enumerate(self.plans[w]):
+            if own is None:
                 pair = (array_refs[array], held_ref)
             else:
-                pair = (array_refs[array].at[index], held_ref.at[me ^ source, :, aim])
+                spot = me % self.low ^ mask
+                pair = (array_refs[array].at[own], held_ref.at[aim[0], spot, :, aim[1]])
             found.append(pltpu.make_async_copy(*pair, sems.at[w, slot]))
         return found
 
@@ -520,7 +548,7 @@
         return sum_call(self.me, "end_sum", start, ins, None, outs, body, 4)
 
 
-def pack_body(sizes, me_ref, small_ref, *refs):
+def pack_body(sizes, me_ref, times_ref, small_ref, *refs):
     shards, out_ref = refs[:-1], refs[-1]
     start = 0
     for ref in shards:
@@ -542,8 +570,12 @@
     inner = spread(step, inner_size, lax.rem(place, width))
     row = lax.broadcasted_iota(jnp.int32, inner.shape, 0)
     inner = jnp.where(row == place // width, inner, 0.0)
-    times = spread(step + inner_size, steps, me * steps)
-    out_ref[start:] = jnp.concatenate([vectors, inner + times]).astype(BF16)
+    lane = lax.broadcasted_iota(jnp.int32, inner.shape, 1)
+    for j in range(steps):
+        time = times_ref[j]
+        digit = jnp.where(row == 4, time >> 6, jnp.where(row == 5, time & 63, 0))
+        inner += jnp.where(lane == me * steps + j, digit, 0).astype(F32)
+    out_ref[start:] = jnp.concatenate([vectors, inner]).astype(BF16)
 
 
 def pack(me, shards, vectors, inner, times):
@@ -554,17 +586,13 @@
         small += jnp.pad(vector.astype(F32)[None], ((line, 7 - line), (0, 256 - step)))
     rest = 256 - sizes[1] - step
     small += jnp.pad(inner.astype(F32)[None], ((0, 0), (step, rest)))
-    for line, digits in ((4, times // 64), (5, times % 64)):
-        left = step + sizes[1]
-        right = 256 - left - sizes[2]
-        small += jnp.pad(digits.astype(F32)[None], ((line, 7 - line), (left, right)))
     small = small.astype(BF16)
     rows = len(shards) * step + 16
     return call(
         functools.partial(pack_body, sizes),
         "pack",
         (1,),
-        [(me.reshape(1), SMEM_SPEC)]
+        [(me.reshape(1), SMEM_SPEC), (times, SMEM_SPEC)]
         + [(array, full_spec(array.shape)) for array in (small, *shards)],
         [((rows, width), BF16, full_spec((rows, width)))],
         [],
@@ -587,7 +615,7 @@
         weights.wait(0, me, arrays, tw, sems)
         temb_ref[...] = matmul(feats_ref[...], flat(tw[...]))
         weights.wait(4, me, arrays, lw, sems)
-        lines_ref[...] = jnp.sum(lw[...].astype(F32), axis=0)
+        lines_ref[...] = jnp.sum(lw[...].astype(F32), axis=(0, 1))
         for w, held in ((1, qw), (2, kw), (3, vw)):
             weights.wait(w, me, arrays, held, sems)
 
@@ -623,10 +651,12 @@
     )
 
 
-def same_document(segc_ref, segr_ref, bias_ref, block):
+def same_document(seg_ref, bias_ref, block):
     @pl.when(block == 0)
     def _():
-        bias_ref[...] = jnp.where(segc_ref[0] == segr_ref[0], 0.0, -1e30)
+        row = seg_ref[0].astype(F32)
+        column = jnp.transpose(jnp.broadcast_to(row, (128, row.shape[1])))[:, :1]
+        bias_ref[...] = jnp.where(column == row, 0.0, -1e30)
 
 
 def own_lanes(shape, head, head_dim):
@@ -634,8 +664,8 @@
     return (lanes // head_dim) == head
 
 
-def attend_body(head_dim, segc_ref, segr_ref, q_ref, k_ref, v_ref, out_ref, log_ref, bias_ref):
-    same_document(segc_ref, segr_ref, bias_ref, pl.program_id(1))
+def attend_body(head_dim, seg_ref, q_ref, k_ref, v_ref, out_ref, log_ref, bias_ref):
+    same_document(seg_ref, bias_ref, pl.program_id(1))
     queries, key_rows, values = q_ref[...], k_ref[...], v_ref[...]
     scale = 1.0 / math.sqrt(head_dim)
     per = queries.shape[1] // head_dim
@@ -655,9 +685,9 @@
 
 
 def attend_back_body(
-    head_dim, segc_ref, segr_ref, q_ref, k_ref, v_ref, log_ref, g_ref, gq_ref, gk_ref, gv_ref, sums_ref, rows_ref, bias_ref
+    head_dim, seg_ref, q_ref, k_ref, v_ref, log_ref, g_ref, gq_ref, gk_ref, gv_ref, sums_ref, rows_ref, bias_ref
 ):
-    same_document(segc_ref, segr_ref, bias_ref, pl.program_id(1))
+    same_document(seg_ref, bias_ref, pl.program_id(1))
     queries, key_rows, values, grads = q_ref[...], k_ref[...], v_ref[...], g_ref[...]
     scale = 1.0 / math.sqrt(head_dim)
     per = queries.shape[1] // head_dim
@@ -693,11 +723,10 @@
 
 def attention_args(segments, start, lanes, head_dim):
     row_length, per = segments.shape[1], lanes // head_dim
-    segc = pl.BlockSpec((1, row_length, 1), lambda i, j: (start + i, 0, 0))
-    segr = pl.BlockSpec((1, 1, row_length), lambda i, j: (start + i, 0, 0))
+    segs = pl.BlockSpec((1, 1, row_length), lambda i, j: (start + i, 0, 0))
     block = pl.BlockSpec((row_length, lanes), lambda i, j: (start + i, j))
     log_spec = pl.BlockSpec((1, 1, per, row_length), lambda i, j: (start + i, j, 0, 0))
-    return [(segments[:, :, None], segc), (segments[:, None, :], segr)], block, log_spec
+    return [(segments[:, None, :], segs)], block, log_spec
 
 
 def attend(queries, key_rows, values, segments, lanes=256):
@@ -794,10 +823,10 @@
     def _():
         weights.wait(1, me, arrays, iw, sems)
 
-    width, hidden = ow.shape[2], iw.shape[2]
+    width, hidden = ow.shape[3], iw.shape[3]
 
     def inner(start):
-        pre = matmul(low, flat(iw[:, :, start : start + chunk]))
+        pre = matmul(low, flat(iw[:, :, :, start : start + chunk]))
         line, place = 8 + start // width, start % width
         return pre + lines_ref[line : line + 1, place : place + chunk]
 
@@ -897,56 +926,67 @@
     )
 
 
-def ffn_back_body(weights, tile, row_length, chunk, me_ref, *refs):
+def ffn_back_body(weights, tile, row_length, me_ref, *refs):
     count = len(weights.arrays)
     arrays, refs = refs[:count], refs[count:]
     (gs_ref, gs_low_ref, slope_ref, normed_ref, spread_ref, lines_ref) = refs[:6]
     (gi_ref, gm_ref, gm_low_ref, gc_ref, ibg_ref, sums_ref, rows_ref) = refs[6:13]
-    uw, ow, iw, sems = refs[13:17]
+    uw, ow, iw, sems, held_ref = refs[13:18]
     me, step = me_ref[0], pl.program_id(0)
+    last = pl.num_programs(0) - 1
 
     @pl.when(step == 0)
     def _():
         for w, held in ((0, uw), (2, iw), (1, ow)):
             weights.start(w, me, arrays, held, sems)
+        sums_ref[...] = jnp.zeros_like(sums_ref)
+        rows_ref[...] = jnp.zeros_like(rows_ref)
+        ibg_ref[...] = jnp.zeros_like(ibg_ref)
         weights.wait(0, me, arrays, uw, sems)
 
-    unit = uw.shape[1]
-    hidden = iw.shape[2]
-    for start in range(0, hidden, chunk):
-        columns = slice(start, start + chunk)
-        held = flat(uw[start // unit : (start + chunk) // unit])
-        grad_active = matmul_right(gs_low_ref[...], held)
-        gi_ref[:, columns] = (grad_active * slope_ref[:, columns].astype(F32)).astype(BF16)
+    def through_hidden(first_time=False):
+        part = gi_ref.shape[1] // uw.shape[0]
+        for z in range(uw.shape[0]):
+            columns = slice(z * part, (z + 1) * part)
+            grad_active = matmul_right(gs_low_ref[...], flat(uw[z]))
+            gi = (grad_active * slope_ref[:, columns].astype(F32)).astype(BF16)
+            gi_ref[:, columns] = gi
+            ibg_ref[:, columns] += jnp.sum(gi.astype(F32), axis=0, keepdims=True)
+        if first_time:
+            weights.wait(2, me, arrays, iw, sems)
+        return gs_ref[...] + matmul_right(gi_ref[...], flat(iw[...]))
+
+    def through_norm(grad_first):
+        normed = normed_ref[...]
+        grad_mixed = norm_back(grad_first * lines_ref[4:5], normed, spread_ref[...])
+        gm_ref[...] = grad_mixed
+        low = grad_mixed.astype(BF16)
+        gm_low_ref[...] = low
+        row = pl.ds((step - 1) * tile // row_length, 1)
+        rows_ref[row, :] += jnp.sum(grad_mixed, axis=0, keepdims=True)
+        values = {2: low.astype(F32), 4: grad_first * normed, 5: grad_first}
+        for line, value in values.items():
+            sums_ref[line : line + 1] += jnp.sum(value, axis=0, keepdims=True)
+        gc_ref[...] = matmul_right(low, flat(ow[...])).astype(BF16)
 
     @pl.when(step == 0)
     def _():
-        weights.wait(2, me, arrays, iw, sems)
-
-    grad_first = gs_ref[...] + matmul_right(gi_ref[...], flat(iw[...]))
-    add_to(ibg_ref, gi_ref[...].astype(F32), step)
-    normed = normed_ref[...]
-    grad_mixed = norm_back(grad_first * lines_ref[4:5], normed, spread_ref[...])
-    gm_ref[...] = grad_mixed
-
-    @pl.when(step == 0)
+        held_ref[...] = through_hidden(True)
+        weights.wait(1, me, arrays, ow, sems)
+
+    @pl.when((step > 0) & (step < last))
     def _():
-        rows_ref[...] = jnp.zeros_like(rows_ref)
-
-    row = pl.ds(step * tile // row_length, 1)
-    rows_ref[row, :] += jnp.sum(grad_mixed, axis=0, keepdims=True)
-    low = grad_mixed.astype(BF16)
-    gm_low_ref[...] = low
-    add_lines(sums_ref, {2: low.astype(F32), 4: grad_first * normed, 5: grad_first}, step)
-
-    @pl.when(step == 0)
+        grad_first = held_ref[...]
+        later = through_hidden()
+        through_norm(grad_first)
+        held_ref[...] = later
+
+    @pl.when(step == last)
     def _():
-        weights.wait(1, me, arrays, ow, sems)
-
-    gc_ref[...] = matmul_right(low, flat(ow[...])).astype(BF16)
-
-
-def ffn_back(net, me, flow_u, flow_io, gs, gs_low, slope, normed, spread, lines, row_length, tile=256, chunk=1024):
+        through_norm(held_ref[...])
+
+
+def ffn_back(net, me, flow_u, flow_io, gs, gs_low, slope, normed, spread, lines, row_length, tile=256):
     tokens, width = gs.shape
     hidden = slope.shape[1]
     r = width // net.n
@@ -960,30 +1000,37 @@
         ],
     )
     tile = min(tile, row_length)
-    tiled, wide = tile_spec(tile, width), tile_spec(tile, hidden)
+    steps = tokens // tile
+
+    def ahead(columns):
+        return pl.BlockSpec((tile, columns), lambda i: (jnp.minimum(i, steps - 1), 0))
+
+    def behind(columns):
+        return pl.BlockSpec((tile, columns), lambda i: (jnp.maximum(i - 1, 0), 0))
+
     ins = (
         [(me.reshape(1), SMEM_SPEC)]
         + [(array, ANY_SPEC) for array in weights.arrays]
-        + [(gs, tiled), (gs_low, tiled), (slope, wide), (normed, tiled)]
-        + [(spread, tile_spec(tile, 1)), (lines, full_spec(lines.shape))]
+        + [(gs, ahead(width)), (gs_low, ahead(width)), (slope, ahead(hidden))]
+        + [(normed, behind(width)), (spread, behind(1)), (lines, full_spec(lines.shape))]
     )
     outs = [
-        ((tokens, hidden), BF16, wide),
-        ((tokens, width), F32, tiled),
-        ((tokens, width), BF16, tiled),
-        ((tokens, width), BF16, tiled),
+        ((tokens, hidden), BF16, ahead(hidden)),
+        ((tokens, width), F32, behind(width)),
+        ((tokens, width), BF16, behind(width)),
+        ((tokens, width), BF16, behind(width)),
         ((1, hidden), F32, full_spec((1, hidden))),
         ((8, width), F32, full_spec((8, width))),
         ((8, width), F32, full_spec((8, width))),
     ]
     return call(
-        functools.partial(ffn_back_body, weights, tile, row_length, chunk),
+        functools.partial(ffn_back_body, weights, tile, row_length),
         "ffn_back",
-        (tokens // tile,),
+        (steps + 1,),
         ins,
         outs,
-        weights.scratch(),
-        38,
+        weights.scratch() + [pltpu.VMEM((tile, width), F32)],
+        36,
     )
 
 
@@ -1224,11 +1271,11 @@
     ]
     shard_io = after(jnp.concatenate([output_weight] + inner_blocks), far)
     far_io = net.gather_far(shard_io)
-    far = net.stacked(far)
+    far = net.stacked(far, me)
     near = net.gather_near(far)
     pieces, corners, _ = net.gather_corner(far, near)
     flow = net.gather_core(pieces)
-    far_io, corners, shard_u = after((net.stacked(far_io), corners, outer_weight), ())
+    far_io, corners, shard_u = after((net.stacked(far_io, me), corners, outer_weight), ())
     near_io = net.gather_near(far_io)
     flow += net.gather_core(corners)
     far_u = net.gather_far(after(shard_u, flow))
@@ -1239,7 +1286,7 @@
     temb, lines, stream_low, queries, key_rows, values = project(
         net, me, flow, feats_in, x, row_length
     )
-    far_u = net.stacked(after(far_u, queries))
+    far_u = net.stacked(after(far_u, queries), me)
     near_u = net.gather_near(far_u)
     near_io, queries = after((near_io, queries), far_u)
     pieces, corners, sent = net.gather_corner(far_io, near_io)
@@ -1337,11 +1384,12 @@
     for row in range(1, rows):
         (grad_stream,) = stream_back(net, me, *back, row, row_length, grad_stream)
     inner_sum.hold(grad_stream), outer_sum.hold(grad_stream)
-    output_weight_grad, inner_weight_grad = inner_sum.end([1, hidden // model_width], r)
-    (outer_weight_grad,) = outer_sum.end([1], outer_weight.shape[0])
     ends = after(ends, (grad_stream, inner_sum.received()))
     sources, ends = net.gather_round(sources, ends, net.masks(net.near))
     sent = stream_sum.hold(grad_stream).far()
+    inner_sum.hold(sent), outer_sum.hold(sent)
+    output_weight_grad, inner_weight_grad = inner_sum.end([1, hidden // model_width], r)
+    (outer_weight_grad,) = outer_sum.end([1], outer_weight.shape[0])
     sources, ends = net.gather_round(sources, after(ends, sent), net.masks(net.middle))
     sources, ends = net.gather_round(
         sources, after(ends, stream_sum.received()), net.masks(net.outer)
@@ -1351,7 +1399,8 @@
         stream_sum, r, sizes
     )
     own = model_width // n
-    steps_all = (lines[12] * 64.0 + lines[13])[: n * rows]
+    steps_all = after(lines, grad_stream)
+    steps_all = (steps_all[12] * 64.0 + steps_all[13])[: n * rows]
     feats_own = own_features(steps_all, me * own, own).astype(BF16).astype(F32)
     time_weight_grad = lax.dot_general(
         feats_own,

time: 459 us -> 452 us (0.985)
  other arithmetic: 14 us -> 8.55 us
    pallas_call x13, Pallas kernels: 226 us -> 218 us  [call(): pl.pallas_call(run, grid=grid, in_specs=[spec for _, spec in ins] + [ANY_...]
    pallas_call x0 -> x3, Pallas kernels: none -> 4.68 us  [stacked(): pl.pallas_call(body, grid=(count,), in_specs=[pl.BlockSpec(memory_space=p...]
    another operation x6 -> x3, other arithmetic: 6.91 us -> 2.27 us  [the longest x3 4.63 us: stacked(): return ([0] + self.masks(self.outer), jnp.stack(parts))]
  transfers between devices with their start and end apart: 66 -> 66, of which waited for: 22 -> 25; matrix products, arithmetic and copies ran while one was open for 3% -> 2% of each run, Pallas kernels for 50% -> 50%
where the time goes in v5:
time: 452 us; the launch traced here: 444 us
  Pallas kernels  266 us (59%)
  starting transfers between devices  86.2 us (19%)
  waiting for transfers between devices  71.8 us (16%)
  local copies, waits for them, and re-layouts  8.91 us (2%)
  other arithmetic  8.55 us (2%)
    pallas_call x13, Pallas kernels, call(): pl.pallas_call(run, grid=grid, in_specs=[spec for _, spec in ins] + [ANY_...  218 us
    ppermute x66, starting transfers between devices, swap(): return lax.ppermute(array, 'fsdp', [(i, i ^ mask) for i in range(self.n)])  86.2 us
    ppermute x66, waiting for transfers between devices, swap(): return lax.ppermute(array, 'fsdp', [(i, i ^ mask) for i in range(self.n)])  71.8 us
    pallas_call x12, Pallas kernels, sum_call(): pl.pallas_call(body or functools.partial(sum_body, groups), grid_spec=gri...  39.4 us
  transfers between devices with their start and end apart: 66, of which 25 were waited for; matrix products, arithmetic and copies ran while one was open for 2% of the time, Pallas kernels for 50%

profile of v5, /device:TPU:0, one launch (start us, length us, event | category | flops | bytes accessed | tf_op | source)
XLA Modules:
  0.0 444.3 jit_solution(14724170478874150432)
XLA Ops:
  10.3 13.7 %collective-permute-done.refs_1_ = bf16[144,1024]{1,0:T(8,128)(2,1)S(1)} collective-permute-done((bf16[144,1024]{1,0:T(8,128)(2,1)}, bf16[144,1024]{1,0:T(8,128)(2,1)S(1)}, u32[]{:S(2)}, u32[]{:S(2)}) %collective-permute-start) | collective-permute-done | bytes 294944 | tf_op jit(solution)/shard_map/ppermute | solution.py:112
  24.0 5.8 %collective-permute-done.2.refs_3_ = bf16[144,1024]{1,0:T(8,128)(2,1)S(1)} collective-permute-done((bf16[144,1024]{1,0:T(8,128)(2,1)}, bf16[144,1024]{1,0:T(8,128)(2,1)S(1)}, u32[]{:S(2)}, u32[]{:S(2)}) %collective-permute-start.2) | collective-permute-done | bytes 294944 | tf_op jit(solution)/shard_map/ppermute | solution.py:112
  34.2 7.8 %collective-permute-start.3 = (bf16[160,1024]{1,0:T(8,128)(2,1)S(1)}, bf16[160,1024]{1,0:T(8,128)(2,1)S(1)}, u32[]{:S(2)}, u32[]{:S(2)}) collective-permute-start(bf16[160,1024]{1,0:T(8,128)(2,1)S(1)} %slice_dynamic-update-slice_fusion.refs_0_), channel_id=1, source_target_pairs={{0,16},{1,17},{2,18},{3,19},{4,20},{5,21},{6,22},{7,23},{8,24},{9,... | collective-permute-start | bytes 983048 | tf_op jit(solution)/shard_map/ppermute | solution.py:112
  43.5 14.4 %collective-permute-done.6.low_in.refs_3_ = bf16[4,144,1024]{2,1,0:T(8,128)(2,1)S(1)} collective-permute-done((bf16[4,144,1024]{2,1,0:T(8,128)(2,1)S(1)}, bf16[4,144,1024]{2,1,0:T(8,128)(2,1)S(1)}, u32[]{:S(2)}, u32[]{:S(2)}) %collective-permute-start.6) | collective-permute-done | bytes 1179680 | tf_op jit(solution)/shard_map/ppermute | solution.py:112
  66.7 5.6 %collective-permute-done.8.refs_7_ = bf16[2,144,1024]{2,1,0:T(8,128)(2,1)S(1)} collective-permute-done((bf16[2,144,1024]{2,1,0:T(8,128)(2,1)S(1)}, bf16[2,144,1024]{2,1,0:T(8,128)(2,1)S(1)}, u32[]{:S(2)}, u32[]{:S(2)}) %collective-permute-start.8) | collective-permute-done | bytes 589856 | tf_op jit(solution)/shard_map/ppermute | solution.py:112
  76.8 10.0 %collective-permute-start.15 = (bf16[128,1024]{1,0:T(8,128)(2,1)}, bf16[128,1024]{1,0:T(8,128)(2,1)}, u32[]{:S(2)}, u32[]{:S(2)}) collective-permute-start(bf16[128,1024]{1,0:T(8,128)(2,1)} %refs_0_.3), channel_id=1, source_target_pairs={{0,16},{1,17},{2,18},{3,19},{4,20},{5,21},{6,22},{7,23},{8,24},{9,... | collective-permute-start | bytes 786440 | tf_op jit(solution)/shard_map/ppermute | solution.py:112
  89.1 13.5 %project.1 = (f32[2,1024]{1,0:T(2,128)}, f32[16,1024]{1,0:T(8,128)}, bf16[1024,1024]{1,0:T(8,128)(2,1)}, bf16[1024,1024]{1,0:T(8,128)(2,1)}, bf16[1024,1024]{1,0:T(8,128)(2,1)}, /*index=5*/bf16[1024,1024]{1,0:T(8,128)(2,1)}) custom-call(s32[1]{0:T(128)} %bitcast.refs_0_.me_ref, bf16[4,144,1024]{2,1,0:T(8,128)(2,1)} %copy-done, ...), custom_call_target="tpu_custom_call" | custom-call | flops 280000004096 | bytes 700000000 | tf_op jit(solution)/shard_map/project/pallas_call | solution.py:355
  114.9 19.9 %attend.1 = (bf16[1024,1024]{1,0:T(8,128)(2,1)}, f32[2,4,4,512]{3,2,1,0:T(4,128)}) custom-call(s32[2,1,512]{2,1,0:T(1,128)} %refs_0_.6, bf16[1024,1024]{1,0:T(8,128)(2,1)} %get-tuple-element.227.refs_1_, bf16[1024,1024]{1,0:T(8,128)(2,1)} %get-tuple-element.228.refs_2_, bf16[1024,1024]{1,0:T(8,128)(2,1)} %get-tuple-element.229.refs_3_), custom_call_target="tpu_custom_call" | custom-call | flops 480000016384 | bytes 1200000000 | tf_op jit(solution)/shard_map/attend/pallas_call | solution.py:355
  138.6 7.9 %collective-permute-done.30.refs_7_.refs_17_ = bf16[2,160,1024]{2,1,0:T(8,128)(2,1)} collective-permute-done((bf16[2,160,1024]{2,1,0:T(8,128)(2,1)}, bf16[2,160,1024]{2,1,0:T(8,128)(2,1)}, u32[]{:S(2)}, u32[]{:S(2)}) %collective-permute-start.30) | collective-permute-done | bytes 655392 | tf_op jit(solution)/shard_map/ppermute | solution.py:112
  153.1 27.8 %ffn_in.1 = (bf16[1024,1024]{1,0:T(8,128)(2,1)}, f32[1024,1024]{1,0:T(8,128)}, f32[1024,1]{1,0:T(8,128)}, bf16[1024,4096]{1,0:T(8,128)(2,1)}, bf16[1024,4096]{1,0:T(8,128)(2,1)}) custom-call(s32[1]{0:T(128)} %bitcast.refs_0_.me_ref, bf16[4,160,1024]{2,1,0:T(8,128)(2,1)} %stacked.3.refs_1_.refs_11_, ...), custom_call_target="tpu_custom_call" | custom-call | flops 599999971328 | bytes 1500000000 | tf_op jit(solution)/shard_map/ffn_in/pallas_call | solution.py:355
  184.7 20.3 %ffn_out.1 = (bf16[1024,1024]{1,0:T(8,128)(2,1)}, f32[1024,1024]{1,0:T(8,128)}, bf16[1024,1024]{1,0:T(8,128)(2,1)}, f32[8,1024]{1,0:T(8,128)}) custom-call(s32[1]{0:T(128)} %bitcast.refs_0_.me_ref, bf16[4,128,1024]{2,1,0:T(8,128)(2,1)} %stacked.5.refs_1_, bf16[4,128,1024]{2,1,0:T(8,128)(2,1)} %collective-permute-done.18.high_in.refs_2_, ...), custom_call_target="tpu_custom_call" | custom-call | flops 399999991808 | bytes 1000000000 | tf_op jit(solution)/shard_map/ffn_out/pallas_call | solution.py:355
  205.0 13.1 %product.1 = (bf16[16,128,1024]{2,1,0:T(8,128)(2,1)}, bf16[16,128,1024]{2,1,0:T(8,128)(2,1)}) custom-call(s32[1]{0:T(128)} %bitcast.refs_0_.me_ref, bf16[1024,4096]{1,0:T(8,128)(2,1)} %get-tuple-element.247.refs_11_.refs_1_, bf16[1024,1024]{1,0:T(8,128)(2,1)} %get-tuple-element.251.refs_2_.refs_22_), custom_call_target="tpu_custom_call" | custom-call | flops 299999985664 | bytes 750000000 | tf_op jit(solution)/shard_map/product/pallas_call | solution.py:355
  218.3 33.1 %ffn_back.1 = (bf16[1024,4096]{1,0:T(8,128)(2,1)}, f32[1024,1024]{1,0:T(8,128)}, bf16[1024,1024]{1,0:T(8,128)(2,1)}, bf16[1024,1024]{1,0:T(8,128)(2,1)}, f32[1,4...) custom-call(s32[1]{0:T(128)} %bitcast.refs_0_.me_ref, bf16[4,128,1024]{2,1,0:T(8,128)(2,1)} %stacked.5.refs_1_, ...), custom_call_target="tpu_custom_call" | custom-call | flops 719999991808 | bytes 1800000000 | tf_op jit(solution)/shard_map/ffn_back/pallas_call | solution.py:355
  257.2 17.9 %inner_product.1 = (bf16[16,160,1024]{2,1,0:T(8,128)(2,1)}, bf16[16,160,1024]{2,1,0:T(8,128)(2,1)}) custom-call(s32[1]{0:T(128)} %bitcast.refs_0_.me_ref, bf16[1024,1024]{1,0:T(8,128)(2,1)} %get-tuple-element.241.refs_11_.refs_1_, bf16[1024,1024]{1,0:T(8,128)(2,1)} %get-tuple-element.261.refs_2_, bf16[1024,1024]{1,0:T(8,128)(2,1)} %get-tuple-element.267.refs_3_, ...), custom_call_target="tpu_custom_call" | custom-call | flops 359999995904 | bytes 900000000 | tf_op jit(solution)/shard_map/inner_product/pallas_call | solution.py:355
  275.0 4.6 %near_sum.3 = (bf16[4,128,1024]{2,1,0:T(8,128)(2,1)}, bf16[4,128,1024]{2,1,0:T(8,128)(2,1)}) custom-call(s32[1]{0:T(128)} %bitcast.refs_0_.me_ref, bf16[16,128,1024]{2,1,0:T(8,128)(2,1)} %get-tuple-element.377.refs_0_.refs_2_.refs_4_.refs_8_, bf16[16,128,1024]{2,1,0:T(8,128)(2,1)} %collective-permute-done.36.refs_1_.refs_3_.refs_5_.refs_9_, ...), custom_call_target="tpu_custom_call" | custom-call | flops 200000000 | bytes 500000 | tf_op jit(solution)/shard_map/near_sum/pallas_call | solution.py:400
  281.6 18.5 %attend_back.2 = (bf16[1024,1024]{1,0:T(8,128)(2,1)}, bf16[1024,1024]{1,0:T(8,128)(2,1)}, bf16[1024,1024]{1,0:T(8,128)(2,1)}, f32[8,1024]{1,0:T(8,128)}, f32[8,1024]{1,0:T(8,128)}) custom-call(s32[2,1,512]{2,1,0:T(1,128)} %refs_0_.6, bf16[1024,1024]{1,0:T(8,128)(2,1)} %get-tuple-element.227.refs_1_, bf16[1024,1024]{1,0:T(8,128)(2,1)} %get-tuple-element.228.refs_2_, ...), custom_call_target="tpu_custom_call" | custom-call | flops 380000010240 | bytes 950000000 | tf_op jit(solution)/shard_map/attend_back/pallas_call | solution.py:355
  309.7 5.8 %collective-permute-start.44 = (bf16[1,128,1024]{2,1,0:T(8,128)(2,1)}, bf16[1,128,1024]{2,1,0:T(8,128)(2,1)}, u32[]{:S(2)}, u32[]{:S(2)}) collective-permute-start(bf16[1,128,1024]{2,1,0:T(8,128)(2,1)} %get-tuple-element.290), channel_id=1, source_target_pairs={{0,16},{1,17},{2,18},{3,19},{4,20},{5,21},{6,22},{7,23},{8,24},{9,... | collective-permute-start | bytes 786440 | tf_op jit(solution)/shard_map/ppermute | solution.py:112
  318.7 18.8 %attend_back.3 = (bf16[1024,1024]{1,0:T(8,128)(2,1)}, bf16[1024,1024]{1,0:T(8,128)(2,1)}, bf16[1024,1024]{1,0:T(8,128)(2,1)}, f32[8,1024]{1,0:T(8,128)}, f32[8,1024]{1,0:T(8,128)}) custom-call(s32[2,1,512]{2,1,0:T(1,128)} %refs_0_.6, bf16[1024,1024]{1,0:T(8,128)(2,1)} %get-tuple-element.227.refs_1_, ...), custom_call_target="tpu_custom_call", output_to_operand_aliasing={{0}: (6, {}), {1}: (7, {}), {2}: (8, {})} | custom-call | flops 380000010240 | bytes 950000000 | tf_op jit(solution)/shard_map/attend_back/pallas_call | solution.py:355
  338.6 5.0 %near_sum.4 = (bf16[4,160,1024]{2,1,0:T(8,128)(2,1)}, bf16[4,160,1024]{2,1,0:T(8,128)(2,1)}) custom-call(s32[1]{0:T(128)} %bitcast.refs_0_.me_ref, bf16[16,160,1024]{2,1,0:T(8,128)(2,1)} %get-tuple-element.355.refs_0_.refs_2_.refs_4_.refs_8_, bf16[16,160,1024]{2,1,0:T(8,128)(2,1)} %collective-permute-done.39.refs_1_.refs_3_.refs_5_.refs_9_, ...), custom_call_target="tpu_custom_call" | custom-call | flops 200000000 | bytes 500000 | tf_op jit(solution)/shard_map/near_sum/pallas_call | solution.py:400
  346.8 11.7 %triple_product.1 = (bf16[16,104,1024]{2,1,0:T(8,128)(2,1)}, bf16[16,104,1024]{2,1,0:T(8,128)(2,1)}) custom-call(s32[1]{0:T(128)} %bitcast.refs_0_.me_ref, bf16[16,16,1024]{2,1,0:T(8,128)(2,1)} %bitcast.47, bf16[1024,1024]{1,0:T(8,128)(2,1)} %get-tuple-element.309.refs_2_, bf16[1024,1024]{1,0:T(8,128)(2,1)} %get-tuple-element.300.refs_3_.refs_12_, ...), custom_call_target="tpu_custom_call" | custom-call | flops 260000006144 | bytes 650000000 | tf_op jit(solution)/shard_map/triple_product/pallas_call | solution.py:355
  358.5 11.4 %stream_back.2 = (f32[1024,1024]{1,0:T(8,128)}, f32[8,1024]{1,0:T(8,128)}) custom-call(s32[1]{0:T(128)} %bitcast.refs_0_.me_ref, bf16[4,144,1024]{2,1,0:T(8,128)(2,1)} %copy-done, bf16[4,144,1024]{2,1,0:T(8,128)(2,1)} %copy-done.2, bf16[4,144,1024]{2,1,0:T(8,128)(2,1)} %copy-done.1, bf16[4,144,1024]{2,1,0:T(8,128)(2,1)} %copy-done.21, ...), custom_call_target="tpu_custom_call" | custom-call | flops 199999995904 | bytes 500000000 | tf_op jit(solution)/shard_map/stream_back/pallas_call | solution.py:355
  386.2 4.4 near_sum.5
  392.5 9.8 %stream_back.3 = f32[1024,1024]{1,0:T(8,128)} custom-call(s32[1]{0:T(128)} %bitcast.refs_0_.me_ref, bf16[4,144,1024]{2,1,0:T(8,128)(2,1)} %copy-done, bf16[4,144,1024]{2,1,0:T(8,128)(2,1)} %copy-done.2, bf16[4,144,1024]{2,1,0:T(8,128)(2,1)} %copy-done.1, bf16[4,144,1024]{2,1,0:T(8,128)(2,1)} %copy-done.21, ...), custom_call_target="tpu_custom_call", output_to_operand_aliasing={{}: (15, {})} | custom-call | flops 199999995904 | bytes 500000000 | tf_op jit(solution)/shard_map/stream_back/pallas_call | solution.py:355
  424.6 7.9 %collective-permute-start.63 = (f32[8,2,1024]{2,1,0:T(2,128)S(1)}, f32[8,2,1024]{2,1,0:T(2,128)S(1)}, u32[]{:S(2)}, u32[]{:S(2)}) collective-permute-start(f32[8,2,1024]{2,1,0:T(2,128)S(1)} %pad_maximum_fusion.1), channel_id=1, source_target_pairs={{0,16},{1,17},{2,18},{3,19},{4,20},{5,21},{6,22},{7,23},{8,24},{9,... | collective-permute-start | bytes 196616 | tf_op jit(solution)/shard_map/ppermute | solution.py:112
  (238 shorter events, 134.0 us)
Async XLA Ops:
  31.0 26.9 %collective-permute-start.6 = (bf16[4,144,1024]{2,1,0:T(8,128)(2,1)S(1)}, bf16[4,144,1024]{2,1,0:T(8,128)(2,1)S(1)}, u32[]{:S(2)}, u32[]{:S(2)}) collective-permute-start(bf16[4,144,1024]{2,1,0:T(8,128)(2,1)S(1)} %stacked.4.refs_1_), channel_id=1, source_target_pairs={{0,4},{1,5},{2,6},{3,7},{4,0},{5,1},{6,2},{7,3},{8,12},{9,13},{10,... | collective-permute-start | bytes 3538952 | tf_op jit(solution)/shard_map/ppermute | solution.py:112
  32.6 26.5 %collective-permute-start.7 = (bf16[4,144,1024]{2,1,0:T(8,128)(2,1)S(1)}, bf16[4,144,1024]{2,1,0:T(8,128)(2,1)S(1)}, u32[]{:S(2)}, u32[]{:S(2)}) collective-permute-start(bf16[4,144,1024]{2,1,0:T(8,128)(2,1)S(1)} %stacked.4.refs_1_), channel_id=1, source_target_pairs={{0,2},{1,3},{2,0},{3,1},{4,6},{5,7},{6,4},{7,5},{8,10},{9,11},{10,... | collective-permute-start | bytes 3538952 | tf_op jit(solution)/shard_map/ppermute | solution.py:112
  34.2 29.6 %collective-permute-start.3 = (bf16[160,1024]{1,0:T(8,128)(2,1)S(1)}, bf16[160,1024]{1,0:T(8,128)(2,1)S(1)}, u32[]{:S(2)}, u32[]{:S(2)}) collective-permute-start(bf16[160,1024]{1,0:T(8,128)(2,1)S(1)} %slice_dynamic-update-slice_fusion.refs_0_), channel_id=1, source_target_pairs={{0,16},{1,17},{2,18},{3,19},{4,20},{5,21},{6,22},{7,23},{8,24},{9,... | collective-permute-start | bytes 983048 | tf_op jit(solution)/shard_map/ppermute | solution.py:112
  74.8 36.3 %collective-permute-start.20 = (bf16[4,160,1024]{2,1,0:T(8,128)(2,1)}, bf16[4,160,1024]{2,1,0:T(8,128)(2,1)}, u32[]{:S(2)}, u32[]{:S(2)}) collective-permute-start(bf16[4,160,1024]{2,1,0:T(8,128)(2,1)} %stacked.3.refs_1_.refs_11_), channel_id=1, source_target_pairs={{0,2},{1,3},{2,0},{3,1},{4,6},{5,7},{6,4},{7,5},{8,10},{9,11},{10,... | collective-permute-start | bytes 3932168 | tf_op jit(solution)/shard_map/ppermute | solution.py:112
  75.3 35.7 %collective-permute-start.21 = (bf16[4,160,1024]{2,1,0:T(8,128)(2,1)}, bf16[4,160,1024]{2,1,0:T(8,128)(2,1)}, u32[]{:S(2)}, u32[]{:S(2)}) collective-permute-start(bf16[4,160,1024]{2,1,0:T(8,128)(2,1)} %stacked.3.refs_1_.refs_11_), channel_id=1, source_target_pairs={{0,4},{1,5},{2,6},{3,7},{4,0},{5,1},{6,2},{7,3},{8,12},{9,13},{10,... | collective-permute-start | bytes 3932168 | tf_op jit(solution)/shard_map/ppermute | solution.py:112
  76.8 25.8 %collective-permute-start.15 = (bf16[128,1024]{1,0:T(8,128)(2,1)}, bf16[128,1024]{1,0:T(8,128)(2,1)}, u32[]{:S(2)}, u32[]{:S(2)}) collective-permute-start(bf16[128,1024]{1,0:T(8,128)(2,1)} %refs_0_.3), channel_id=1, source_target_pairs={{0,16},{1,17},{2,18},{3,19},{4,20},{5,21},{6,22},{7,23},{8,24},{9,... | collective-permute-start | bytes 786440 | tf_op jit(solution)/shard_map/ppermute | solution.py:112
  108.6 26.4 %collective-permute-start.18 = (bf16[4,128,1024]{2,1,0:T(8,128)(2,1)}, bf16[4,128,1024]{2,1,0:T(8,128)(2,1)}, u32[]{:S(2)}, u32[]{:S(2)}) collective-permute-start(bf16[4,128,1024]{2,1,0:T(8,128)(2,1)} %stacked.5.refs_1_), channel_id=1, source_target_pairs={{0,2},{1,3},{2,0},{3,1},{4,6},{5,7},{6,4},{7,5},{8,10},{9,11},{10,... | collective-permute-start | bytes 3145736 | tf_op jit(solution)/shard_map/ppermute | solution.py:112
  109.6 26.4 %collective-permute-start.19 = (bf16[4,128,1024]{2,1,0:T(8,128)(2,1)}, bf16[4,128,1024]{2,1,0:T(8,128)(2,1)}, u32[]{:S(2)}, u32[]{:S(2)}) collective-permute-start(bf16[4,128,1024]{2,1,0:T(8,128)(2,1)} %stacked.5.refs_1_), channel_id=1, source_target_pairs={{0,4},{1,5},{2,6},{3,7},{4,0},{5,1},{6,2},{7,3},{8,12},{9,13},{10,... | collective-permute-start | bytes 3145736 | tf_op jit(solution)/shard_map/ppermute | solution.py:112
  113.2 33.3 %collective-permute-start.30 = (bf16[2,160,1024]{2,1,0:T(8,128)(2,1)}, bf16[2,160,1024]{2,1,0:T(8,128)(2,1)}, u32[]{:S(2)}, u32[]{:S(2)}) collective-permute-start(bf16[2,160,1024]{2,1,0:T(8,128)(2,1)} %get-tuple-element.225), channel_id=1, source_target_pairs={{0,2},{1,3},{2,0},{3,1},{4,6},{5,7},{6,4},{7,5},{8,10},{9,11},{10,... | collective-permute-start | bytes 1966088 | tf_op jit(solution)/shard_map/ppermute | solution.py:112
  113.7 32.9 %collective-permute-start.31 = (bf16[2,160,1024]{2,1,0:T(8,128)(2,1)}, bf16[2,160,1024]{2,1,0:T(8,128)(2,1)}, u32[]{:S(2)}, u32[]{:S(2)}) collective-permute-start(bf16[2,160,1024]{2,1,0:T(8,128)(2,1)} %get-tuple-element.226), channel_id=1, source_target_pairs={{0,4},{1,5},{2,6},{3,7},{4,0},{5,1},{6,2},{7,3},{8,12},{9,13},{10,... | collective-permute-start | bytes 1966088 | tf_op jit(solution)/shard_map/ppermute | solution.py:112
  149.8 33.7 %collective-permute-start.22 = (bf16[4,128,1024]{2,1,0:T(8,128)(2,1)}, bf16[4,128,1024]{2,1,0:T(8,128)(2,1)}, u32[]{:S(2)}, u32[]{:S(2)}) collective-permute-start(bf16[4,128,1024]{2,1,0:T(8,128)(2,1)} %stacked.5.refs_1_), channel_id=1, source_target_pairs={{0,1},{1,0},{2,3},{3,2},{4,5},{5,4},{6,7},{7,6},{8,9},{9,8},{10,11... | collective-permute-start | bytes 3145736 | tf_op jit(solution)/shard_map/ppermute | solution.py:112
  150.0 30.9 %collective-permute-start.25 = (bf16[2,128,1024]{2,1,0:T(8,128)(2,1)}, bf16[2,128,1024]{2,1,0:T(8,128)(2,1)}, u32[]{:S(2)}, u32[]{:S(2)}) collective-permute-start(bf16[2,128,1024]{2,1,0:T(8,128)(2,1)} %get-tuple-element.233), channel_id=1, source_target_pairs={{0,2},{1,3},{2,0},{3,1},{4,6},{5,7},{6,4},{7,5},{8,10},{9,11},{10,... | collective-permute-start | bytes 1572872 | tf_op jit(solution)/shard_map/ppermute | solution.py:112
  151.6 29.4 %collective-permute-start.26 = (bf16[2,128,1024]{2,1,0:T(8,128)(2,1)}, bf16[2,128,1024]{2,1,0:T(8,128)(2,1)}, u32[]{:S(2)}, u32[]{:S(2)}) collective-permute-start(bf16[2,128,1024]{2,1,0:T(8,128)(2,1)} %get-tuple-element.234), channel_id=1, source_target_pairs={{0,4},{1,5},{2,6},{3,7},{4,0},{5,1},{6,2},{7,3},{8,12},{9,13},{10,... | collective-permute-start | bytes 1572872 | tf_op jit(solution)/shard_map/ppermute | solution.py:112
  151.9 31.6 %collective-permute-start.23 = (bf16[4,128,1024]{2,1,0:T(8,128)(2,1)}, bf16[4,128,1024]{2,1,0:T(8,128)(2,1)}, u32[]{:S(2)}, u32[]{:S(2)}) collective-permute-start(bf16[4,128,1024]{2,1,0:T(8,128)(2,1)} %collective-permute-done.18.high_in.refs_2_), channel_id=1, source_target_pairs={{0,1},{1,0},{2,3},{3,2},{4,5},{5,4},{6,7},{7,6},{8,9},{9,8},{10,11... | collective-permute-start | bytes 3145736 | tf_op jit(solution)/shard_map/ppermute | solution.py:112
  151.9 31.6 %collective-permute-start.24 = (bf16[4,128,1024]{2,1,0:T(8,128)(2,1)}, bf16[4,128,1024]{2,1,0:T(8,128)(2,1)}, u32[]{:S(2)}, u32[]{:S(2)}) collective-permute-start(bf16[4,128,1024]{2,1,0:T(8,128)(2,1)} %collective-permute-done.19.low_in.refs_3_), channel_id=1, source_target_pairs={{0,1},{1,0},{2,3},{3,2},{4,5},{5,4},{6,7},{7,6},{8,9},{9,8},{10,11... | collective-permute-start | bytes 3145736 | tf_op jit(solution)/shard_map/ppermute | solution.py:112
  218.1 34.6 %collective-permute-start.36 = (bf16[16,128,1024]{2,1,0:T(8,128)(2,1)}, bf16[16,128,1024]{2,1,0:T(8,128)(2,1)}, u32[]{:S(2)}, u32[]{:S(2)}) collective-permute-start(bf16[16,128,1024]{2,1,0:T(8,128)(2,1)} %get-tuple-element.254), channel_id=1, source_target_pairs={{0,1},{1,0},{2,3},{3,2},{4,5},{5,4},{6,7},{7,6},{8,9},{9,8},{10,11... | collective-permute-start | bytes 12582920 | tf_op jit(solution)/shard_map/ppermute | solution.py:112
  275.0 25.1 %collective-permute-start.39 = (bf16[16,160,1024]{2,1,0:T(8,128)(2,1)}, bf16[16,160,1024]{2,1,0:T(8,128)(2,1)}, u32[]{:S(2)}, u32[]{:S(2)}) collective-permute-start(bf16[16,160,1024]{2,1,0:T(8,128)(2,1)} %get-tuple-element.270), channel_id=1, source_target_pairs={{0,1},{1,0},{2,3},{3,2},{4,5},{5,4},{6,7},{7,6},{8,9},{9,8},{10,11... | collective-permute-start | bytes 15728648 | tf_op jit(solution)/shard_map/ppermute | solution.py:112
  279.6 25.9 %collective-permute-start.40 = (bf16[4,128,1024]{2,1,0:T(8,128)(2,1)}, bf16[4,128,1024]{2,1,0:T(8,128)(2,1)}, u32[]{:S(2)}, u32[]{:S(2)}) collective-permute-start(bf16[4,128,1024]{2,1,0:T(8,128)(2,1)} %get-tuple-element.275), channel_id=1, source_target_pairs={{0,2},{1,3},{2,0},{3,1},{4,6},{5,7},{6,4},{7,5},{8,10},{9,11},{10,... | collective-permute-start | bytes 3145736 | tf_op jit(solution)/shard_map/ppermute | solution.py:112
  281.2 25.6 %collective-permute-start.41 = (bf16[4,128,1024]{2,1,0:T(8,128)(2,1)}, bf16[4,128,1024]{2,1,0:T(8,128)(2,1)}, u32[]{:S(2)}, u32[]{:S(2)}) collective-permute-start(bf16[4,128,1024]{2,1,0:T(8,128)(2,1)} %get-tuple-element.276), channel_id=1, source_target_pairs={{0,4},{1,5},{2,6},{3,7},{4,0},{5,1},{6,2},{7,3},{8,12},{9,13},{10,... | collective-permute-start | bytes 3145736 | tf_op jit(solution)/shard_map/ppermute | solution.py:112
  302.8 35.8 %collective-permute-start.42 = (bf16[2,160,1024]{2,1,0:T(8,128)(2,1)}, bf16[2,160,1024]{2,1,0:T(8,128)(2,1)}, u32[]{:S(2)}, u32[]{:S(2)}) collective-permute-start(bf16[2,160,1024]{2,1,0:T(8,128)(2,1)} %get-tuple-element.284), channel_id=1, source_target_pairs={{0,2},{1,3},{2,0},{3,1},{4,6},{5,7},{6,4},{7,5},{8,10},{9,11},{10,... | collective-permute-start | bytes 1966088 | tf_op jit(solution)/shard_map/ppermute | solution.py:112
  304.2 34.4 %collective-permute-start.43 = (bf16[2,160,1024]{2,1,0:T(8,128)(2,1)}, bf16[2,160,1024]{2,1,0:T(8,128)(2,1)}, u32[]{:S(2)}, u32[]{:S(2)}) collective-permute-start(bf16[2,160,1024]{2,1,0:T(8,128)(2,1)} %get-tuple-element.285), channel_id=1, source_target_pairs={{0,4},{1,5},{2,6},{3,7},{4,0},{5,1},{6,2},{7,3},{8,12},{9,13},{10,... | collective-permute-start | bytes 1966088 | tf_op jit(solution)/shard_map/ppermute | solution.py:112
  309.7 28.8 %collective-permute-start.44 = (bf16[1,128,1024]{2,1,0:T(8,128)(2,1)}, bf16[1,128,1024]{2,1,0:T(8,128)(2,1)}, u32[]{:S(2)}, u32[]{:S(2)}) collective-permute-start(bf16[1,128,1024]{2,1,0:T(8,128)(2,1)} %get-tuple-element.290), channel_id=1, source_target_pairs={{0,16},{1,17},{2,18},{3,19},{4,20},{5,21},{6,22},{7,23},{8,24},{9,... | collective-permute-start | bytes 786440 | tf_op jit(solution)/shard_map/ppermute | solution.py:112
  343.6 33.0 %collective-permute-start.50 = (bf16[4,160,1024]{2,1,0:T(8,128)(2,1)}, bf16[4,160,1024]{2,1,0:T(8,128)(2,1)}, u32[]{:S(2)}, u32[]{:S(2)}) collective-permute-start(bf16[4,160,1024]{2,1,0:T(8,128)(2,1)} %get-tuple-element.305), channel_id=1, source_target_pairs={{0,2},{1,3},{2,0},{3,1},{4,6},{5,7},{6,4},{7,5},{8,10},{9,11},{10,... | collective-permute-start | bytes 3932168 | tf_op jit(solution)/shard_map/ppermute | solution.py:112
  344.5 32.0 %collective-permute-start.51 = (bf16[4,160,1024]{2,1,0:T(8,128)(2,1)}, bf16[4,160,1024]{2,1,0:T(8,128)(2,1)}, u32[]{:S(2)}, u32[]{:S(2)}) collective-permute-start(bf16[4,160,1024]{2,1,0:T(8,128)(2,1)} %get-tuple-element.306), channel_id=1, source_target_pairs={{0,4},{1,5},{2,6},{3,7},{4,0},{5,1},{6,2},{7,3},{8,12},{9,13},{10,... | collective-permute-start | bytes 3932168 | tf_op jit(solution)/shard_map/ppermute | solution.py:112
  (74 other events, 990.8 us)
